TPU v7x, 32 devices: a whole 2x2x4 slice. The times are simulated.
32 devices in a mesh: seq: 16 (over z, y, x), head: 2 (over core).
Axes of the slice: x: 2, y: 2, z: 4, core: 2. Of those that a mesh axis runs over, the one named last changes fastest.
Arguments:
- tokens: bfloat16 [2, 2, 4096, 768], P(None, None, 'seq', 'head'), may hold values from -6 to 6
- doc_starts: int32 [2, 2, 4096], P(None, None, 'seq'), may hold values from 0 to 1, as said below
- norm_gain: float32 [768], replicated, may hold values from 0.5 to 1.5
- input_gate_features: bfloat16 [768, 2, 1536], P('seq', None, 'head'), may hold values from -0.21875 to 0.21875
- input_state_weight: bfloat16 [768, 256], P('seq'), may hold values from -0.21875 to 0.21875
- input_step_weight: bfloat16 [768, 24], P('seq', 'head'), may hold values from -0.21875 to 0.21875
- conv_taps_x: float32 [4, 1536], P(None, 'head'), may hold values from -3 to 3
- conv_bias_x: float32 [1536], P('head'), may hold values from -1.8 to 1.8
- conv_taps_bc: float32 [4, 256], replicated, may hold values from -3 to 3
- conv_bias_bc: float32 [256], replicated, may hold values from -1.8 to 1.8
- step_bias: float32 [24], P('head'), may hold values from -1 to 1
- decay_log: float32 [24], P('head')
- skip_gain: float32 [24], P('head'), may hold values from 0.5 to 1.5
- inner_gain: float32 [1536], P('head'), may hold values from 0.5 to 1.5
- output_projection: bfloat16 [1536, 768], P('head', 'seq'), may hold values from -0.15625 to 0.15625
- out_grad: bfloat16 [2, 2, 4096, 768], P(None, None, 'seq', 'head'), may hold values from -6 to 6
Outputs:
- mixed: bfloat16 [2, 2, 4096, 768], P(None, None, 'seq', 'head')
- tokens_grad: float32 [2, 2, 4096, 768], P(None, None, 'seq', 'head')
- norm_gain_grad: float32 [768], replicated
- in_gate_x_grad: float32 [768, 2, 1536], P('seq', None, 'head')
- in_states_grad: float32 [768, 256], P('seq')
- in_steps_grad: float32 [768, 24], P('seq', 'head')
- conv_taps_x_grad: float32 [4, 1536], P(None, 'head')
- conv_bias_x_grad: float32 [1536], P('head')
- conv_taps_bc_grad: float32 [4, 256], replicated
- conv_bias_bc_grad: float32 [256], replicated
- step_bias_grad: float32 [24], P('head')
- decay_log_grad: float32 [24], P('head')
- skip_gain_grad: float32 [24], P('head')
- inner_gain_grad: float32 [1536], P('head')
- out_proj_grad: float32 [1536, 768], P('head', 'seq')
Inputs may be any that keep to these rules, and one draw needn't show every extreme that they name: `doc_starts`: every sequence begins with a 1. In each micro-batch one of the 2 sequences, drawn from the seed, is a single document; the others hold documents of max(2, 25) to max(2, 25) + max(2, 256 - max(2, 25)) positions, the last one of a sequence possibly shorter.
All inputs are finite; a program needn't handle non-finite values.
Results may differ from a plain program's by a relative error of at most 0.019.
The roundings to bfloat16 on the way count: a program that leaves them out, or rounds other values in their place, can miss the bound.
Values may be sent and summed in bfloat16 or wider, within the bound.
A program may use at most 448 MiB of HBM per device.

v0:
```python
import jax
import jax.numpy as jnp
from jax import lax
from jax.sharding import PartitionSpec as P

BLOCK = 256


EPSILON = 1e-05
EXACT_MATMUL = lax.Precision.HIGHEST


def from_behind(block, axis, distance):
    devices = range(lax.axis_size(axis))
    route = [(i - distance, i) for i in devices if i - distance in devices]
    return lax.ppermute(block, axis, route)


def carried_in(part, axis, combine, identity):
    place = lax.axis_index(axis)
    gathered = jax.tree.map(lambda a: lax.all_gather(a, axis), part)
    state = jax.tree.map(lambda a, e: jnp.zeros_like(a) + jnp.asarray(e, a.dtype), part, identity)

    def one(lap, state):
        return combine(
            state, jax.tree.map(lambda a: lax.dynamic_index_in_dim(a, lap, 0, False), gathered)
        )

    return lax.fori_loop(0, place, one, state)


def entering(value, axis, combine, identity):
    count, position = (lax.axis_size(axis), lax.axis_index(axis))
    everything = jax.tree.map(
        lambda part, kind: lax.all_gather(part.astype(kind), axis),
        value,
        jax.tree.map(lambda a: jnp.bfloat16 if a.dtype == jnp.float32 else a.dtype, value),
    )
    start = jax.tree.map(
        lambda part, zero: jnp.broadcast_to(jnp.asarray(zero, part.dtype), part.shape),
        value,
        identity,
    )

    def lap(k, before):
        at = count - 1 - k
        reached = at > position
        new = combine(
            before, jax.tree.map(lambda part, own: part[at].astype(own.dtype), everything, value)
        )
        return jax.tree.map(lambda a, b: jnp.where(reached, a, b), new, before)

    return lax.fori_loop(0, count, lap, start)


def swish(inputs):
    return inputs * jax.nn.sigmoid(inputs)


def swish_slope(inputs):
    sigma = jax.nn.sigmoid(inputs)
    return sigma + inputs * sigma * (1.0 - sigma)


def block_step(decay_rate, hstate, pieces):
    values, in_state, out_state, step_size, doc_number, entry_number = pieces
    log_decay = jnp.cumsum(step_size * decay_rate, axis=1)
    length = doc_number.shape[1]
    places = jnp.arange(length)
    causal = places[:, None] >= places[None, :]
    allowed = causal[None] & (doc_number[:, :, None] == doc_number[:, None, :])
    allowed_h = allowed[..., None]
    spread = log_decay[:, :, None, :] - log_decay[:, None, :, :]
    decay_mat = jnp.where(allowed_h, jnp.exp(jnp.where(allowed_h, spread, 0.0)), 0.0)
    scores = jnp.einsum(
        "sin,sjn->sij",
        out_state.astype(jnp.bfloat16),
        in_state.astype(jnp.bfloat16),
        preferred_element_type=jnp.float32,
    )
    mixing = scores[..., None] * decay_mat * step_size[:, None, :, :]
    inside = jnp.einsum("sijh,sjhp->sihp", mixing, values, precision=EXACT_MATMUL)
    entry_decay = jnp.exp(log_decay) * (doc_number == entry_number[:, None])[..., None]
    carried = (
        jnp.einsum("sin,shpn->sihp", out_state, hstate, precision=EXACT_MATMUL)
        * entry_decay[..., None]
    )
    tail_weight = (
        jnp.exp(log_decay[:, -1:, :] - log_decay)
        * (doc_number == doc_number[:, -1:])[..., None]
        * step_size
    )
    new_state = entry_decay[:, -1, :, None, None] * hstate + jnp.einsum(
        "sjh,sjhp,sjn->shpn", tail_weight, values, in_state, precision=EXACT_MATMUL
    )
    return (new_state, inside + carried)


def to_blocks(source):
    shaped = source.reshape((source.shape[0], source.shape[1] // BLOCK, BLOCK) + source.shape[2:])
    return jnp.moveaxis(shaped, 1, 0)


def run_blocks(
    values, in_state, out_state, step_size, decay_rate, doc_number, entry_number, hstate
):
    stepper = jax.checkpoint(block_step)

    def advance(current, pieces):
        return stepper(decay_rate, current, pieces)

    pieces = (
        to_blocks(values),
        to_blocks(in_state),
        to_blocks(out_state),
        to_blocks(step_size),
        to_blocks(doc_number),
        jnp.moveaxis(entry_number, 1, 0),
    )
    last_state, outputs = lax.scan(advance, hstate, pieces)
    merged = jnp.moveaxis(outputs, 0, 1)
    return (merged.reshape(values.shape), last_state)


def block_entry_numbers(doc_number):
    shifted = jnp.concatenate([jnp.zeros_like(doc_number[:, :1]), doc_number[:, :-1]], axis=1)
    return shifted[:, ::BLOCK]


def chain_combine(earlier, later):
    return (later[0] * earlier[0], later[1] + later[0][..., None, None] * earlier[1])


def fetch_weights(input_gate_features, input_state_weight, input_step_weight, output_projection):
    return (
        lax.all_gather(input_gate_features, "seq", axis=0, tiled=True),
        lax.all_gather(input_state_weight, "seq", axis=0, tiled=True),
        lax.all_gather(input_step_weight, "seq", axis=0, tiled=True),
        lax.all_gather(output_projection, "seq", axis=1, tiled=True),
    )


def shards(
    tokens,
    doc_starts,
    norm_gain,
    input_gate_features,
    input_state_weight,
    input_step_weight,
    conv_taps_x,
    conv_bias_x,
    conv_taps_bc,
    conv_bias_bc,
    step_bias,
    decay_log,
    skip_gain,
    inner_gain,
    output_projection,
    out_grad,
):
    seq_count = tokens.shape[1]
    length = tokens.shape[2]
    half_model = tokens.shape[3]
    head_count = step_bias.shape[0]
    inner_local = inner_gain.shape[0]
    head_size = inner_local // head_count
    state_size = conv_taps_bc.shape[1] // 2
    taps_count = conv_taps_x.shape[0]
    inner_total = inner_local * lax.axis_size("head")
    model_total = input_gate_features.shape[0] * lax.axis_size("seq")
    own_start = lax.axis_index("head") * half_model
    decay_rate = -jnp.exp(decay_log)
    conv_taps = jnp.concatenate([conv_taps_x, conv_taps_bc], axis=1)
    conv_bias = jnp.concatenate([conv_bias_x, conv_bias_bc])
    channels = conv_bias.shape[0]
    total_gate_x = jnp.zeros((model_total,) + input_gate_features.shape[1:], jnp.float32)
    total_states = jnp.zeros((model_total, input_state_weight.shape[1]), jnp.float32)
    total_steps = jnp.zeros((model_total, head_count), jnp.float32)
    total_out = jnp.zeros((inner_local, model_total), jnp.float32)
    total_gain = jnp.zeros((model_total,), jnp.float32)
    total_taps = jnp.zeros((taps_count, channels), jnp.float32)
    total_bias = jnp.zeros((channels,), jnp.float32)
    total_step_bias = jnp.zeros((head_count,), jnp.float32)
    total_decay = jnp.zeros((head_count,), jnp.float32)
    total_skip = jnp.zeros((head_count,), jnp.float32)
    total_inner = jnp.zeros((inner_local,), jnp.float32)
    mixed_outs = []
    token_grads = []
    for micro_index in range(tokens.shape[0]):
        fetched = fetch_weights(
            input_gate_features, input_state_weight, input_step_weight, output_projection
        )
        (
            complete_gate_features,
            complete_state_weight,
            complete_step_weight,
            complete_output_weight,
        ) = fetched
        full_tokens = lax.all_gather(tokens[micro_index], "head", axis=2, tiled=True).astype(
            jnp.float32
        )
        row_scale = lax.rsqrt(jnp.mean(full_tokens * full_tokens, axis=-1, keepdims=True) + EPSILON)
        unit_rows = full_tokens * row_scale
        normalized_rows = (unit_rows * norm_gain).astype(jnp.bfloat16)
        gate_x_proj = jnp.einsum(
            "hun,nmy->humy",
            normalized_rows,
            complete_gate_features,
            preferred_element_type=jnp.float32,
        )
        gate_projected = gate_x_proj[:, :, 0]
        feature_projected = gate_x_proj[:, :, 1].astype(jnp.bfloat16)
        state_projected = jnp.einsum(
            "zxw,wt->zxt",
            normalized_rows,
            complete_state_weight,
            preferred_element_type=jnp.float32,
        ).astype(jnp.bfloat16)
        step_projected = jnp.einsum(
            "zxw,wt->zxt", normalized_rows, complete_step_weight, preferred_element_type=jnp.float32
        )
        conv_input = jnp.concatenate([feature_projected, state_projected], axis=-1)
        edge_rows = from_behind(conv_input[:, length - taps_count + 1 :], "seq", 1)
        extended = jnp.concatenate([edge_rows, conv_input], axis=1).astype(jnp.float32)
        conv_result = conv_bias + conv_taps[0] * extended[:, 0:length]
        for tap_index in range(1, taps_count):
            conv_result = (
                conv_result + conv_taps[tap_index] * extended[:, tap_index : tap_index + length]
            )
        activated = lax.optimization_barrier(swish(conv_result).astype(jnp.bfloat16)).astype(
            jnp.float32
        )
        head_values = activated[..., :inner_local].reshape(seq_count, length, head_count, head_size)
        in_state = activated[..., inner_local : inner_local + state_size]
        out_state = activated[..., inner_local + state_size :]
        step_pre = step_projected + step_bias
        step_size = jax.nn.softplus(step_pre)
        doc_number = jnp.cumsum(doc_starts[micro_index], axis=1)
        entry_number = block_entry_numbers(doc_number)
        start_state = jnp.zeros((seq_count, head_count, head_size, state_size), jnp.float32)

        def local_scan(values, in_states_arg, out_states_arg, steps_arg, rates_arg):
            return run_blocks(
                values,
                in_states_arg,
                out_states_arg,
                steps_arg,
                rates_arg,
                doc_number,
                entry_number,
                start_state,
            )

        (scanned, local_end), scan_back = jax.vjp(
            local_scan, head_values, in_state, out_state, step_size, decay_rate
        )
        entry_decay = (
            jnp.exp(jnp.cumsum(step_size * decay_rate, axis=1)) * (doc_number == 0)[..., None]
        )
        device_decay = entry_decay[:, -1]
        prefix = carried_in(
            (device_decay, local_end),
            "seq",
            chain_combine,
            (jnp.ones_like(device_decay), jnp.zeros_like(local_end)),
        )
        incoming = prefix[1]

        def carried(out_states_arg, steps_arg, rates_arg):
            entry_weight = (
                jnp.exp(jnp.cumsum(steps_arg * rates_arg, axis=1)) * (doc_number == 0)[..., None]
            )
            return (
                entry_weight[..., None]
                * jnp.einsum("sln,shpn->slhp", out_states_arg, incoming, precision=EXACT_MATMUL),
                entry_weight[:, -1],
            )

        (from_prior, unused_decay), carried_back = jax.vjp(
            carried, out_state, step_size, decay_rate
        )
        mixed_heads = scanned + from_prior + skip_gain[:, None] * head_values
        mixed_flat = mixed_heads.reshape(seq_count, length, inner_local)
        gate_swish = swish(gate_projected)
        gated_out = mixed_flat * gate_swish
        square_sum = lax.psum(jnp.sum(gated_out * gated_out, axis=-1), "head")
        inner_scale = lax.rsqrt(square_sum / inner_total + EPSILON)[..., None]
        gated_normalized = (gated_out * inner_scale * inner_gain).astype(jnp.bfloat16)
        partial_out = jnp.einsum(
            "amz,ze->ame",
            gated_normalized,
            complete_output_weight,
            preferred_element_type=jnp.float32,
        )
        branch_half = lax.psum_scatter(
            partial_out.astype(jnp.bfloat16), "head", scatter_dimension=2, tiled=True
        ).astype(jnp.float32)
        mixed_outs.append(
            (tokens[micro_index].astype(jnp.float32) + branch_half).astype(jnp.bfloat16)
        )
        gradient_complete = lax.all_gather(out_grad[micro_index], "head", axis=2, tiled=True)
        total_out = total_out + jnp.einsum(
            "uhi,uhv->iv", gated_normalized, gradient_complete, preferred_element_type=jnp.float32
        )
        grad_norm = jnp.einsum(
            "czy,ay->cza",
            gradient_complete,
            complete_output_weight,
            preferred_element_type=jnp.float32,
        )
        total_inner = total_inner + jnp.sum(grad_norm * gated_out * inner_scale, axis=(0, 1))
        grad_scaled = grad_norm * inner_gain
        cross_sum = lax.psum(jnp.sum(grad_scaled * gated_out, axis=-1), "head")
        grad_gated = inner_scale * grad_scaled - gated_out * inner_scale**3 * (
            cross_sum[..., None] / inner_total
        )
        grad_mixed = (grad_gated * gate_swish).reshape(seq_count, length, head_count, head_size)
        grad_gate = (grad_gated * mixed_flat * swish_slope(gate_projected)).astype(jnp.bfloat16)
        total_skip = total_skip + jnp.sum(grad_mixed * head_values, axis=(0, 1, 3))
        prior_grad = jnp.einsum(
            "slh,slhp,sln->shpn", entry_decay, grad_mixed, out_state, precision=EXACT_MATMUL
        )
        suffix = entering(
            (device_decay, prior_grad),
            "seq",
            chain_combine,
            (jnp.ones_like(device_decay), jnp.zeros_like(prior_grad)),
        )
        later_grad = suffix[1]
        grad_values, grad_in, grad_out_state, grad_steps, grad_rates = scan_back(
            (grad_mixed, later_grad)
        )
        extra_out, extra_steps, extra_rates = carried_back(
            (grad_mixed, jnp.sum(later_grad * incoming, axis=(2, 3)))
        )
        grad_values = grad_values + skip_gain[:, None] * grad_mixed
        grad_out_state = grad_out_state + extra_out
        grad_steps = grad_steps + extra_steps
        grad_rates = grad_rates + extra_rates
        total_decay = total_decay + grad_rates * decay_rate
        gradient_before_activation = grad_steps * jax.nn.sigmoid(step_pre)
        total_step_bias = total_step_bias + jnp.sum(gradient_before_activation, axis=(0, 1))
        state_grads = lax.psum(
            jnp.concatenate([grad_in, grad_out_state], axis=-1).astype(jnp.bfloat16), "head"
        ).astype(jnp.float32)
        grad_act = jnp.concatenate(
            [grad_values.reshape(seq_count, length, inner_local), state_grads], axis=-1
        )
        grad_conv = grad_act * swish_slope(conv_result)
        total_bias = total_bias + jnp.sum(grad_conv, axis=(0, 1))
        total_taps = total_taps + jnp.stack(
            [
                jnp.sum(extended[:, tap_index : tap_index + length] * grad_conv, axis=(0, 1))
                for tap_index in range(taps_count)
            ]
        )
        grad_ext = jnp.pad(conv_taps[0] * grad_conv, ((0, 0), (0, taps_count - 1), (0, 0)))
        for tap_index in range(1, taps_count):
            grad_ext = grad_ext + jnp.pad(
                conv_taps[tap_index] * grad_conv,
                ((0, 0), (tap_index, taps_count - 1 - tap_index), (0, 0)),
            )
        back_edge = from_behind(grad_ext[:, : taps_count - 1], "seq", -1)
        grad_input = grad_ext[:, taps_count - 1 :] + jnp.pad(
            back_edge, ((0, 0), (length - taps_count + 1, 0), (0, 0))
        )
        grad_x = grad_input[..., :inner_local].astype(jnp.bfloat16)
        gradient_state_vectors = grad_input[..., inner_local:]
        gradient_stacked = jnp.stack([grad_gate, grad_x], axis=2)
        total_gate_x = total_gate_x + jnp.einsum(
            "wor,wojb->rjb", normalized_rows, gradient_stacked, preferred_element_type=jnp.float32
        )
        normalized_wide_rows = normalized_rows.astype(jnp.float32)
        total_states = total_states + jnp.einsum(
            "cgp,cgt->pt", normalized_wide_rows, gradient_state_vectors, precision=EXACT_MATMUL
        )
        total_steps = total_steps + jnp.einsum(
            "cgp,cgt->pt", normalized_wide_rows, gradient_before_activation, precision=EXACT_MATMUL
        )
        grad_part = jnp.einsum(
            "einf,bnf->eib",
            gradient_stacked,
            complete_gate_features,
            preferred_element_type=jnp.float32,
        )
        grad_part = grad_part + jnp.einsum(
            "cea,pa->cep",
            gradient_before_activation,
            complete_step_weight.astype(jnp.float32),
            precision=EXACT_MATMUL,
        )
        grad_normed = lax.psum(grad_part.astype(jnp.bfloat16), "head").astype(jnp.float32)
        grad_normed = grad_normed + jnp.einsum(
            "cea,pa->cep",
            gradient_state_vectors,
            complete_state_weight.astype(jnp.float32),
            precision=EXACT_MATMUL,
        )
        total_gain = total_gain + jnp.sum(grad_normed * unit_rows, axis=(0, 1))
        grad_unit = grad_normed * norm_gain
        grad_tokens = row_scale * (
            grad_unit - unit_rows * jnp.mean(grad_unit * unit_rows, axis=-1, keepdims=True)
        )
        own_half = lax.dynamic_slice_in_dim(grad_tokens, own_start, half_model, axis=2)
        token_grads.append(out_grad[micro_index].astype(jnp.float32) + own_half)
    weight_grads = (
        lax.psum_scatter(total_gate_x, "seq", scatter_dimension=0, tiled=True),
        lax.psum_scatter(total_states, "seq", scatter_dimension=0, tiled=True),
        lax.psum_scatter(total_steps, "seq", scatter_dimension=0, tiled=True),
        lax.psum_scatter(total_out, "seq", scatter_dimension=1, tiled=True),
    )
    small_grads = lax.psum(
        (total_gain, total_taps, total_bias, total_step_bias, total_decay, total_skip, total_inner),
        "seq",
    )
    gain_grad = small_grads[0]
    return (
        jnp.stack(mixed_outs),
        jnp.stack(token_grads),
        gain_grad,
        weight_grads[0],
        weight_grads[1],
        weight_grads[2],
        small_grads[1][:, :inner_local],
        small_grads[2][:inner_local],
        small_grads[1][:, inner_local:],
        small_grads[2][inner_local:],
        small_grads[3],
        small_grads[4],
        small_grads[5],
        small_grads[6],
        weight_grads[3],
    )


def solution(mesh):
    placed = (
        P(None, None, "seq", "head"),
        P(None, None, "seq"),
        P(),
        P("seq", None, "head"),
        P("seq", None),
        P("seq", "head"),
        P(None, "head"),
        P("head"),
        P(),
        P(),
        P("head"),
        P("head"),
        P("head"),
        P("head"),
        P("head", "seq"),
        P(None, None, "seq", "head"),
    )
    return jax.shard_map(
        shards,
        mesh=mesh,
        in_specs=placed,
        out_specs=(
            P(None, None, "seq", "head"),
            P(None, None, "seq", "head"),
            P(),
            P("seq", None, "head"),
            P("seq", None),
            P("seq", "head"),
            P(None, "head"),
            P("head"),
            P(),
            P(),
            P("head"),
            P("head"),
            P("head"),
            P("head"),
            P("head", "seq"),
        ),
        check_vma=False,
    )
```

profile of v0, /device:TPU:0, one launch (start us, length us, event | category | flops | bytes accessed | tf_op | source)
XLA Modules:
  0.0 1516.3 jit_solution(6795804578379464079)
XLA Ops:
  9.6 45.4 %all_gather.68 = bf16[768,256]{1,0:T(8,128)(2,1)S(1)} all-gather(bf16[48,256]{1,0:T(8,128)(2,1)} %param.28), channel_id=1, replica_groups=mesh['seq'=16,'head'=2] {'seq'}, dimensions={0}, use_global_device_ids=true | all-gather | bytes 417792 | tf_op jit(solution)/shard_map/all_gather | solution.py:137
  63.9 35.9 %all-gather.12 = bf16[16,48,12]{1,2,0:T(8,128)(2,1)S(1)} all-gather(bf16[1,48,12]{1,2,0:T(8,128)(2,1)S(1)} %bitcast.712), channel_id=1, replica_groups=mesh['seq'=16,'head'=2] {'seq'}, dimensions={0}, use_global_device_ids=true | all-gather | bytes 19584 | tf_op jit(solution)/shard_map/all_gather | solution.py:138
  110.0 3.9 multiply_multiply_fusion.4
  120.6 4.1 collective-permute-start
  131.1 4.1 fusion.119
  150.1 3.3 fusion.120
  162.5 40.3 %all-gather.5 = f32[32,1,12]{2,1,0:T(1,128)} all-gather(f32[2,1,12]{2,1,0:T(1,128)S(1)} %bitcast.713), channel_id=7, replica_groups=mesh['seq'=16,'head'=2] {'seq'}, dimensions={0}, use_global_device_ids=true | all-gather | bytes 1632 | tf_op jit(solution)/shard_map/all_gather | solution.py:21
  202.8 37.8 %all-gather.2 = f32[32,1,12]{2,1,0:T(1,128)} all-gather(f32[2,1,12]{2,1,0:T(1,128)S(1)} %bitcast.714), channel_id=4, replica_groups=mesh['seq'=16,'head'=2] {'seq'}, dimensions={0}, use_global_device_ids=true | all-gather | bytes 1632 | tf_op jit(solution)/shard_map/all_gather | solution.py:21
  247.8 3.6 fusion.133
  273.9 6.1 fusion.14
  280.0 6.1 fusion.21
  286.1 9.6 all-gather.26.cloned.1.call-done
  298.8 149.8 %all-gather.24.cloned.1.call-done = f32[32,12,64,128]{3,2,1,0:T(8,128)} async-done(((f32[2,12,64,128]{3,2,1,0:T(8,128)}), f32[32,12,64,128]{3,2,1,0:T(8,128)}) %all-gather.24.cloned.1.call-update) | async-done | bytes 12582928 | tf_op jit(solution)/shard_map/all_gather | solution.py:21
  449.5 10.4 while.40
  462.2 5.6 multiply_reduce_fusion.26
  467.8 3.6 multiply_reduce_fusion.27
  480.0 6.1 multiply_reduce_fusion.13
  488.5 8.2 multiply_reduce_fusion.14
  510.3 83.7 %all-gather.10 = bf16[32,1,12]{2,1,0:T(2,128)(2,1)S(1)} all-gather(bf16[2,1,12]{2,1,0:T(2,128)(2,1)S(1)} %copy.542), channel_id=12, replica_groups=mesh['seq'=16,'head'=2] {'seq'}, dimensions={0}, use_global_device_ids=true | all-gather | bytes 816 | tf_op jit(solution)/shard_map/all_gather | solution.py:35
  594.7 35.6 %all-gather.11 = bf16[32,1,12]{2,1,0:T(2,128)(2,1)S(1)} all-gather(bf16[2,1,12]{2,1,0:T(2,128)(2,1)S(1)} %copy.585), channel_id=13, replica_groups=mesh['seq'=16,'head'=2] {'seq'}, dimensions={0}, use_global_device_ids=true | all-gather | bytes 816 | tf_op jit(solution)/shard_map/all_gather | solution.py:35
  633.9 4.9 fusion.142
  638.8 3.4 fusion.139
  642.2 37.6 %while.43 = (s32[]{:T(128)}, f32[2,12,64,128]{3,2,1,0:T(8,128)}, s32[]{:T(128)}, bf16[16,2,12,64,128]{4,3,2,1,0:T(8,128)(2,1)}, bf16[16,2,12]{2,1,0:T(2,128)(2,1...) while((s32[]{:T(128)}, f32[2,12,64,128]{3,2,1,0:T(8,128)}, s32[]{:T(128)}, ...), condition=%wide.region_45.46_spmd.clone, body=%wide.region_44.45_spmd.clone.sunk | while | flops 983072 | bytes 1966495 | solution.py:53
  686.7 49.7 %all-gather.28.cloned.1.call-done = bf16[32,12,64,128]{3,2,1,0:T(8,128)(2,1)} async-done(((bf16[2,12,64,128]{3,2,1,0:T(8,128)(2,1)}), bf16[32,12,64,128]{3,2,1,0:T(8,128)(2,1)}) %all-gather.28.cloned.1.call-update) | async-done | bytes 6291472 | tf_op jit(solution)/shard_map/all_gather | solution.py:35
  736.4 29.8 %while.42 = (s32[]{:T(128)}, f32[2,12,64,128]{3,2,1,0:T(8,128)S(1)}, s32[]{:T(128)}, bf16[16,2,12,64,128]{4,3,2,1,0:T(8,128)(2,1)}, bf16[16,2,12]{2,1,0:T(2,128)...) while((s32[]{:T(128)}, f32[2,12,64,128]{3,2,1,0:T(8,128)S(1)}, s32[]{:T(128)}, ...), condition=%wide.region_23.24_spmd.clone, body=%wide.region_22.23_spmd.clone.sunk | while | flops 983072 | bytes 1966495 | solution.py:53
  791.1 10.8 fusion.30
  809.6 10.9 fusion.28
  850.4 4.4 fusion.188
  854.8 3.7 fusion.178
  865.9 3.2 convolution_convert_fusion.1
  894.6 5.0 reduce-window.128
  902.5 5.0 reduce-window.132
  910.5 5.0 reduce-window.126
  922.9 5.0 reduce-window.134
  931.6 8.2 bitcast_add_fusion.7
  944.4 8.2 bitcast_add_fusion.5
  963.0 4.9 multiply_add_fusion.3
  970.0 9.1 multiply_reduce_fusion.5
  979.2 6.6 broadcast_multiply_fusion.6
  985.8 3.4 pad_add_fusion
  1010.3 3.8 bitcast_add_fusion.2
  1027.2 55.6 %reduce-scatter.23.cloned.1.call-done = f32[48,12]{1,0:T(8,128)} async-done(((f32[768,12]{1,0:T(8,128)}), f32[48,12]{1,0:T(8,128)}) %reduce-scatter.23.cloned.1.call-update) | async-done | bytes 2320
  1089.6 15.8 %all-reduce.24.cloned.1.call-done = (bf16[2,256,768]{2,1,0:T(8,128)(2,1)}, bf16[2,256,768]{2,1,0:T(8,128)(2,1)}) async-done(((bf16[2,256,768]{2,1,0:T(8,128)(2,1)}, bf16[2,256,768]{2,1,0:T(8,128)(2,1)}), (bf16[2,256,768]{2,1,0:T(8,128)(2,1)}, bf16[2,256,768]{2,1,0:T(8,128)(2,1)})) %all-reduce.24.cloned.1.call-update) | async-done | bytes 1572880 | tf_op jit(solution)/shard_map/psum | solution.py:392
  1107.6 5.5 multiply_reduce_fusion.16
  1113.2 78.2 %all-reduce.16 = (f32[768]{0:T(1024)}, f32[4,1024]{1,0:T(4,128)S(1)}, f32[1024]{0:T(1024)S(1)}, f32[12]{0:T(128)}, f32[12]{0:T(128)}, /*index=5*/f32[12]{0:T(128)}, f32[768]{0:T(1024)}) all-reduce(f32[768]{0:T(1024)S(1)} %add.547, f32[4,1024]{1,0:T(4,128)S(1)} %maximum_add_fusion, ...), channel_id=1, replica_groups=mesh['seq'=16,'head'=2] {'seq'}, use_global_device_ids=true, to_apply=%region_66.67 | all-reduce | flops 6692 | bytes 53536 | tf_op jit(solution)/shard_map/psum | solution.py:412
  1196.7 53.3 %reduce-scatter.13.cloned.1.call-done = f32[48,2,768]{2,0,1:T(8,128)} async-done(((f32[768,2,768]{2,0,1:T(8,128)}), f32[48,2,768]{2,0,1:T(8,128)}) %reduce-scatter.13.cloned.1.call-update) | async-done | bytes 294928 | tf_op jit(solution)/shard_map/reduce_scatter | solution.py:407
  1251.9 130.2 %reduce-scatter.17.cloned.1.call-done = f32[768,48]{0,1:T(8,128)} async-done(((f32[768,768]{0,1:T(8,128)}), f32[768,48]{0,1:T(8,128)}) %reduce-scatter.17.cloned.1.call-update) | async-done | bytes 147472 | tf_op jit(solution)/shard_map/reduce_scatter | solution.py:410
  1382.1 127.2 %reduce-scatter.15.cloned.1.call-done = f32[48,256]{1,0:T(8,128)} async-done(((f32[768,256]{1,0:T(8,128)}), f32[48,256]{1,0:T(8,128)}) %reduce-scatter.15.cloned.1.call-update) | async-done | bytes 49168 | tf_op jit(solution)/shard_map/reduce_scatter | solution.py:408
  (751 shorter events, 374.6 us)
Async XLA Ops:
  7.2 109.1 %all-gather.20.cloned.1.call-start = ((), (), s32[]{:S(2)}) async-start(), calls=%async_computation.6 | async-start | bytes 2506752 | tf_op jit(solution)/shard_map/all_gather | solution.py:136
  8.8 239.0 %all-gather.22.cloned.1.call-start = ((), (), s32[]{:S(2)}) async-start(), calls=%async_computation.7 | async-start | bytes 1253376 | tf_op jit(solution)/shard_map/all_gather | solution.py:139
  9.6 286.1 %all-gather.26.cloned.1.call-start = ((), (), s32[]{:S(2)}) async-start(), calls=%async_computation.12 | async-start | bytes 13369344 | tf_op jit(solution)/shard_map/all_gather | solution.py:21
  58.8 57.5 %copy-start.28 = (bf16[1,2,256,768]{3,2,1,0:T(8,128)(2,1)}, bf16[1,2,256,768]{3,2,1,0:T(8,128)(2,1)S(1)}, u32[]{:S(2)}) copy-start(bf16[1,2,256,768]{3,2,1,0:T(8,128)(2,1)S(1)} %all-gather) | copy-start | bytes 2359300
  59.0 57.3 %copy-start.120 = (f32[2,256]{1,0:T(2,128)}, f32[2,256]{1,0:T(2,128)S(1)}, u32[]{:S(2)}) copy-start(f32[2,256]{1,0:T(2,128)S(1)} %add_rsqrt_fusion.3) | copy-start | bytes 6148
  61.4 63.3 %copy-start.23 = (bf16[1,2,256,768]{3,2,1,0:T(8,128)(2,1)}, bf16[1,2,256,768]{3,2,1,0:T(8,128)(2,1)S(1)}, u32[]{:S(2)}) copy-start(bf16[1,2,256,768]{3,2,1,0:T(8,128)(2,1)S(1)} %all-gather.3) | copy-start | bytes 2359300
  61.6 63.1 %copy-start.110 = (f32[2,256]{1,0:T(2,128)}, f32[2,256]{1,0:T(2,128)S(1)}, u32[]{:S(2)}) copy-start(f32[2,256]{1,0:T(2,128)S(1)} %add_rsqrt_fusion.1) | copy-start | bytes 6148
  100.8 30.2 %copy-start.112 = (f32[1,1024]{1,0:T(1,128)}, f32[1,1024]{1,0:T(1,128)S(1)}, u32[]{:S(2)}) copy-start(f32[1,1024]{1,0:T(1,128)S(1)} %get-tuple-element.1002) | copy-start | bytes 12292
  100.9 30.2 %copy-start.114 = (f32[1,1024]{1,0:T(1,128)}, f32[1,1024]{1,0:T(1,128)S(1)}, u32[]{:S(2)}) copy-start(f32[1,1024]{1,0:T(1,128)S(1)} %get-tuple-element.1003) | copy-start | bytes 12292
  100.9 30.2 %copy-start.116 = (f32[1,1024]{1,0:T(1,128)}, f32[1,1024]{1,0:T(1,128)S(1)}, u32[]{:S(2)}) copy-start(f32[1,1024]{1,0:T(1,128)S(1)} %get-tuple-element.1004) | copy-start | bytes 12292
  100.9 30.2 %copy-start.118 = (f32[1,1024]{1,0:T(1,128)}, f32[1,1024]{1,0:T(1,128)S(1)}, u32[]{:S(2)}) copy-start(f32[1,1024]{1,0:T(1,128)S(1)} %get-tuple-element.1005) | copy-start | bytes 12292
  120.6 8.7 collective-permute-start
  127.4 3.4 collective-permute-start.1
  135.3 130.7 %copy-start.15 = (bf16[2,256,1024]{2,1,0:T(8,128)(2,1)}, bf16[2,256,1024]{2,1,0:T(8,128)(2,1)S(1)}, u32[]{:S(2)}) copy-start(bf16[2,256,1024]{2,1,0:T(8,128)(2,1)S(1)} %get-tuple-element.934) | copy-start | bytes 3145732
  143.8 304.8 %all-gather.24.cloned.1.call-start = ((), (), s32[]{:S(2)}) async-start(), calls=%async_computation.11 | async-start | bytes 13369344 | tf_op jit(solution)/shard_map/all_gather | solution.py:21
  153.4 9.2 copy-start.149
  153.4 488.8 %all-gather.30.cloned.1.call-start = ((), (), s32[]{:S(2)}) async-start(), calls=%async_computation.14 | async-start | bytes 6684672 | tf_op jit(solution)/shard_map/all_gather | solution.py:35
  295.8 153.8 %copy-start.3 = (f32[2,12,64,128]{3,2,1,0:T(8,128)}, f32[2,12,64,128]{3,2,1,0:T(8,128)S(1)}, u32[]{:S(2)}) copy-start(f32[2,12,64,128]{3,2,1,0:T(8,128)S(1)} %get-tuple-element.686) | copy-start | bytes 2359300
  502.8 233.7 %all-gather.28.cloned.1.call-start = ((), (), s32[]{:S(2)}) async-start(), calls=%async_computation.13 | async-start | bytes 6684672 | tf_op jit(solution)/shard_map/all_gather | solution.py:35
  508.9 459.0 %all-reduce.26.cloned.1.call-start = ((), (), s32[]{:S(2)}) async-start(), calls=%async_computation.19 | async-start | bytes 1048576 | tf_op jit(solution)/shard_map/psum | solution.py:343
  509.6 124.3 %copy-start.4 = (f32[2,12,64,128]{3,2,1,0:T(8,128)S(1)}, f32[2,12,64,128]{3,2,1,0:T(8,128)}, u32[]{:S(2)}) copy-start(f32[2,12,64,128]{3,2,1,0:T(8,128)} %copy-done.3) | copy-start | bytes 2359300
  642.2 38.3 %copy-start.136 = (f32[12]{0:T(128)S(1)}, f32[12]{0:T(128)}, u32[]{:S(2)}) copy-start(f32[12]{0:T(128)} %copy-done.135) | copy-start | bytes 148
  685.4 51.0 %copy-start.43 = (f32[2,12,2,128]{1,0,3,2:T(2,128)}, f32[2,12,2,128]{1,0,3,2:T(2,128)S(1)}, u32[]{:S(2)}) copy-start(f32[2,12,2,128]{1,0,3,2:T(2,128)S(1)} %copy.702) | copy-start | bytes 73732
  736.4 29.9 %copy-start.27 = (f32[2,256,12]{2,0,1:T(2,128)S(1)}, f32[2,256,12]{2,0,1:T(2,128)}, u32[]{:S(2)}) copy-start(f32[2,256,12]{2,0,1:T(2,128)} %get-tuple-element.690) | copy-start | bytes 73732
  785.5 20.6 %copy-start.13 = (f32[2,12,64,128]{3,2,1,0:T(8,128)}, f32[2,12,64,128]{3,2,1,0:T(8,128)S(1)}, u32[]{:S(2)}) copy-start(f32[2,12,64,128]{3,2,1,0:T(8,128)S(1)} %broadcast.400) | copy-start | bytes 2359300
  791.1 12.7 copy-start.50
  791.1 12.7 copy-start.52
  830.1 9.6 copy-start.155
  865.8 155.0 %reduce-scatter.19.cloned.1.call-start = ((), (), s32[]{:S(2)}) async-start(), calls=%async_computation.15 | async-start | bytes 1179648
  874.3 148.4 %reduce-scatter.21.cloned.1.call-start = ((), (), s32[]{:S(2)}) async-start(), calls=%async_computation.16 | async-start | bytes 1179648
  891.5 191.3 %reduce-scatter.23.cloned.1.call-start = ((), (), s32[]{:S(2)}) async-start(), calls=%async_computation.17 | async-start | bytes 417792
  907.7 12.6 copy-start.78
  908.6 11.9 copy-start.103
  910.5 10.9 copy-start.40
  910.5 10.9 copy-start.70
  921.5 9.9 copy-start.130
  962.9 142.4 %all-reduce.24.cloned.1.call-start = ((), (), s32[]{:S(2)}) async-start(), calls=%async_computation.18 | async-start | bytes 3145728 | tf_op jit(solution)/shard_map/psum | solution.py:392
  970.0 9.2 copy-start.113
  970.0 9.2 copy-start.115
  970.0 9.2 copy-start.117
  970.0 9.2 copy-start.119
  989.4 5.8 collective-permute-start.3
  991.7 6.5 collective-permute-start.2
  1006.3 243.7 %reduce-scatter.13.cloned.1.call-start = ((), (), s32[]{:S(2)}) async-start(), calls=%async_computation.8 | async-start | bytes 5013504 | tf_op jit(solution)/shard_map/reduce_scatter | solution.py:407
  1014.1 367.9 %reduce-scatter.17.cloned.1.call-start = ((), (), s32[]{:S(2)}) async-start(), calls=%async_computation.10 | async-start | bytes 2506752 | tf_op jit(solution)/shard_map/reduce_scatter | solution.py:410
  1019.7 489.6 %reduce-scatter.15.cloned.1.call-start = ((), (), s32[]{:S(2)}) async-start(), calls=%async_computation.9 | async-start | bytes 835584 | tf_op jit(solution)/shard_map/reduce_scatter | solution.py:408
  1086.4 18.9 %copy-start.55 = (bf16[768,256]{1,0:T(8,128)(2,1)S(1)}, bf16[768,256]{1,0:T(8,128)(2,1)}, u32[]{:S(2)}) copy-start(bf16[768,256]{1,0:T(8,128)(2,1)} %copy-done.54) | copy-start | bytes 1179652
  1107.6 85.6 %copy-start.64 = (bf16[2,2,256,384]{3,2,1,0:T(8,128)(2,1)S(1)}, bf16[2,2,256,384]{3,2,1,0:T(8,128)(2,1)}, u32[]{:S(2)}) copy-start(bf16[2,2,256,384]{3,2,1,0:T(8,128)(2,1)} %param.39) | copy-start | bytes 2359300
  (142 other events, 490.4 us)
Sparse Core Ops, SparseCore 0:
  11.3 66.2 all-gather.19
  80.4 54.8 all-gather.21
  143.9 151.7 all-gather.25
  298.3 150.2 all-gather.23
  502.9 138.2 all-gather.29
  643.8 92.5 all-gather.27
  865.9 17.0 all-reduce.25
  885.4 9.4 reduce-scatter.18
  897.1 9.4 reduce-scatter.20
  963.0 119.6 reduce-scatter.22
  1085.8 19.5 all-reduce.23
  1111.2 138.6 reduce-scatter.12
  1255.4 126.5 reduce-scatter.16
  1387.9 121.3 reduce-scatter.14
where the time goes:
time: 1530 us; the launch traced here: 1520 us
  waiting for transfers between devices  598 us (39%)
  blocking collectives  372 us (24%)
  other arithmetic  191 us (12%)
  matrix products  176 us (12%)
  local copies, waits for them, and re-layouts  143 us (9%)
  between operations  16.6 us (1%)
    all_gather x2, waiting for transfers between devices, carried_in(): gathered = jax.tree.map(lambda a: lax.all_gather(a, axis), part)  159 us
    reduce_scatter x1, waiting for transfers between devices, shards(): lax.psum_scatter(total_out, 'seq', scatter_dimension=1, tiled=True)  130 us
    reduce_scatter x1, waiting for transfers between devices, shards(): lax.psum_scatter(total_states, 'seq', scatter_dimension=0, tiled=True)  127 us
    all_gather x2, blocking collectives, entering(): lax.all_gather(part.astype(kind), axis)  119 us
    psum x1, blocking collectives, shards(): lax.psum((total_gain, total_taps, total_bias, total_step_bias, total_deca...  78.2 us
    all_gather x2, blocking collectives, carried_in(): gathered = jax.tree.map(lambda a: lax.all_gather(a, axis), part)  78.1 us
    unnamed x17, waiting for transfers between devices  56.5 us
    select_n x32, other arithmetic, lap(): return jax.tree.map(lambda a, b: jnp.where(reached, a, b), new, before)  56 us
  transfers between devices with their start and end apart: 18, of which 11 were waited for; matrix products, arithmetic and copies ran while one was open for 22% of the time, Pallas kernels for 0%

commit v1 on v0

v1 whole, which is shorter than its diff:
```python
import functools

import jax
import jax.numpy as jnp
from jax import lax
from jax.experimental import pallas as pl
from jax.experimental.pallas import tpu as pltpu
from jax.sharding import PartitionSpec as P

F32 = jnp.float32
BF16 = jnp.bfloat16
EPSILON = 1e-05
MASKED = -1e30
HALO = 16
EDGE = 8
HEAD_ROWS = 16
LANES = 128
MESH = pl.DeviceIdType.MESH
NN = ((1,), (0,))
NT = ((1,), (1,))
TN = ((0,), (0,))
VMEM_LIMIT = 60 * 2**20

GAIN, INNER_GAIN, SKIP, BIAS, STEP_BIAS, RATE, TAPS = 0, 1, 2, 3, 4, 5, 6


def dot(a, b, dims=NN):
    return lax.dot_general(a, b, (dims, ((), ())), preferred_element_type=F32)


def split2(v):
    high = v.astype(BF16)
    return high, (v - high.astype(F32)).astype(BF16)


def split3(v):
    high = v.astype(BF16)
    rest = v - high.astype(F32)
    middle = rest.astype(BF16)
    return high, middle, (rest - middle.astype(F32)).astype(BF16)


def sigmoid(v):
    return 1.0 / (1.0 + jnp.exp(-v))


def softplus(v):
    return jnp.maximum(v, 0.0) + jnp.log1p(jnp.exp(-jnp.abs(v)))


def head_spread(inner, size):
    rows = lax.broadcasted_iota(jnp.int32, (LANES, inner), 0)
    columns = lax.broadcasted_iota(jnp.int32, (LANES, inner), 1)
    return jnp.where(rows == columns // size, 1.0, 0.0).astype(BF16)


def expand(per_head, spread):
    high, low = split2(per_head)
    return dot(high, spread) + dot(low, spread)


def head_sums(wide, spread):
    high, low = split2(wide)
    return dot(high, spread, NT) + dot(low, spread, NT)


def triangle(length, upper=False):
    rows = lax.broadcasted_iota(jnp.int32, (length, length), 0)
    columns = lax.broadcasted_iota(jnp.int32, (length, length), 1)
    kept = rows <= columns if upper else rows >= columns
    return kept, jnp.where(kept, 1.0, 0.0).astype(BF16)


def running_sum(ones, v):
    a, b, c = split3(v)
    return dot(ones, a) + dot(ones, b) + dot(ones, c)


def doc_numbers(doc, ones):
    flags = doc.astype(BF16)
    return dot(ones, flags, NT)[:, :1], dot(flags, ones, NT)[:1]


def call(kernel, grid, in_specs, out_specs, out_shape, scratch=(), name=None, flops=10**9):
    return pl.pallas_call(
        kernel,
        grid=grid,
        in_specs=in_specs,
        out_specs=out_specs,
        out_shape=out_shape,
        scratch_shapes=list(scratch),
        compiler_params=pltpu.CompilerParams(
            vmem_limit_bytes=VMEM_LIMIT, dimension_semantics=("arbitrary",) * len(grid)
        ),
        cost_estimate=pl.CostEstimate(flops=flops, bytes_accessed=10**7, transcendentals=0),
        name=name,
    )


def whole(array):
    rank = len(array.shape)
    return pl.BlockSpec(array.shape, lambda i: (0,) * rank)


def per_seq(array):
    rank = len(array.shape)
    return pl.BlockSpec((1,) + tuple(array.shape[1:]), lambda i: (i,) + (0,) * (rank - 1))


def shape(dims, dtype):
    return jax.ShapeDtypeStruct(tuple(dims), dtype)


def forward_kernel(
    sizes, tok, halo, doc, prm, w, normed_o, gate_o, xs_o, pre_o, act_o, scan_o, state_o, aux_o,
    dec_o, ext,
):
    length, inner, nstate, size, taps = sizes
    channels = inner + 2 * nstate
    first = lax.axis_index("seq") == 0
    edge = jnp.where(first, 0.0, halo[0].astype(F32))
    x = jnp.concatenate([edge, tok[0].astype(F32)], axis=0)
    scale = lax.rsqrt(jnp.mean(x * x, axis=-1, keepdims=True) + EPSILON)
    normed = (x * scale * prm[GAIN : GAIN + 1, : x.shape[1]]).astype(BF16)
    normed_o[0] = normed[HALO:]
    gate_o[0] = dot(normed[HALO:], w[:, :inner])
    xs = dot(normed, w[:, inner : inner + channels]).astype(BF16)
    xs_o[0] = xs
    ext[...] = xs.astype(F32)
    pre = prm[BIAS : BIAS + 1, :channels]
    for k in range(taps):
        start = HALO - taps + 1 + k
        pre = pre + prm[TAPS + k : TAPS + k + 1, :channels] * ext[start : start + length]
    pre_o[0] = pre
    act = (pre * sigmoid(pre)).astype(BF16)
    act_o[0] = act
    step_pre = (
        dot(normed[HALO:], w[:, inner + channels :]) + prm[STEP_BIAS : STEP_BIAS + 1, :LANES]
    )
    step = softplus(step_pre)
    kept, ones = triangle(length)
    log_decay = running_sum(ones, step * prm[RATE : RATE + 1, :LANES])
    doc_col, doc_row = doc_numbers(doc[0], ones)
    entry = jnp.where(doc_col == 0.0, jnp.exp(log_decay), 0.0)
    last = log_decay[length - 1 :]
    tail = jnp.where(doc_col == doc_col[length - 1 :], jnp.exp(last - log_decay), 0.0)
    aux_o[0, :, 0:LANES] = log_decay
    aux_o[0, :, LANES : 2 * LANES] = step
    aux_o[0, :, 2 * LANES : 3 * LANES] = step_pre
    aux_o[0, :, 3 * LANES : 4 * LANES] = entry
    aux_o[0, :, 4 * LANES :] = tail
    spread = head_spread(inner, size)
    values = act[:, :inner].astype(F32)
    inputs = values * expand(step, spread)
    low_inputs = inputs.astype(BF16)
    in_state = act[:, inner : inner + nstate]
    out_state = act[:, inner + nstate :]
    state_o[0] = dot((inputs * expand(tail, spread)).astype(BF16), in_state, TN).astype(BF16)
    scores = dot(out_state, in_state, NT)
    closed = jnp.where(kept & (doc_col == doc_row), 0.0, MASKED)
    log_rows = log_decay.T
    whole_decay = jnp.where(doc_row[:, length - 1 :] == 0.0, jnp.exp(log_rows[:HEAD_ROWS, length - 1 :]), 0.0)
    dec_o[0] = jnp.broadcast_to(whole_decay, (HEAD_ROWS, LANES))
    left = lax.broadcasted_iota(jnp.int32, (length, LANES), 1) < size
    for pair in range(inner // LANES):
        columns = slice(pair * LANES, (pair + 1) * LANES)
        part = low_inputs[:, columns]
        total = None
        for side in range(2):
            h = 2 * pair + side
            decay = jnp.exp(log_decay[:, h : h + 1] - log_rows[h : h + 1] + closed)
            own = jnp.where(left if side == 0 else ~left, part, jnp.zeros_like(part))
            term = dot((scores * decay).astype(BF16), own)
            total = term if total is None else total + term
        scan_o[0, :, columns] = total


def gate_kernel(sizes, scan, act, aux, gate, hin, g, prm, wout, full_o, gn_o, sums_o):
    length, inner, nstate, size, taps = sizes
    spread = head_spread(inner, size)
    values = act[0, :, :inner].astype(F32)
    out_state = act[0, :, inner + nstate :]
    scanned = scan[0] + dot(out_state, hin[0], NT) * expand(aux[0, :, 3 * LANES : 4 * LANES], spread)
    full_o[0] = scanned
    mixed = scanned + prm[SKIP : SKIP + 1, :inner] * values
    gated = mixed * (gate[0] * sigmoid(gate[0]))
    grad_norm = dot(g[0], wout[...])
    gn_o[0] = grad_norm
    squares = jnp.sum(gated * gated, axis=-1, keepdims=True)
    cross = jnp.sum(
        grad_norm * prm[INNER_GAIN : INNER_GAIN + 1, :inner] * gated, axis=-1, keepdims=True
    )
    lane = lax.broadcasted_iota(jnp.int32, (length, LANES), 1)
    sums_o[0] = jnp.where(lane == 0, squares, jnp.where(lane == 1, cross, 0.0))


def output_kernel(
    sizes, total_inner, full, act, aux, gate, gn, sums, sums_in, g, normed, prm, wout,
    keep_o, send_o, dy_o, ggate_o, prior_o, small_o, dout_o, dgate_o, acc_out, acc_gate, wide,
):
    length, inner, nstate, size, taps = sizes
    at = pl.program_id(0)
    spread = head_spread(inner, size)
    values = act[0, :, :inner].astype(F32)
    out_state = act[0, :, inner + nstate :]
    mixed = full[0] + prm[SKIP : SKIP + 1, :inner] * values
    z = gate[0]
    sig = sigmoid(z)
    swish = z * sig
    gated = mixed * swish
    both = sums[0] + sums_in[0]
    inner_scale = lax.rsqrt(both[:, 0:1] / total_inner + EPSILON)
    gain = prm[INNER_GAIN : INNER_GAIN + 1, :inner]
    unit = gated * inner_scale
    normal = (unit * gain).astype(BF16)
    wide[...] = dot(normal, wout[...], NT)
    half = wide.shape[1] // 2
    core = lax.axis_index("head")
    keep_o[0] = wide[:, pl.ds(pl.multiple_of(core * half, LANES), half)]
    send_o[0] = wide[:, pl.ds(pl.multiple_of((1 - core) * half, LANES), half)].astype(BF16)
    grad_norm = gn[0]
    grad_inner = jnp.sum(grad_norm * unit, axis=0, keepdims=True)
    grad_gated = inner_scale * (grad_norm * gain) - unit * (
        inner_scale * inner_scale * (both[:, 1:2] / total_inner)
    )
    dy = grad_gated * swish
    low_dy = dy.astype(BF16)
    dy_o[0] = low_dy
    ggate = (grad_gated * mixed * (sig * (1.0 + z * (1.0 - sig)))).astype(BF16)
    ggate_o[0] = ggate
    grad_skip = jnp.sum(dy * values, axis=0, keepdims=True)
    entry = expand(aux[0, :, 3 * LANES : 4 * LANES], spread)
    prior_o[0] = dot((dy * entry).astype(BF16), out_state, TN).astype(BF16)
    rows = jnp.concatenate([grad_inner, grad_skip, jnp.zeros((6, inner), F32)], axis=0)
    term_out = dot(g[0], normal, TN)
    term_gate = dot(normed[0], ggate, TN)

    @pl.when(at == 0)
    def _():
        small_o[...] = rows
        acc_out[...] = term_out
        acc_gate[...] = term_gate

    @pl.when(at > 0)
    def _():
        small_o[...] += rows
        acc_out[...] += term_out
        acc_gate[...] += term_gate

    @pl.when(at == pl.num_programs(0) - 1)
    def _():
        dout_o[...] = acc_out[...].astype(BF16)
        dgate_o[...] = acc_gate[...].astype(BF16)


def backward_kernel(
    sizes, full, act, aux, dy, hin, later, state, doc, pre, prm,
    gcx_o, own_o, send_o, gpre_o, small_o, edge_o, slope_o, dcb,
):
    length, inner, nstate, size, taps = sizes
    at = pl.program_id(0)
    core = lax.axis_index("head")
    spread = head_spread(inner, size)
    log_decay = aux[0, :, 0:LANES]
    step = aux[0, :, LANES : 2 * LANES]
    step_pre = aux[0, :, 2 * LANES : 3 * LANES]
    entry = aux[0, :, 3 * LANES : 4 * LANES]
    tail = aux[0, :, 4 * LANES :]
    values = act[0, :, :inner].astype(F32)
    in_state = act[0, :, inner : inner + nstate]
    out_state = act[0, :, inner + nstate :]
    low_dy = dy[0]
    wide_dy = low_dy.astype(F32)
    step_wide = expand(step, spread)
    tail_wide = expand(tail, spread)
    entry_wide = expand(entry, spread)
    inputs = values * step_wide
    low_inputs = inputs.astype(BF16)
    kept, ones = triangle(length)
    upper, ones_upper = triangle(length, True)
    doc_col, doc_row = doc_numbers(doc[0], ones)
    closed = jnp.where(upper & (doc_col == doc_row), 0.0, MASKED)
    scores = dot(in_state, out_state, NT)
    log_rows = log_decay.T
    left = lax.broadcasted_iota(jnp.int32, (length, LANES), 1) < size
    grad_inputs = tail_wide * dot(in_state, later[0], NT)
    parts = []
    for pair in range(inner // LANES):
        columns = slice(pair * LANES, (pair + 1) * LANES)
        pair_dy = low_dy[:, columns]
        pair_in = low_inputs[:, columns]
        total = grad_inputs[:, columns]
        for side in range(2):
            h = 2 * pair + side
            chosen = left if side == 0 else ~left
            own_dy = jnp.where(chosen, pair_dy, jnp.zeros_like(pair_dy))
            decay = jnp.exp(log_rows[h : h + 1] - log_decay[:, h : h + 1] + closed)
            total = total + dot((scores * decay).astype(BF16), own_dy)
            grad_decay = dot(pair_in, own_dy, NT) * decay
            if h == 0:
                dcb[...] = grad_decay
            else:
                dcb[...] += grad_decay
        parts.append(total)
    grad_inputs = jnp.concatenate(parts, axis=1)
    grad_scores = dcb[...]
    grad_in = dot(grad_scores.astype(BF16), out_state) + dot(
        (inputs * tail_wide).astype(BF16), later[0]
    )
    grad_out = dot(grad_scores.T.astype(BF16), in_state) + dot(
        (wide_dy * entry_wide).astype(BF16), hin[0]
    )
    entry_last = jnp.broadcast_to(entry[length - 1 :], (8, LANES))
    later_wide = later[0].astype(F32)
    lane_ones = jnp.ones((8, nstate), BF16)
    through = head_sums(
        sum(dot(lane_ones, piece, NT) for piece in split2(later_wide * hin[0].astype(F32))), spread
    )
    born = head_sums(
        sum(dot(lane_ones, piece, NT) for piece in split2(later_wide * state[0].astype(F32))), spread
    )
    ending = (born + entry_last * through)[:1]
    grad_log = head_sums(wide_dy * full[0], spread) - head_sums(
        low_inputs.astype(F32) * grad_inputs, spread
    )
    grad_rate_step = running_sum(ones_upper, grad_log) + ending
    rate = prm[RATE : RATE + 1, :LANES]
    grad_step = head_sums(values * grad_inputs, spread) + rate * grad_rate_step
    gpre = grad_step * sigmoid(step_pre)
    lane = lax.broadcasted_iota(jnp.int32, (length, LANES), 1)
    gpre = jnp.where(lane < inner // size, gpre, 0.0)
    gpre_o[0] = gpre
    grad_values = step_wide * grad_inputs + prm[SKIP : SKIP + 1, :inner] * wide_dy
    px = pre[0, :, :inner]
    sig = sigmoid(px)
    gcx = grad_values * (sig * (1.0 + px * (1.0 - sig)))
    gcx_o[0] = gcx
    edge_o[0] = gcx[:EDGE]
    is_first = core == 0
    own_o[0] = jnp.where(is_first, grad_in, grad_out)
    send_o[0] = jnp.where(is_first, grad_out, grad_in).astype(BF16)
    ps = pre[0, :EDGE, pl.ds(pl.multiple_of(inner + core * nstate, LANES), nstate)]
    sig = sigmoid(ps)
    slope_o[0] = sig * (1.0 + ps * (1.0 - sig))
    rows = jnp.concatenate(
        [
            jnp.sum(gpre, axis=0, keepdims=True),
            rate * jnp.sum(step * grad_rate_step, axis=0, keepdims=True),
            jnp.zeros((6, LANES), F32),
        ],
        axis=0,
    )

    @pl.when(at == 0)
    def _():
        small_o[...] = rows

    @pl.when(at > 0)
    def _():
        small_o[...] += rows


def conv_kernel(
    sizes, gcx, own, recv, edge, edge_state, pre, xs, gpre, ggate, normed, prm, w,
    part_o, dx_o, small_o, acc, ext, gext,
):
    length, inner, nstate, size, taps = sizes
    at = pl.program_id(0)
    core = lax.axis_index("head")
    last = lax.axis_index("seq") == lax.axis_size("seq") - 1
    mine = pl.ds(pl.multiple_of(inner + core * nstate, LANES), nstate)
    channels = inner + nstate
    ps = pre[0, :, mine]
    sig = sigmoid(ps)
    gst = (own[0] + recv[0].astype(F32)) * (sig * (1.0 + ps * (1.0 - sig)))
    gext[:length, :inner] = gcx[0]
    gext[:length, inner:] = gst
    gext[length:, :inner] = jnp.where(last, 0.0, edge[0])
    gext[length:, inner:] = jnp.where(last, 0.0, edge_state[0])
    ext[:, :inner] = xs[0, :, :inner].astype(F32)
    ext[:, inner:] = xs[0, :, mine].astype(F32)
    grad_conv = gext[:length]
    grad_in = None
    rows = []
    for k in range(taps):
        row = jnp.concatenate(
            [prm[TAPS + k : TAPS + k + 1, :inner], prm[TAPS + k : TAPS + k + 1, mine]], axis=1
        )
        term = row * gext[taps - 1 - k : taps - 1 - k + length]
        grad_in = term if grad_in is None else grad_in + term
        start = HALO - taps + 1 + k
        rows.append(jnp.sum(ext[start : start + length] * grad_conv, axis=0, keepdims=True))
    rows.append(jnp.sum(grad_conv, axis=0, keepdims=True))
    rows.append(jnp.zeros((8 - taps - 1, channels), F32))
    rows = jnp.concatenate(rows, axis=0)
    low = grad_in.astype(BF16)
    low_pre = gpre[0].astype(BF16)
    part = dot(ggate[0], w[:, :inner], NT)
    part = part + dot(low[:, :inner], w[:, inner : 2 * inner], NT)
    wst = w[:, pl.ds(pl.multiple_of(2 * inner + core * nstate, LANES), nstate)]
    part = part + dot(low[:, inner:], wst, NT)
    part = part + dot(low_pre, w[:, 2 * inner + 2 * nstate :], NT)
    part_o[0] = part.astype(BF16)
    stacked = jnp.concatenate([low, low_pre], axis=1)
    term = dot(normed[0], stacked, TN)

    @pl.when(at == 0)
    def _():
        small_o[...] = rows
        acc[...] = term

    @pl.when(at > 0)
    def _():
        small_o[...] += rows
        acc[...] += term

    @pl.when(at == pl.num_programs(0) - 1)
    def _():
        dx_o[...] = acc[...].astype(BF16)


def tokens_kernel(sizes, tok, part, recv, g, prm, out_o, small_o, wide):
    at = pl.program_id(0)
    core = lax.axis_index("head")
    x = tok[0].astype(F32)
    model = x.shape[1]
    scale = lax.rsqrt(jnp.mean(x * x, axis=-1, keepdims=True) + EPSILON)
    unit = x * scale
    grad_normed = part[0].astype(F32) + recv[0].astype(F32)
    r = grad_normed * prm[GAIN : GAIN + 1, :model]
    wide[...] = scale * (r - unit * jnp.mean(r * unit, axis=-1, keepdims=True))
    half = model // 2
    out_o[0] = g[0].astype(F32) + wide[:, pl.ds(pl.multiple_of(core * half, LANES), half)]
    rows = jnp.concatenate(
        [jnp.sum(grad_normed * unit, axis=0, keepdims=True), jnp.zeros((7, model), F32)], axis=0
    )

    @pl.when(at == 0)
    def _():
        small_o[...] = rows

    @pl.when(at > 0)
    def _():
        small_o[...] += rows


def swap_heads(v):
    return lax.ppermute(v, "head", [(0, 1), (1, 0)])


def shift(v, distance):
    devices = range(lax.axis_size("seq"))
    return lax.ppermute(
        v, "seq", [(i - distance, i) for i in devices if i - distance in devices]
    )


def plain_gather(w_in, w_out, tokens, grads, tails):
    return (
        lax.all_gather(w_in, "seq", axis=0, tiled=True),
        lax.all_gather(w_out, "seq", axis=0, tiled=True),
        lax.all_gather(tokens, "head", axis=2, tiled=True),
        lax.all_gather(grads, "head", axis=2, tiled=True),
        lax.all_gather(shift(tails, 1), "head", axis=2, tiled=True),
    )


def plain_scan(state, decay, size, backward):
    count, place = lax.axis_size("seq"), lax.axis_index("seq")
    heads = state.shape[1] // size
    wide = jnp.repeat(decay[:, :heads, 0], size, axis=1)[..., None]
    states = lax.all_gather(state, "seq")
    decays = lax.all_gather(wide, "seq")

    def one(k, carried):
        at = count - 1 - k if backward else k
        reached = at > place if backward else at < place
        return jnp.where(reached, decays[at] * carried + states[at].astype(F32), carried)

    return lax.fori_loop(0, count, one, jnp.zeros(state.shape, F32)).astype(BF16)


def plain_states(send, own, slope, edge):
    recv = swap_heads(send)
    mine = (own[:, :EDGE] + recv[:, :EDGE].astype(F32)) * slope
    return recv, shift(edge, -1), shift(mine, -1)


def plain_sum(pieces, small, shared):
    totals = [
        lax.psum_scatter(p.astype(F32), "seq", scatter_dimension=0, tiled=True) for p in pieces
    ]
    shared = lax.psum(shared, ("seq", "head"))
    return totals, lax.psum(small, "seq"), shared


def plain_both(v):
    return lax.all_gather(v, "head", axis=1, tiled=True)


PLANE = 4
LINE = 4
OFFSETS = (0, -1, 1, -2, 2, -3, 3)


def place():
    s, c = lax.axis_index("seq"), lax.axis_index("head")
    return s, c, s // PLANE, (s // 2) % 2, s % 2


def remote(src, dst, send_sem, recv_sem, device):
    return pltpu.make_async_remote_copy(
        src_ref=src,
        dst_ref=dst,
        send_sem=send_sem,
        recv_sem=recv_sem,
        device_id=device,
        device_id_type=MESH,
    )


def greet(relations):
    barrier = pltpu.get_barrier_semaphore()
    total = 0
    for exists, device in relations:
        if exists is True:
            pl.semaphore_signal(barrier, inc=1, device_id=device, device_id_type=MESH)
            total = total + 1
        else:
            pl.when(exists)(
                functools.partial(
                    pl.semaphore_signal, barrier, inc=1, device_id=device, device_id_type=MESH
                )
            )
            total = total + jnp.where(exists, 1, 0)
    pl.semaphore_wait(barrier, total)


def comm_call(kernel, ins, outs, scratch, collective, name, anywhere=False):
    space = pl.ANY if anywhere else pltpu.VMEM
    return pl.pallas_call(
        kernel,
        in_specs=[pl.BlockSpec(memory_space=space) for _ in ins],
        out_specs=[pl.BlockSpec(memory_space=space) for _ in outs],
        out_shape=outs,
        scratch_shapes=list(scratch),
        compiler_params=pltpu.CompilerParams(
            collective_id=collective, has_side_effects=True, vmem_limit_bytes=VMEM_LIMIT
        ),
        name=name,
    )(*ins)


def dma(*dims):
    return pltpu.SemaphoreType.DMA(dims)


SUM_OFFSETS = (3, -3, 2, -2, 1, -1, 0)


class Refs:
    def __init__(self, names, refs):
        self.__dict__.update(zip(names, refs))


def fused_call(body, steps, ins, outs, scratch, collective, name):
    names = list(ins) + list(outs) + list(scratch)

    def kernel(*refs):
        body(Refs(names, refs))

    results = pl.pallas_call(
        kernel,
        grid=(steps,) if steps else (),
        in_specs=[spec for _, spec in ins.values()],
        out_specs=[spec for _, spec in outs.values()],
        out_shape=[shaped for shaped, _ in outs.values()],
        scratch_shapes=list(scratch.values()),
        compiler_params=pltpu.CompilerParams(
            collective_id=collective,
            has_side_effects=True,
            vmem_limit_bytes=VMEM_LIMIT,
            dimension_semantics=("arbitrary",) if steps else None,
        ),
        name=name,
    )(*[array for array, _ in ins.values()])
    return Refs(list(outs), results)


ANYWHERE = pl.BlockSpec(memory_space=pl.ANY)
INSIDE = pl.BlockSpec(memory_space=pltpu.VMEM)


def stepped(array, index):
    rank = len(array.shape)
    return pl.BlockSpec((1,) + tuple(array.shape[1:]), lambda k: (index(k),) + (0,) * (rank - 1))


def during(first, count=4):
    return lambda k: jnp.clip(k - first, 0, count - 1)


def cyclic(last, count=4):
    return lambda k: jnp.where(k < last, k % count, count - 1)


def either(core, own, other):
    low = jnp.where(core == 0, own, other)
    return jnp.concatenate([low, jnp.where(core == 0, other, own)], axis=1)


class Gather:
    def __init__(self, pieces, rows, sems):
        self.pieces, self.rows = pieces, rows
        self.local, self.zs, self.zr, self.as_, self.ar, self.bs, self.br = sems
        self.s, self.c, self.z, self.y, self.x = place()
        s, c = self.s, self.c
        self.up, self.down = self.z < LINE - 1, self.z > 0
        self.to_x, self.to_y = (s + 1 - 2 * self.x, c), (s + 2 - 4 * self.y, c)
        self.to_up, self.to_down = (s + PLANE, c), (s - PLANE, c)
        self.span = range(len(pieces))

    @staticmethod
    def semaphores(n):
        return dict(
            g0=dma(n), g1=dma(n, 2, 4), g2=dma(n, 4), g3=dma(n, 4), g4=dma(n, 4), g5=dma(n, 4, 2),
            g6=dma(n, 4, 2),
        )

    def at(self, p, index, count=1):
        src, dst, start, width, order = self.pieces[p]
        begin = pl.multiple_of(index * self.rows, 16)
        return dst.at[pl.ds(begin, count * self.rows), pl.ds(start, width)]

    def own(self, p):
        src, dst, start, width, order = self.pieces[p]
        return src.at[:, pl.ds(start, width)]

    def local_copy(self, p):
        return pltpu.make_async_copy(self.own(p), self.at(p, self.s), self.local.at[p])

    def z_copy(self, p, off):
        zz = self.z + off
        dst = self.at(p, zz * PLANE + self.y * 2 + self.x)
        src = self.own(p) if off == 0 else dst
        step = abs(off)
        moves = []
        if off <= 0:
            sems = self.zs.at[p, 0, step], self.zr.at[p, zz]
            moves.append((self.up, remote(src, dst, *sems, self.to_up)))
        if off >= 0:
            sems = self.zs.at[p, 1, step], self.zr.at[p, zz]
            moves.append((self.down, remote(src, dst, *sems, self.to_down)))
        return moves

    def first_copy(self, p, off):
        zz = self.z + off
        dst = self.at(p, zz * PLANE + self.y * 2 + self.x)
        src = self.own(p) if off == 0 else dst
        device = self.to_x if self.pieces[p][4] else self.to_y
        return remote(src, dst, self.as_.at[p, zz], self.ar.at[p, zz], device)

    def second_copies(self, p, off):
        zz = self.z + off
        if self.pieces[p][4]:
            pair = self.at(p, zz * PLANE + self.y * 2, 2)
            return [remote(pair, pair, self.bs.at[p, zz, 0], self.br.at[p, zz, 0], self.to_y)]
        copies = []
        for k in range(2):
            block = self.at(p, zz * PLANE + k * 2 + self.x)
            copies.append(
                remote(block, block, self.bs.at[p, zz, k], self.br.at[p, zz, k], self.to_x)
            )
        return copies

    def exists(self, off):
        zz = self.z + off
        return (zz >= 0) & (zz < LINE)

    def begin(self):
        for p in self.span:
            for there, copy in self.z_copy(p, 0):
                pl.when(there)(copy.start)
            self.first_copy(p, 0).start()
            self.local_copy(p).start()

    def z_arrived(self, *offs):
        for off in offs:

            @pl.when(self.exists(off))
            def _():
                for p in self.span:
                    for there, copy in self.z_copy(p, off):
                        copy.wait_recv()
                        pl.when(there)(copy.start)
                    self.first_copy(p, off).start()

    def first_arrived(self, *offs):
        for off in offs:

            @pl.when(self.exists(off))
            def _():
                for p in self.span:
                    if off == 0:
                        self.local_copy(p).wait()
                    self.first_copy(p, off).wait_recv()
                    for copy in self.second_copies(p, off):
                        copy.start()

    def finish(self):
        for off in OFFSETS:

            @pl.when(self.exists(off))
            def _():
                for p in self.span:
                    for copy in self.second_copies(p, off):
                        copy.wait()
                    self.first_copy(p, off).wait_send()
                    for there, copy in self.z_copy(p, off):
                        pl.when(there)(copy.wait_send)


class Scan:
    def __init__(self, backward, size, state, decay, out, refs):
        self.state, self.decay, self.out, self.size = state, decay, out, size
        (
            self.slots, self.rates, self.total, self.through, self.arriving, self.leaving,
            self.staged, self.s1, self.r1, self.s2, self.r2, self.zs, self.zr, self.s3, self.r3,
        ) = refs
        s, c, z, y, x = place()
        self.c, self.p = c, s % PLANE
        self.base = s - self.p
        self.order = tuple(range(PLANE - 1, -1, -1)) if backward else tuple(range(PLANE))
        self.rows = state.shape[1] // PLANE
        self.place = LINE - 1 - z if backward else z
        self.before, self.after = self.place > 0, self.place < LINE - 1
        self.step = -PLANE if backward else PLANE
        self.s = s

    @staticmethod
    def scratch(count, rows, nstate, heads):
        quarter = rows // PLANE
        return dict(
            slots=pltpu.VMEM((count, PLANE, quarter, nstate), BF16),
            rates=pltpu.VMEM((count, PLANE, heads, nstate), F32),
            total=pltpu.VMEM((count, quarter, nstate), F32),
            through=pltpu.VMEM((count, 8, nstate), F32),
            arriving=pltpu.VMEM((count, quarter, nstate), BF16),
            leaving=pltpu.VMEM((count, quarter, nstate), BF16),
            staged=pltpu.VMEM((count, PLANE, quarter, nstate), BF16),
            s1=dma(count, PLANE), r1=dma(count, PLANE),
            s2=dma(count, PLANE), r2=dma(count, PLANE),
            zs=dma(count), zr=dma(count),
            s3=dma(count, PLANE), r3=dma(count, PLANE),
        )

    def relations(self):
        plane = [(self.p != j, (self.base + j, self.c)) for j in range(PLANE)]
        return plane + [
            (self.before, (self.s - self.step, self.c)),
            (self.after, (self.s + self.step, self.c)),
        ]

    def part(self, j):
        return pl.ds(pl.multiple_of(j * self.rows, 16), self.rows)

    def first(self, i, j, slot):
        device = (self.base + j, self.c)
        return [
            remote(
                self.state.at[i, self.part(j)], self.slots.at[i, slot],
                self.s1.at[i, j], self.r1.at[i, slot], device,
            ),
            remote(
                self.decay.at[i], self.rates.at[i, slot], self.s2.at[i, j], self.r2.at[i, slot],
                device,
            ),
        ]

    def z_copy(self, i):
        return remote(
            self.leaving.at[i], self.arriving.at[i], self.zs.at[i], self.zr.at[i],
            (self.s + self.step, self.c),
        )

    def last(self, i, j, quarter):
        return remote(
            self.staged.at[i, j], self.out.at[i, self.part(quarter)],
            self.s3.at[i, j], self.r3.at[i, quarter], (self.base + j, self.c),
        )

    def others(self, act):
        for j in range(PLANE):
            pl.when(self.p != j)(functools.partial(act, j))

    def start(self, i):
        def send(j):
            for copy in self.first(i, j, self.p):
                copy.start()

        self.others(send)
        self.slots[i, self.p] = self.state[i, self.part(self.p)]
        self.rates[i, self.p] = self.decay[i]

    def pieces(self):
        for n in range(self.rows // self.size):
            yield n, slice(n * self.size, (n + 1) * self.size)

    def rate(self, i, j, n):
        return self.rates[i, j, pl.ds(self.p * (self.rows // self.size) + n, 1)]

    def fold(self, i):
        def arrived(j):
            for copy in self.first(i, j, j):
                copy.wait_recv()

        self.others(arrived)
        for n, rows in self.pieces():
            held = self.slots[i, self.order[0], rows].astype(F32)
            rate = self.rate(i, self.order[0], n)
            for j in self.order[1:]:
                own = self.rate(i, j, n)
                held = own * held + self.slots[i, j, rows].astype(F32)
                rate = own * rate
            self.total[i, rows] = held
            self.through[i, n : n + 1] = rate

    def chain(self, i):
        @pl.when(self.before)
        def _():
            self.z_copy(i).wait_recv()

        @pl.when(jnp.logical_not(self.before))
        def _():
            self.arriving[i] = jnp.zeros(self.arriving.shape[1:], BF16)

        for n, rows in self.pieces():
            self.leaving[i, rows] = (
                self.total[i, rows]
                + self.through[i, n : n + 1] * self.arriving[i, rows].astype(F32)
            ).astype(BF16)
        pl.when(self.after)(self.z_copy(i).start)
        for n, rows in self.pieces():
            held = self.arriving[i, rows].astype(F32)
            for at, j in enumerate(self.order):
                self.staged[i, j, rows] = held.astype(BF16)
                if at < PLANE - 1:
                    held = self.rate(i, j, n) * held + self.slots[i, j, rows].astype(F32)
        self.others(lambda j: self.last(i, j, self.p).start())
        self.out[i, self.part(self.p)] = self.staged[i, self.p]

    def events(self, k):
        count = self.state.shape[0]
        pl.when((k >= 0) & (k < count))(lambda: self.start(k))
        pl.when((k >= 1) & (k <= count))(lambda: self.fold(k - 1))
        at = k - 1 - self.place
        pl.when((at >= 0) & (at < count))(lambda: self.chain(at))

    def arrived(self, i):
        self.others(lambda j: self.last(i, j, j).wait_recv())

    def finish(self):
        @pl.loop(0, self.state.shape[0])
        def _(i):
            def close(j):
                for copy in self.first(i, j, self.p):
                    copy.wait_send()
                self.last(i, j, self.p).wait_send()

            self.others(close)
            pl.when(self.after)(self.z_copy(i).wait_send)


class Reduce:
    def __init__(self, pieces, rows, refs):
        self.pieces, self.rows = pieces, rows
        (
            self.near, self.mid, self.above, self.below, self.mid_send, self.kept,
            self.s1, self.r1, self.s2, self.r2, self.sz, self.rz,
        ) = refs
        self.s, self.c, self.z, self.y, self.x = place()
        s, c = self.s, self.c
        self.up, self.down = self.z < LINE - 1, self.z > 0
        self.to_x, self.to_y = (s + 1 - 2 * self.x, c), (s + 2 - 4 * self.y, c)
        self.to_up, self.to_down = (s + PLANE, c), (s - PLANE, c)
        self.span = range(len(pieces))

    @staticmethod
    def scratch(n, rows, wide):
        return dict(
            near=pltpu.VMEM((LINE, 2 * rows, wide), BF16),
            mid=pltpu.VMEM((LINE, rows, wide), BF16),
            above=pltpu.VMEM((LINE, rows, wide), BF16),
            below=pltpu.VMEM((LINE, rows, wide), BF16),
            mid_send=pltpu.VMEM((LINE, rows, wide), BF16),
            kept=pltpu.VMEM((LINE, rows, wide), F32),
            t1=dma(n, LINE, 2), u1=dma(n, LINE, 2), t2=dma(n, LINE),
            u2=dma(n, LINE), tz=dma(n, LINE), uz=dma(n, 2, LINE),
        )

    def columns(self, p):
        return pl.ds(self.pieces[p][6], self.pieces[p][2])

    def source(self, p, index, count=1):
        ref, start, width = self.pieces[p][:3]
        begin = pl.multiple_of(index * self.rows, 16)
        return ref.at[pl.ds(begin, count * self.rows), pl.ds(start, width)]

    def index(self, zz, yy, xx):
        return zz * PLANE + yy * 2 + xx

    def near_copies(self, p, zz):
        if self.pieces[p][3]:
            return [
                remote(
                    self.source(p, self.index(zz, 1 - self.y, 0), 2),
                    self.near.at[zz, :, self.columns(p)],
                    self.s1.at[p, zz, 0], self.r1.at[p, zz, 0], self.to_y,
                )
            ]
        return [
            remote(
                self.source(p, self.index(zz, k, 1 - self.x)),
                self.near.at[zz, pl.ds(k * self.rows, self.rows), self.columns(p)],
                self.s1.at[p, zz, k], self.r1.at[p, zz, k], self.to_x,
            )
            for k in range(2)
        ]

    def mid_copy(self, p, zz):
        at = self.columns(p)
        return remote(
            self.mid_send.at[zz, :, at], self.mid.at[zz, :, at],
            self.s2.at[p, zz], self.r2.at[p, zz], self.to_x if self.pieces[p][3] else self.to_y,
        )

    def line_copy(self, p, zz, upward):
        at = self.columns(p)
        target = self.above if upward else self.below
        return remote(
            self.mid_send.at[zz, :, at], target.at[zz, :, at],
            self.sz.at[p, zz], self.rz.at[p, 0 if upward else 1, zz],
            self.to_up if upward else self.to_down,
        )

    def exists(self, off):
        zz = self.z + off
        return (zz >= 0) & (zz < LINE)

    def rows_of(self, k):
        return pl.ds(pl.multiple_of(k * self.rows, 16), self.rows)

    def begin(self, *pieces):
        for off in SUM_OFFSETS:

            @pl.when(self.exists(off))
            def _():
                for p in pieces or self.span:
                    for copy in self.near_copies(p, self.z + off):
                        copy.start()

    def second(self, *offs):
        for off in offs:

            @pl.when(self.exists(off))
            def _():
                zz = self.z + off
                y, x = self.y, self.x
                for p in self.span:
                    for copy in self.near_copies(p, zz):
                        copy.wait_recv()
                    own = self.index(zz, y, x)
                    if self.pieces[p][3]:
                        other, mine = self.index(zz, y, 1 - x), x
                    else:
                        other, mine = self.index(zz, 1 - y, x), y
                    at = self.columns(p)
                    sent = self.source(p, other)[...].astype(F32) + self.near[
                        zz, self.rows_of(1 - mine), at
                    ].astype(F32)
                    self.mid_send[zz, :, at] = sent.astype(BF16)
                    self.mid_copy(p, zz).start()
                    self.kept[zz, :, at] = self.source(p, own)[...].astype(F32) + self.near[
                        zz, self.rows_of(mine), at
                    ].astype(F32)

    def third(self, *offs, only=None):
        for off in offs:

            @pl.when(self.exists(off))
            def _():
                zz = self.z + off
                for p in self.span if only is None else only:
                    at = self.columns(p)
                    self.mid_copy(p, zz).wait_recv()
                    self.kept[zz, :, at] = self.kept[zz, :, at] + self.mid[zz, :, at].astype(F32)
                    if off >= 0:

                        @pl.when(self.down)
                        def _():
                            self.line_copy(p, zz, True).wait_recv()
                            self.kept[zz, :, at] = self.kept[zz, :, at] + self.above[
                                zz, :, at
                            ].astype(F32)

                    if off <= 0:

                        @pl.when(self.up)
                        def _():
                            self.line_copy(p, zz, False).wait_recv()
                            self.kept[zz, :, at] = self.kept[zz, :, at] + self.below[
                                zz, :, at
                            ].astype(F32)

                    if off == 0:
                        _, _, width, _, out, start, _ = self.pieces[p]
                        out[:, start : start + width] = self.kept[zz, :, at]
                    else:
                        self.mid_copy(p, zz).wait_send()
                        self.mid_send[zz, :, at] = self.kept[zz, :, at].astype(BF16)
                        self.line_copy(p, zz, off > 0).start()

    def finish(self):
        for off in SUM_OFFSETS:

            @pl.when(self.exists(off))
            def _():
                zz = self.z + off
                for p in self.span:
                    for copy in self.near_copies(p, zz):
                        copy.wait_send()
                    if off == 0:
                        self.mid_copy(p, zz).wait_send()
                    else:
                        self.line_copy(p, zz, off > 0).wait_send()


def picked(r, names):
    return tuple(r.__dict__[n] for n in names)


GATHER_REFS = tuple(Gather.semaphores(1))
SCAN_REFS = tuple(Scan.scratch(1, PLANE, 1, 1))
REDUCE_REFS = tuple(Reduce.scratch(1, 16, 1))


def main_body(sizes, total_inner, r):
    length, inner, nstate, size, taps = sizes
    channels = inner + 2 * nstate
    heads = inner // size
    count = r.tok.shape[0]
    half = r.tok.shape[2]
    s, c, z, y, x = place()
    to_core, to_prv = (s, 1 - c), (s - 1, c)
    nxt, prv = s < LINE * PLANE - 1, s > 0
    first_gather = Gather(
        ((r.w1, r.w, 0, 640, True), (r.w1, r.w, 640, r.w1.shape[1] - 640, False)),
        r.w1.shape[0],
        picked(r, GATHER_REFS),
    )
    second_gather = Gather(
        ((r.w2, r.w2_full, 0, inner, True), (r.w2, r.w2_full, inner, inner, False)),
        r.w2.shape[0],
        picked(r, SECOND_REFS),
    )
    prefix = Scan(False, size, r.state, r.dec, r.hin, picked(r, SCAN_REFS))
    suffix = Scan(True, size, r.prior, r.dec, r.later, picked(r, SUFFIX_REFS))
    reduce_ = Reduce(
        ((r.dout, 0, inner, True, r.g_out, 0, 0), (r.dgate, 0, inner, False, r.g_gate, 0, inner)),
        r.g_out.shape[0],
        picked(r, REDUCE_REFS),
    )
    spread = head_spread(inner, size)
    mine = pl.ds(pl.multiple_of(inner + c * nstate, LANES), nstate)
    side = pl.ds(pl.multiple_of(c * half, LANES), half)
    other_side = pl.ds(pl.multiple_of((1 - c) * half, LANES), half)
    log_at, step_at, pre_at, entry_at, tail_at = (
        slice(n * LANES, (n + 1) * LANES) for n in range(5)
    )
    own_at, slope_at, gpre_at = (
        slice(half + n * nstate, half + (n + 1) * nstate) for n in range(3)
    )
    left = lax.broadcasted_iota(jnp.int32, (length, LANES), 1) < size

    def swap(n, source, target):
        return lambda i: remote(
            source.at[i], target.at[i], r.ss.at[n, i], r.rs.at[n, i], to_core
        )

    swap_tokens = swap(0, r.tok, r.tok_in)
    swap_grads = swap(1, r.g, r.g_in)
    swap_sums = swap(2, r.sums, r.sums_in)
    swap_out = swap(3, r.osend, r.out_in)
    swap_states = swap(4, r.bsend, r.brecv)

    def send_edge(i):
        return remote(r.edge.at[i], r.edge_in.at[i], r.ss.at[5, i], r.rs.at[5, i], to_prv)

    def halo_copy(k):
        tails = r.tok.at[:, pl.ds(length - HALO, HALO), :]
        device = (s + 1, c if k == 0 else 1 - c)
        return remote(tails, r.halo.at[:, :, side], r.hs.at[k], r.hr.at[k], device)

    stores = dict(
        normed=lambda i: (r.normed_s.at[i, pl.ds(HALO, length)], r.normed.at[i]),
        xs=lambda i: (r.xs_s.at[i], r.xs.at[i]),
        ggate=lambda i: (r.ggate_s.at[i], r.ggate.at[i]),
        keep=lambda i: (r.gate.at[i, :, pl.ds(0, half)], r.keep.at[i]),
        gcx=lambda i: (r.gn.at[i], r.gcx.at[i]),
        gpre=lambda i: (r.gate.at[i, :, gpre_at], r.gpre.at[i]),
        gst=lambda i: (r.gate.at[i, :, own_at], r.gst.at[i]),
        w=lambda i: (r.w, r.w_out),
        w2=lambda i: (r.w2_full.at[:, pl.ds(0, inner)], r.w2_out),
    )

    def store(name, i):
        source, target = stores[name](i)
        n = tuple(stores).index(name)
        return pltpu.make_async_copy(source, target, r.store.at[n, i])

    def bias_row(at):
        return r.prm[BIAS : BIAS + 1, at]

    def conv(at):
        pre = r.prm[BIAS : BIAS + 1, at]
        for t in range(taps):
            start = HALO - taps + 1 + t
            pre = pre + r.prm[TAPS + t : TAPS + t + 1, at] * r.ext[start : start + length, at]
        return pre

    greet(
        prefix.relations()
        + [
            (True, to_core),
            (nxt, (s + 1, c)),
            (nxt, (s + 1, 1 - c)),
            (prv, (s - 1, c)),
            (prv, (s - 1, 1 - c)),
        ]
    )
    first_gather.begin()
    for k in range(2):
        pl.when(nxt)(halo_copy(k).start)
    for i in range(count):
        swap_tokens(i).start()
    r.small[...] = jnp.zeros_like(r.small)
    first_gather.z_arrived(-1, 1)
    first_gather.first_arrived(0)
    for i in range(count):
        swap_grads(i).start()

    @pl.loop(0, count)
    def _(i):
        swap_tokens(i).wait()
        own, other = r.tok[i].astype(F32), r.tok_in[i].astype(F32)
        scale = lax.rsqrt(
            jnp.mean(own * own + other * other, axis=-1, keepdims=True) * 0.5 + EPSILON
        )
        gain_own = r.prm[GAIN : GAIN + 1, side]
        gain_other = r.prm[GAIN : GAIN + 1, other_side]
        r.normed_s[i, HALO:, side] = (own * scale * gain_own).astype(BF16)
        r.normed_s[i, HALO:, other_side] = (other * scale * gain_other).astype(BF16)

    first_gather.z_arrived(-2, 2)
    first_gather.first_arrived(-1, 1)
    for k in range(2):
        pl.when(nxt)(halo_copy(k).wait_send)
        pl.when(prv)(halo_copy(k).wait_recv)

    @pl.when(prv)
    def _():
        for i in range(count):
            edge = r.halo[i].astype(F32)
            scale = lax.rsqrt(jnp.mean(edge * edge, axis=-1, keepdims=True) + EPSILON)
            r.normed_s[i, :HALO] = (
                edge * scale * r.prm[GAIN : GAIN + 1, : edge.shape[1]]
            ).astype(BF16)

    @pl.when(jnp.logical_not(prv))
    def _():
        for i in range(count):
            r.normed_s[i, :HALO] = jnp.zeros((HALO, 2 * half), BF16)

    first_gather.z_arrived(-3, 3)
    first_gather.first_arrived(-2, 2, -3, 3)
    second_gather.begin()
    first_gather.finish()
    store("w", 0).start()
    kept, ones = triangle(length)

    @pl.loop(0, count)
    def _(i):
        xs = dot(r.normed_s[i], r.w[:, :channels]).astype(BF16)
        r.xs_s[i] = xs
        r.ext[...] = xs.astype(F32)
        pre = conv(slice(0, channels))
        act = (pre * sigmoid(pre)).astype(BF16)
        r.act[i] = act
        step_pre = (
            dot(r.normed_s[i, HALO:], r.w[:, channels:])
            + r.prm[STEP_BIAS : STEP_BIAS + 1, :LANES]
        )
        step = softplus(step_pre)
        log_decay = running_sum(ones, step * r.prm[RATE : RATE + 1, :LANES])
        doc_col, doc_row = doc_numbers(r.doc[i], ones)
        entry = jnp.where(doc_col == 0.0, jnp.exp(log_decay), 0.0)
        last = log_decay[length - 1 :]
        tail = jnp.where(doc_col == doc_col[length - 1 :], jnp.exp(last - log_decay), 0.0)
        r.aux[i, :, log_at] = log_decay
        r.aux[i, :, step_at] = step
        r.aux[i, :, pre_at] = step_pre
        r.aux[i, :, entry_at] = entry
        r.aux[i, :, tail_at] = tail
        log_rows = log_decay.T
        whole_decay = jnp.where(
            doc_row[:, length - 1 :] == 0.0, jnp.exp(log_rows[:HEAD_ROWS, length - 1 :]), 0.0
        )
        r.dec[i] = jnp.broadcast_to(whole_decay, (HEAD_ROWS, LANES))
        inputs = act[:, :inner].astype(F32) * expand(step, spread)
        r.low[i] = inputs.astype(BF16)
        r.state[i] = dot(
            (inputs * expand(tail, spread)).astype(BF16), act[:, inner : inner + nstate], TN
        ).astype(BF16)
        prefix.events(i)
        store("normed", i).start()
        store("xs", i).start()

        @pl.when(i == 1)
        def _():
            second_gather.z_arrived(-1, 1)
            second_gather.first_arrived(0)

        @pl.when(i == 2)
        def _():
            second_gather.z_arrived(-2, 2)
            second_gather.first_arrived(-1, 1)

        @pl.when(i == 3)
        def _():
            second_gather.z_arrived(-3, 3)
            second_gather.first_arrived(-2, 2)

    @pl.loop(0, count)
    def _(i):
        log_decay = r.aux[i, :, log_at]
        log_rows = log_decay.T
        doc_col, doc_row = doc_numbers(r.doc[i], ones)
        closed = jnp.where(kept & (doc_col == doc_row), 0.0, MASKED)
        scores = dot(r.act[i, :, inner + nstate :], r.act[i, :, inner : inner + nstate], NT)
        for pair in range(inner // LANES):
            columns = slice(pair * LANES, (pair + 1) * LANES)
            part = r.low[i, :, columns]
            total = None
            for h in (2 * pair, 2 * pair + 1):
                decay = jnp.exp(log_decay[:, h : h + 1] - log_rows[h : h + 1] + closed)
                own = jnp.where(left if h % 2 == 0 else ~left, part, jnp.zeros_like(part))
                term = dot((scores * decay).astype(BF16), own)
                total = term if total is None else total + term
            r.full[i, :, columns] = total
        prefix.events(i + count)

        @pl.when(i == 0)
        def _():
            second_gather.first_arrived(-3, 3)

    second_gather.finish()
    store("w2", 0).start()
    for i in range(count):
        swap_grads(i).wait()

    @pl.loop(0, count)
    def _(i):
        r.gate[i] = dot(r.normed_s[i, HALO:], r.w2_full[:, :inner])
        r.gn[i] = dot(either(c, r.g[i], r.g_in[i]), r.w2_full[:, inner:])

    @pl.loop(0, count)
    def _(i):
        prefix.arrived(i)
        values = r.act[i, :, :inner].astype(F32)
        entry = expand(r.aux[i, :, entry_at], spread)
        scanned = r.full[i] + dot(r.act[i, :, inner + nstate :], r.hin[i], NT) * entry
        r.full[i] = scanned
        mixed = scanned + r.prm[SKIP : SKIP + 1, :inner] * values
        gate = r.gate[i]
        gated = mixed * (gate * sigmoid(gate))
        squares = jnp.sum(gated * gated, axis=-1, keepdims=True)
        cross = jnp.sum(
            r.gn[i] * r.prm[INNER_GAIN : INNER_GAIN + 1, :inner] * gated, axis=-1, keepdims=True
        )
        lane = lax.broadcasted_iota(jnp.int32, (length, LANES), 1)
        r.sums[i] = jnp.where(lane == 0, squares, jnp.where(lane == 1, cross, 0.0))
        swap_sums(i).start()

    prefix.finish()

    @pl.loop(0, count)
    def _(i):
        swap_sums(i).wait_recv()
        values = r.act[i, :, :inner].astype(F32)
        mixed = r.full[i] + r.prm[SKIP : SKIP + 1, :inner] * values
        gate = r.gate[i]
        sig = sigmoid(gate)
        swish = gate * sig
        gated = mixed * swish
        both = r.sums[i] + r.sums_in[i]
        inner_scale = lax.rsqrt(both[:, 0:1] / total_inner + EPSILON)
        gain = r.prm[INNER_GAIN : INNER_GAIN + 1, :inner]
        unit = gated * inner_scale
        r.normal[i] = (unit * gain).astype(BF16)
        grad_norm = r.gn[i]
        grad_inner = jnp.sum(grad_norm * unit, axis=0, keepdims=True)
        grad_gated = inner_scale * (grad_norm * gain) - unit * (
            inner_scale * inner_scale * (both[:, 1:2] / total_inner)
        )
        dy = grad_gated * swish
        r.dy[i] = dy.astype(BF16)
        r.ggate_s[i] = (
            grad_gated * mixed * (sig * (1.0 + gate * (1.0 - sig)))
        ).astype(BF16)
        entry = expand(r.aux[i, :, entry_at], spread)
        r.prior[i] = dot(
            (dy * entry).astype(BF16), r.act[i, :, inner + nstate :], TN
        ).astype(BF16)
        suffix.events(i)
        r.small[1:2, :inner] += grad_inner
        per_head = head_sums(
            jnp.broadcast_to(jnp.sum(dy * values, axis=0, keepdims=True), (8, inner)), spread
        )
        r.small[2:3, :LANES] += per_head[:1]
        store("ggate", i).start()

    @pl.loop(0, count)
    def _(i):
        r.ginputs[...] = dot(r.normal[i], r.w2_full[:, inner:], NT)
        r.gate[i, :, :half] = r.ginputs[:, side]
        r.osend[i] = r.ginputs[:, other_side].astype(BF16)
        swap_out(i).start()
        store("keep", i).start()
        suffix.events(i + count)

    def weights_gradient(source, target, values, rows):
        for n in range(inner // 256):
            at = slice(n * 256, (n + 1) * 256)
            total = None
            for i in range(count):
                term = dot(source(i), values[i, :, at], TN)
                total = term if total is None else total + term
            target[rows, at] = total.astype(BF16)

    weights_gradient(lambda i: r.g[i], r.dout, r.normal, side)
    weights_gradient(lambda i: r.g_in[i], r.dout, r.normal, other_side)
    reduce_.begin(0)
    weights_gradient(lambda i: r.normed_s[i, HALO:], r.dgate, r.ggate_s, slice(None))
    reduce_.begin(1)

    @pl.loop(0, count)
    def _(i):
        suffix.arrived(i)
        log_decay = r.aux[i, :, log_at]
        step = r.aux[i, :, step_at]
        entry = r.aux[i, :, entry_at]
        values = r.act[i, :, :inner].astype(F32)
        in_state = r.act[i, :, inner : inner + nstate]
        out_state = r.act[i, :, inner + nstate :]
        later = r.later[i]
        wide_dy = r.dy[i].astype(F32)
        step_wide = expand(step, spread)
        tail_wide = expand(r.aux[i, :, tail_at], spread)
        entry_wide = expand(entry, spread)
        upper, ones_upper = triangle(length, True)
        doc_col, doc_row = doc_numbers(r.doc[i], ones)
        closed = jnp.where(upper & (doc_col == doc_row), 0.0, MASKED)
        scores = dot(in_state, out_state, NT)
        log_rows = log_decay.T
        r.ginputs[...] = tail_wide * dot(in_state, later, NT)
        for pair in range(inner // LANES):
            columns = slice(pair * LANES, (pair + 1) * LANES)
            pair_dy = r.dy[i, :, columns]
            pair_in = r.low[i, :, columns]
            total = r.ginputs[:, columns]
            for h in (2 * pair, 2 * pair + 1):
                chosen = left if h % 2 == 0 else ~left
                own_dy = jnp.where(chosen, pair_dy, jnp.zeros_like(pair_dy))
                decay = jnp.exp(log_rows[h : h + 1] - log_decay[:, h : h + 1] + closed)
                total = total + dot((scores * decay).astype(BF16), own_dy)
                grad_decay = dot(pair_in, own_dy, NT) * decay
                if h == 0:
                    r.dcb[...] = grad_decay
                else:
                    r.dcb[...] += grad_decay
            r.ginputs[:, columns] = total
        grad_inputs = r.ginputs[...]
        grad_scores = r.dcb[...]
        inputs = values * step_wide
        grad_in = dot(grad_scores.astype(BF16), out_state) + dot(
            (inputs * tail_wide).astype(BF16), later
        )
        grad_out = dot(grad_scores.T.astype(BF16), in_state) + dot(
            (wide_dy * entry_wide).astype(BF16), r.hin[i]
        )
        is_first = c == 0
        r.gate[i, :, own_at] = jnp.where(is_first, grad_in, grad_out)
        r.bsend[i] = jnp.where(is_first, grad_out, grad_in).astype(BF16)
        swap_states(i).start()
        entry_last = jnp.broadcast_to(entry[length - 1 :], (8, LANES))
        later_wide = later.astype(F32)
        lane_ones = jnp.ones((8, nstate), BF16)

        def state_sums(other):
            pieces = split2(later_wide * other.astype(F32))
            return head_sums(sum(dot(lane_ones, piece, NT) for piece in pieces), spread)

        ending = (state_sums(r.state[i]) + entry_last * state_sums(r.hin[i]))[:1]
        grad_log = head_sums(wide_dy * r.full[i], spread) - head_sums(
            r.low[i].astype(F32) * grad_inputs, spread
        )
        grad_rate_step = running_sum(ones_upper, grad_log) + ending
        rate = r.prm[RATE : RATE + 1, :LANES]
        grad_step = head_sums(values * grad_inputs, spread) + rate * grad_rate_step
        lane = lax.broadcasted_iota(jnp.int32, (length, LANES), 1)
        gpre = jnp.where(lane < heads, grad_step * sigmoid(r.aux[i, :, pre_at]), 0.0)
        r.gate[i, :, gpre_at] = gpre
        store("gpre", i).start()
        grad_values = step_wide * grad_inputs + r.prm[SKIP : SKIP + 1, :inner] * wide_dy
        r.ext[...] = r.xs_s[i].astype(F32)
        px = conv(slice(0, inner))
        sig = sigmoid(px)
        gcx = grad_values * (sig * (1.0 + px * (1.0 - sig)))
        r.gn[i] = gcx
        store("gcx", i).start()
        r.edge[i, :, :inner] = gcx[:EDGE]
        ps = conv(mine)
        sig = sigmoid(ps)
        r.gate[i, :, slope_at] = sig * (1.0 + ps * (1.0 - sig))
        r.small[3:4, :LANES] += jnp.sum(gpre, axis=0, keepdims=True)
        r.small[4:5, :LANES] += rate * jnp.sum(step * grad_rate_step, axis=0, keepdims=True)

        def finish_states(n):
            swap_states(n).wait_recv()
            gst = (r.gate[n, :, own_at] + r.brecv[n].astype(F32)) * r.gate[n, :, slope_at]
            r.gate[n, :, own_at] = gst
            store("gst", n).start()
            r.edge[n, :, inner:] = gst[:EDGE]
            pl.when(prv)(send_edge(n).start)

        pl.when(i > 0)(lambda: finish_states(i - 1))

        @pl.when(i == 0)
        def _():
            reduce_.second(3, -3, 2, -2)

        @pl.when(i == 1)
        def _():
            reduce_.second(1, -1, 0)
            reduce_.third(3, -3)

        @pl.when(i == 2)
        def _():
            reduce_.third(2, -2)

        @pl.when(i == count - 1)
        def _():
            finish_states(i)
            reduce_.third(1, -1)

    reduce_.third(0)
    reduce_.finish()
    suffix.finish()

    @pl.loop(0, count)
    def _(i):
        swap_sums(i).wait_send()
        swap_out(i).wait()
        swap_states(i).wait_send()
        pl.when(prv)(send_edge(i).wait_send)
        pl.when(nxt)(send_edge(i).wait_recv)
        for name in stores:
            if name not in SINGLE:
                store(name, i).wait()

    for name in SINGLE:
        store(name, 0).wait()


SINGLE = tuple(dict(w=0, w2=0))
SECOND_REFS = tuple("s" + n for n in GATHER_REFS)
SHARED_REFS = tuple(dict(total=0, through=0, leaving=0, staged=0))
SUFFIX_REFS = tuple(n if n in SHARED_REFS else "s" + n for n in SCAN_REFS)


def main_call(sizes, total_inner, tok, g, doc, prm, w1, w2):
    length, inner, nstate, size, taps = sizes
    count, _, half = tok.shape
    model = 2 * half
    channels = inner + 2 * nstate
    rows = w1.shape[0]
    ins = dict(
        tok=(tok, INSIDE), g=(g, INSIDE), doc=(doc, INSIDE), prm=(prm, INSIDE),
        w1=(w1, ANYWHERE), w2=(w2, ANYWHERE),
    )
    outs = dict(
        normed=(shape((count, length, model), BF16), ANYWHERE),
        xs=(shape((count, HALO + length, channels), BF16), ANYWHERE),
        ggate=(shape((count, length, inner), BF16), ANYWHERE),
        keep=(shape((count, length, half), F32), ANYWHERE),
        gpre=(shape((count, length, LANES), F32), ANYWHERE),
        gcx=(shape((count, length, inner), F32), ANYWHERE),
        gst=(shape((count, length, nstate), F32), ANYWHERE),
        out_in=(shape((count, length, half), BF16), ANYWHERE),
        edge_in=(shape((count, EDGE, inner + nstate), F32), ANYWHERE),
        w_out=(shape((model, w1.shape[1]), BF16), ANYWHERE),
        w2_out=(shape((model, inner), BF16), ANYWHERE),
        tok_in=(shape(tok.shape, BF16), INSIDE),
        small=(shape((8, channels), F32), INSIDE),
        g_out=(shape((rows, inner), F32), INSIDE),
        g_gate=(shape((rows, inner), F32), INSIDE),
    )

    def vmem(*dims, dtype=F32):
        return pltpu.VMEM(dims, dtype)

    def low(*dims):
        return pltpu.VMEM(dims, BF16)

    scratch = dict(
        g_in=low(count, length, half),
        halo=low(count, HALO, model),
        w=low(model, w1.shape[1]),
        w2_full=low(model, 2 * inner),
        normed_s=low(count, HALO + length, model),
        xs_s=low(count, HALO + length, channels),
        act=low(count, length, channels),
        aux=vmem(count, length, 5 * LANES),
        low=low(count, length, inner),
        dec=vmem(count, HEAD_ROWS, LANES),
        state=low(count, inner, nstate),
        hin=low(count, inner, nstate),
        prior=low(count, inner, nstate),
        later=low(count, inner, nstate),
        full=vmem(count, length, inner),
        gate=vmem(count, length, inner),
        gn=vmem(count, length, inner),
        sums=vmem(count, length, LANES),
        sums_in=vmem(count, length, LANES),
        normal=low(count, length, inner),
        dy=low(count, length, inner),
        ggate_s=low(count, length, inner),
        osend=low(count, length, half),
        dout=low(model, inner),
        dgate=low(model, inner),
        ext=vmem(HALO + length, channels),
        ginputs=vmem(length, inner),
        dcb=vmem(length, length),
        bsend=low(count, length, nstate),
        brecv=low(count, length, nstate),
        edge=vmem(count, EDGE, inner + nstate),
        ss=dma(6, count),
        rs=dma(6, count),
        hs=dma(2),
        hr=dma(2),
        store=dma(9, count),
    )
    scan = Scan.scratch(count, inner, nstate, HEAD_ROWS)
    gather = Gather.semaphores(2)
    scratch.update(zip(SUFFIX_REFS, scan.values()))
    scratch.update(scan)
    scratch.update(gather)
    scratch.update(zip(SECOND_REFS, gather.values()))
    scratch.update(Reduce.scratch(2, rows, 2 * inner))
    return fused_call(
        functools.partial(main_body, sizes, total_inner), None, ins, outs, scratch, 1, "main"
    )


def back_body(sizes, r):
    length, inner, nstate, size, taps = sizes
    k = pl.program_id(0)
    s, c, z, y, x = place()
    to_core = (s, 1 - c)
    wide = inner + nstate + LANES
    reduce_ = Reduce(
        (
            (r.dx, 0, wide // 2, True, r.g_x, 0, 0),
            (r.dx, wide // 2, wide // 2, False, r.g_x, wide // 2, wide // 2),
        ),
        r.g_x.shape[0],
        picked(r, REDUCE_REFS),
    )
    lines = [(z != j, (s + (j - z) * PLANE, c)) for j in range(LINE)]

    def swap_part(i):
        return remote(r.part.at[i], r.part_in.at[i], r.ps.at[i], r.pr.at[i], to_core)

    def small_copy(src, dst, at, device):
        return remote(src, dst, r.qs.at[at], r.qr.at[at], device)

    core_copy = small_copy(r.bc, r.bc_in, 0, to_core)
    x_copy = small_copy(r.work.at[0], r.from_x, 1, reduce_.to_x)
    y_copy = small_copy(r.work.at[1], r.from_y, 2, reduce_.to_y)
    states_copy = small_copy(r.states_s.at[c], r.states_s.at[c], 7, to_core)

    def z_small(j, slot):
        return remote(
            r.work.at[2], r.from_z.at[slot], r.qs.at[3 + j], r.qr.at[3 + slot],
            (s + (j - z) * PLANE, c),
        )

    @pl.when(k == 0)
    def _():
        greet([(True, reduce_.to_x), (True, reduce_.to_y), (True, to_core)] + lines)

    @pl.when(k < 4)
    def _():
        last = s == lax.axis_size("seq") - 1
        mine = pl.ds(pl.multiple_of(inner + c * nstate, LANES), nstate)
        r.gext[:length, :inner] = r.gcx[0]
        r.gext[:length, inner:] = r.gst[0]
        r.gext[length:] = jnp.where(last, 0.0, r.edge_in[0])
        r.ext[:, :inner] = r.xs[0, :, :inner].astype(F32)
        r.ext[:, inner:] = r.xs[0, :, mine].astype(F32)
        grad_conv = r.gext[:length]
        grad_in = None
        rows = []
        for t in range(taps):
            row = jnp.concatenate(
                [r.prm[TAPS + t : TAPS + t + 1, :inner], r.prm[TAPS + t : TAPS + t + 1, mine]],
                axis=1,
            )
            term = row * r.gext[taps - 1 - t : taps - 1 - t + length]
            grad_in = term if grad_in is None else grad_in + term
            start = HALO - taps + 1 + t
            rows.append(
                jnp.sum(r.ext[start : start + length] * grad_conv, axis=0, keepdims=True)
            )
        rows.append(jnp.sum(grad_conv, axis=0, keepdims=True))
        rows.append(jnp.zeros((8 - taps - 1, inner + nstate), F32))
        rows = jnp.concatenate(rows, axis=0)
        low = grad_in.astype(BF16)
        low_pre = r.gpre[0].astype(BF16)
        part = dot(r.ggate[0], r.w2[:, :inner], NT)
        part = part + dot(low[:, :inner], r.w[:, :inner], NT)
        part = part + dot(low[:, inner:], r.w[:, mine], NT)
        part = part + dot(low_pre, r.w[:, inner + 2 * nstate :], NT)
        r.part[k] = part.astype(BF16)
        swap_part(k).start()
        stacked = jnp.concatenate([low, low_pre], axis=1)
        term = dot(r.normed[0], stacked, TN)

        @pl.when(k == 0)
        def _():
            r.conv_rows[...] = rows
            r.acc[...] = term

        @pl.when(k > 0)
        def _():
            r.conv_rows[...] += rows
            r.acc[...] += term

    @pl.when(k == 3)
    def _():
        r.dx[...] = r.acc[...].astype(BF16)
        reduce_.begin()
        own = r.conv_rows[:, inner:]
        r.bc[:, :nstate] = jnp.where(c == 0, own, 0.0)
        r.bc[:, nstate:] = jnp.where(c == 1, own, 0.0)
        core_copy.start()

    @pl.when(k >= 4)
    def _():
        i = k - 4
        swap_part(i).wait_recv()
        own_tok = r.tok[0].astype(F32)
        tok = either(c, own_tok, r.tok_in[0].astype(F32))
        model = tok.shape[1]
        scale = lax.rsqrt(jnp.mean(tok * tok, axis=-1, keepdims=True) + EPSILON)
        unit = tok * scale
        grad_normed = r.part[i].astype(F32) + r.part_in[i].astype(F32)
        grad = grad_normed * r.prm[GAIN : GAIN + 1, :model]
        r.wide[...] = scale * (grad - unit * jnp.mean(grad * unit, axis=-1, keepdims=True))
        half = model // 2
        r.tokens_grad[0] = (
            r.g[0].astype(F32) + r.wide[:, pl.ds(pl.multiple_of(c * half, LANES), half)]
        )
        r.mixed[0] = (own_tok + (r.keep[0] + r.out_in[0].astype(F32))).astype(BF16)
        gain = jnp.sum(grad_normed * unit, axis=0, keepdims=True)

        @pl.when(i == 0)
        def _():
            r.gain_row[...] = gain

        @pl.when(i > 0)
        def _():
            r.gain_row[...] += gain

    @pl.when(k == 4)
    def _():
        reduce_.second(3, -3, 2, -2)

    @pl.when(k == 5)
    def _():
        reduce_.second(1, -1, 0)
        reduce_.third(3, -3)

    @pl.when(k == 6)
    def _():
        reduce_.third(2, -2)

    @pl.when(k == 7)
    def _():
        core_copy.wait_recv()
        r.work[0] = jnp.zeros(r.work.shape[1:], F32)
        r.work[0, 0:8] = r.small[...]
        r.work[0, 0:1, :inner] = r.gain_row[...]
        r.work[0, 8:16, :inner] = r.conv_rows[:, :inner]
        r.work[0, 16:24, : 2 * nstate] = r.bc[...] + r.bc_in[...]
        x_copy.start()
        reduce_.third(1, -1)
        x_copy.wait_recv()
        r.work[1] = r.work[0] + r.from_x[...]
        y_copy.start()
        reduce_.third(0, only=(1,))
        r.states_s[c] = r.g_x[:, inner : inner + nstate]
        states_copy.start()
        y_copy.wait_recv()
        r.work[2] = r.work[1] + r.from_y[...]
        for j in range(LINE):
            pl.when(z != j)(z_small(j, z).start)
        r.from_z[z] = r.work[2]
        reduce_.third(0, only=(0,))
        for j in range(LINE):
            pl.when(z != j)(z_small(j, j).wait_recv)
        r.sums[...] = (r.from_z[0] + r.from_z[1]) + (r.from_z[2] + r.from_z[3])
        states_copy.wait()
        r.states[...] = r.states_s[...]
        core_copy.wait_send()
        x_copy.wait_send()
        y_copy.wait_send()
        for j in range(LINE):
            pl.when(z != j)(z_small(j, z).wait_send)
        reduce_.finish()

        @pl.loop(0, 4)
        def _(i):
            swap_part(i).wait_send()


def back_call(sizes, m, tok, g, prm):
    length, inner, nstate, size, taps = sizes
    count, _, half = g.shape
    model = 2 * half
    channels = inner + 2 * nstate
    rows = model // lax.axis_size("seq")
    wide = inner + nstate + LANES
    first, second = during(0), during(4)
    ins = dict(
        gcx=(m.gcx, stepped(m.gcx, first)),
        gst=(m.gst, stepped(m.gst, first)),
        gpre=(m.gpre, stepped(m.gpre, first)),
        ggate=(m.ggate, stepped(m.ggate, first)),
        edge_in=(m.edge_in, stepped(m.edge_in, first)),
        xs=(m.xs, stepped(m.xs, first)),
        normed=(m.normed, stepped(m.normed, first)),
        tok=(tok, stepped(tok, second)),
        tok_in=(m.tok_in, stepped(m.tok_in, second)),
        g=(g, stepped(g, second)),
        keep=(m.keep, stepped(m.keep, second)),
        out_in=(m.out_in, stepped(m.out_in, second)),
        small=(m.small, whole(m.small)),
        prm=(prm, whole(prm)),
        w=(m.w_out, whole(m.w_out)),
        w2=(m.w2_out, whole(m.w2_out)),
    )
    grads = shape((count, length, half), F32)
    mixed = shape((count, length, half), BF16)
    g_x = shape((rows, wide), F32)
    states = shape((2, rows, nstate), F32)
    sums = shape((24, channels), F32)
    outs = dict(
        tokens_grad=(grads, stepped(grads, second)),
        mixed=(mixed, stepped(mixed, second)),
        g_x=(g_x, whole(g_x)),
        sums=(sums, whole(sums)),
        states=(states, whole(states)),
    )
    scratch = dict(
        part=pltpu.VMEM((count, length, model), BF16),
        part_in=pltpu.VMEM((count, length, model), BF16),
        acc=pltpu.VMEM((model, wide), F32),
        dx=pltpu.VMEM((model, wide), BF16),
        conv_rows=pltpu.VMEM((8, inner + nstate), F32),
        gain_row=pltpu.VMEM((1, model), F32),
        ext=pltpu.VMEM((HALO + length, inner + nstate), F32),
        gext=pltpu.VMEM((length + EDGE, inner + nstate), F32),
        wide=pltpu.VMEM((length, model), F32),
        states_s=pltpu.VMEM((2, rows, nstate), F32),
        bc=pltpu.VMEM((8, 2 * nstate), F32),
        bc_in=pltpu.VMEM((8, 2 * nstate), F32),
        work=pltpu.VMEM((3, 24, channels), F32),
        from_x=pltpu.VMEM((24, channels), F32),
        from_y=pltpu.VMEM((24, channels), F32),
        from_z=pltpu.VMEM((LINE, 24, channels), F32),
        ps=dma(count), pr=dma(count), qs=dma(8), qr=dma(8),
    )
    scratch.update(Reduce.scratch(2, rows, wide))
    return fused_call(functools.partial(back_body, sizes), 8, ins, outs, scratch, 4, "back")


def fused_layer(sizes, total_inner, heads, tok, g, doc, prm, w, w2):
    length, inner, nstate, size, taps = sizes
    model = 2 * tok.shape[2]
    m = main_call(sizes, total_inner, tok, g, doc, prm, w, w2)
    b = back_call(sizes, m, tok, g, prm)
    sums = b.sums
    return (
        b.mixed,
        b.tokens_grad,
        sums[0, :model],
        jnp.stack([m.g_gate, b.g_x[:, :inner]], axis=1),
        jnp.concatenate([b.states[0], b.states[1]], axis=1),
        b.g_x[:, inner + nstate : inner + nstate + heads],
        sums[8 : 8 + taps, :inner],
        sums[8 + taps, :inner],
        sums[16 : 16 + taps, : 2 * nstate],
        sums[16 + taps, : 2 * nstate],
        sums[3, :heads],
        sums[4, :heads],
        sums[2, :heads],
        sums[1, :inner],
        m.g_out.T,
    )


def shards(
    tokens, doc_starts, norm_gain, input_gate_features, input_state_weight, input_step_weight,
    conv_taps_x, conv_bias_x, conv_taps_bc, conv_bias_bc, step_bias, decay_log, skip_gain,
    inner_gain, output_projection, out_grad,
):
    micro, seqs, length, half = tokens.shape
    count = micro * seqs
    model = 2 * half
    heads = step_bias.shape[0]
    inner = inner_gain.shape[0]
    size = inner // heads
    nstate = conv_taps_bc.shape[1] // 2
    taps = conv_taps_x.shape[0]
    channels = inner + 2 * nstate
    rows = input_gate_features.shape[0]
    total_inner = inner * lax.axis_size("head")
    sizes = (length, inner, nstate, size, taps)
    core = lax.axis_index("head")

    tok = tokens.reshape(count, length, half)
    g = out_grad.reshape(count, length, half)
    doc = jnp.broadcast_to(
        doc_starts.reshape(count, 1, length).astype(F32), (count, 8, length)
    )

    def row(v):
        return jnp.pad(v, (0, channels - v.shape[0]))[None]

    prm = jnp.concatenate(
        [
            row(norm_gain),
            row(inner_gain),
            row(jnp.repeat(skip_gain, size)),
            row(jnp.concatenate([conv_bias_x, conv_bias_bc])),
            row(step_bias),
            row(-jnp.exp(decay_log)),
            jnp.concatenate([conv_taps_x, conv_taps_bc], axis=1),
        ],
        axis=0,
    )
    prm = jnp.pad(prm, ((0, 16 - prm.shape[0]), (0, 0)))
    w_own = jnp.concatenate(
        [
            input_gate_features.reshape(rows, 2 * inner),
            input_state_weight,
            jnp.pad(input_step_weight, ((0, 0), (0, LANES - heads))),
        ],
        axis=1,
    )
    w_out_own = output_projection.T

    if lax.axis_size("seq") == PLANE * LINE and lax.axis_size("head") == 2:
        outputs = fused_layer(
            sizes, total_inner, heads, tok, g, doc, prm, w_own[:, inner:],
            jnp.concatenate([w_own[:, :inner], w_out_own], axis=1),
        )
        return tuple(
            o.reshape(tokens.shape) if n < 2 else o for n, o in enumerate(outputs)
        )

    w_in, w_out, tok_full, g_full, halo = plain_gather(
        w_own, w_out_own, tok, g, tok[:, length - HALO :]
    )
    grid = (count,)
    outs = [
        shape((count, length, model), BF16),
        shape((count, length, inner), F32),
        shape((count, HALO + length, channels), BF16),
        shape((count, length, channels), F32),
        shape((count, length, channels), BF16),
        shape((count, length, inner), F32),
        shape((count, inner, nstate), BF16),
        shape((count, length, 5 * LANES), F32),
        shape((count, HEAD_ROWS, LANES), F32),
    ]
    normed, gate, xs, pre, act, scan, state, aux, dec = call(
        functools.partial(forward_kernel, sizes),
        grid,
        [per_seq(tok_full), per_seq(halo), per_seq(doc), whole(prm), whole(w_in)],
        [per_seq(o) for o in outs],
        outs,
        [pltpu.VMEM((HALO + length, channels), F32)],
        name="forward",
    )(tok_full, halo, doc, prm, w_in)

    hin = plain_scan(state, dec, size, False)

    outs = [
        shape((count, length, inner), F32),
        shape((count, length, inner), F32),
        shape((count, length, LANES), F32),
    ]
    ins = (scan, act, aux, gate, hin, g_full)
    full, grad_norm, sums = call(
        functools.partial(gate_kernel, sizes),
        grid,
        [per_seq(a) for a in ins] + [whole(prm), whole(w_out)],
        [per_seq(o) for o in outs],
        outs,
        name="gate",
    )(*ins, prm, w_out)

    sums_in = swap_heads(sums)

    outs = [
        shape((count, length, half), F32),
        shape((count, length, half), BF16),
        shape((count, length, inner), BF16),
        shape((count, length, inner), BF16),
        shape((count, inner, nstate), BF16),
        shape((8, inner), F32),
        shape((model, inner), BF16),
        shape((model, inner), BF16),
    ]
    ins = (full, act, aux, gate, grad_norm, sums, sums_in, g_full, normed)
    keep, send, dy, ggate, prior, small_out, dout, dgate = call(
        functools.partial(output_kernel, sizes, total_inner),
        grid,
        [per_seq(a) for a in ins] + [whole(prm), whole(w_out)],
        [per_seq(o) for o in outs[:5]] + [whole(o) for o in outs[5:]],
        outs,
        [
            pltpu.VMEM((model, inner), F32),
            pltpu.VMEM((model, inner), F32),
            pltpu.VMEM((length, model), F32),
        ],
        name="output",
    )(*ins, prm, w_out)

    mixed = (tok.astype(F32) + (keep + swap_heads(send).astype(F32))).astype(BF16)
    later = plain_scan(prior, dec, size, True)

    outs = [
        shape((count, length, inner), F32),
        shape((count, length, nstate), F32),
        shape((count, length, nstate), BF16),
        shape((count, length, LANES), F32),
        shape((8, LANES), F32),
        shape((count, EDGE, inner), F32),
        shape((count, EDGE, nstate), F32),
    ]
    ins = (full, act, aux, dy, hin, later, state, doc, pre)
    gcx, own, other, gpre, small_scan, edge, slope = call(
        functools.partial(backward_kernel, sizes),
        grid,
        [per_seq(a) for a in ins] + [whole(prm)],
        [per_seq(o) if len(o.shape) == 3 else whole(o) for o in outs],
        outs,
        [pltpu.VMEM((length, length), F32)],
        name="backward",
    )(*ins, prm)

    recv, edge_in, edge_state = plain_states(other, own, slope, edge)

    outs = [
        shape((count, length, model), BF16),
        shape((model, inner + nstate + LANES), BF16),
        shape((8, inner + nstate), F32),
    ]
    ins = (gcx, own, recv, edge_in, edge_state, pre, xs, gpre, ggate, normed)
    part, dx, small_conv = call(
        functools.partial(conv_kernel, sizes),
        grid,
        [per_seq(a) for a in ins] + [whole(prm), whole(w_in)],
        [per_seq(outs[0]), whole(outs[1]), whole(outs[2])],
        outs,
        [
            pltpu.VMEM((model, inner + nstate + LANES), F32),
            pltpu.VMEM((HALO + length, inner + nstate), F32),
            pltpu.VMEM((length + EDGE, inner + nstate), F32),
        ],
        name="conv",
    )(*ins, prm, w_in)

    part_in = swap_heads(part)

    outs = [shape((count, length, half), F32), shape((8, model), F32)]
    ins = (tok_full, part, part_in, g)
    tokens_grad, small_norm = call(
        functools.partial(tokens_kernel, sizes),
        grid,
        [per_seq(a) for a in ins] + [whole(prm)],
        [per_seq(outs[0]), whole(outs[1])],
        outs,
        [pltpu.VMEM((length, model), F32)],
        name="tokens",
    )(*ins, prm)

    small = jnp.concatenate(
        [
            row(small_norm[0]),
            row(small_out[0]),
            row(small_out[1]),
            row(jnp.concatenate([small_scan[0], small_scan[1]])),
            jnp.pad(small_conv[: taps + 1, :inner], ((0, 0), (0, channels - inner))),
            jnp.zeros((16 - 5 - taps, channels), F32),
        ],
        axis=0,
    )
    own_states = small_conv[:, inner:]
    shared = jnp.concatenate(
        [jnp.where(core == 0, own_states, 0.0), jnp.where(core == 1, own_states, 0.0)], axis=1
    )
    (g_out, g_gate, g_x), small, shared = plain_sum((dout, dgate, dx), small, shared)
    g_states = plain_both(g_x[:, inner : inner + nstate])
    return (
        mixed.reshape(tokens.shape),
        tokens_grad.reshape(tokens.shape),
        small[0, :model],
        jnp.stack([g_gate, g_x[:, :inner]], axis=1),
        g_states,
        g_x[:, inner + nstate : inner + nstate + heads],
        small[4 : 4 + taps, :inner],
        small[4 + taps, :inner],
        shared[:taps],
        shared[taps],
        small[3, :heads],
        small[3, LANES : LANES + heads],
        small[2, :inner].reshape(heads, size).sum(axis=1),
        small[1, :inner],
        g_out.T,
    )


def solution(mesh):
    placed = (
        P(None, None, "seq", "head"),
        P(None, None, "seq"),
        P(),
        P("seq", None, "head"),
        P("seq", None),
        P("seq", "head"),
        P(None, "head"),
        P("head"),
        P(),
        P(),
        P("head"),
        P("head"),
        P("head"),
        P("head"),
        P("head", "seq"),
        P(None, None, "seq", "head"),
    )
    return jax.shard_map(
        shards,
        mesh=mesh,
        in_specs=placed,
        out_specs=(
            P(None, None, "seq", "head"),
            P(None, None, "seq", "head"),
            P(),
            P("seq", None, "head"),
            P("seq", None),
            P("seq", "head"),
            P(None, "head"),
            P("head"),
            P(),
            P(),
            P("head"),
            P("head"),
            P("head"),
            P("head"),
            P("head", "seq"),
        ),
        check_vma=False,
    )
```

time: 1530 us -> 215 us (0.14)
  waiting for transfers between devices: 598 us -> 0 us
  blocking collectives: 372 us -> 0 us
  Pallas kernels: 0 us -> 188 us
  other arithmetic: 191 us -> 6.39 us
  matrix products: 176 us -> 0 us
  local copies, waits for them, and re-layouts: 143 us -> 18.8 us
  between operations: 16.6 us -> 0.73 us
    reduce_scatter x3 -> x0, waiting for transfers between devices: 311 us -> none  [the longest x1 130 us: shards(): lax.psum_scatter(total_out, 'seq', scatter_dimension=1, tiled=True)]
    all_gather x10 -> x0, blocking collectives: 288 us -> none  [the longest x2 119 us: entering(): lax.all_gather(part.astype(kind), axis)]
    all_gather x6 -> x0, waiting for transfers between devices: 209 us -> none  [the longest x2 159 us: carried_in(): gathered = jax.tree.map(lambda a: lax.all_gather(a, axis), part)]
    pallas_call x0 -> x2, Pallas kernels: none -> 188 us  [fused_call(): pl.pallas_call(kernel, grid=(steps,) if steps else (), in_specs=[spec for...]
    dot_general x56 -> x0, matrix products: 176 us -> none  [the longest x6 50.3 us: block_step(): jnp.einsum('sijh,sjhp->sihp', mixing, values, precision=EXACT_MATMUL)]
    psum x3 -> x0, blocking collectives: 83.1 us -> none  [the longest x1 78.2 us: shards(): lax.psum((total_gain, total_taps, total_bias, total_step_bias, total_deca...]
    unnamed x17 -> x0, waiting for transfers between devices: 56.5 us -> none
    select_n x32 -> x0, other arithmetic: 56 us -> none  [lap(): return jax.tree.map(lambda a, b: jnp.where(reached, a, b), new, before)]
  transfers between devices with their start and end apart: 18 -> 0, of which waited for: 11 -> 0; matrix products, arithmetic and copies ran while one was open for 22% -> 0% of each run, Pallas kernels for 0% -> 0%
where the time goes in v1:
time: 215 us; the launch traced here: 214 us
  Pallas kernels  188 us (87%)
  local copies, waits for them, and re-layouts  18.8 us (9%)
  other arithmetic  6.39 us (3%)
    pallas_call x2, Pallas kernels, fused_call(): pl.pallas_call(kernel, grid=(steps,) if steps else (), in_specs=[spec for...  188 us
    unnamed x17, local copies, waits for them, and re-layouts  6.03 us

profile of v1, /device:TPU:0, one launch (start us, length us, event | category | flops | bytes accessed | tf_op | source)
XLA Modules:
  0.0 214.2 jit_solution(452117314432925476)
XLA Ops:
  0.6 0.7 exponential_negate_fusion
  1.3 0.7 convert_element_type.22
  2.0 0.7 pad.25
  2.7 0.7 pad_maximum_fusion.5
  3.4 0.7 pad.28
  4.1 0.7 pad.26
  4.8 0.7 broadcast_in_dim.29
  5.5 0.1 reshape.59
  5.6 0.8 copy.31
  6.4 0.7 pad_maximum_fusion.4
  7.1 0.2 concatenate.20
  7.3 0.6 pad.30.refs_3_.refs_13_
  7.9 0.6 broadcast_in_dim.26.refs_2_
  8.5 0.9 copy.34
  9.5 1.4 fusion.1.refs_4_
  10.9 1.6 pad_maximum_fusion.1.refs_5_
  12.4 138.4 %main.1 = (bf16[4,256,768]{2,1,0:T(8,128)(2,1)}, bf16[4,272,1024]{2,1,0:T(8,128)(2,1)}, bf16[4,256,768]{2,1,0:T(8,128)(2,1)}, f32[4,256,384]{2,1,0:T(8,128)}, f3...) custom-call(bf16[4,256,384]{2,1,0:T(8,128)(2,1)} %bitcast.28, ...), custom_call_target="tpu_custom_call" | custom-call | tf_op jit(solution)/shard_map/main/pallas_call | solution.py:572
  150.8 0.0 copy-start.3
  150.8 49.9 %back.1 = (f32[4,256,384]{2,1,0:T(8,128)}, bf16[4,256,384]{2,1,0:T(8,128)(2,1)}, f32[48,1024]{1,0:T(8,128)}, f32[24,1024]{1,0:T(8,128)}, f32[2,48,128]{2,1,0:T(8,128)}) custom-call(f32[4,256,768]{2,1,0:T(8,128)} %get-tuple-element.35.refs_0_, f32[4,256,128]{2,1,0:T(8,128)} %get-tuple-element.36.refs_1_, f32[4,256,128]{2,1,0:T(8,128)} %get-tuple-element.37.refs_2_, ...), custom_call_target="tpu_custom_call" | custom-call | tf_op jit(solution)/shard_map/back/pallas_call | solution.py:572
  200.7 0.0 copy-start.4
  200.7 0.0 copy-start.1
  200.7 1.3 slice.55
  202.0 1.3 slice_bitcast_fusion.3
  203.4 1.3 slice.54
  204.6 1.3 slice.52
  206.0 1.4 slice_reduce_fusion
  207.4 0.7 slice.51
  208.2 0.0 copy-start
  208.2 1.0 slice_bitcast_fusion
  209.2 0.7 copy.33
  209.9 0.0 copy-done.3
  209.9 0.9 copy.32
  210.9 0.0 copy-done.4
  210.9 0.6 pad_maximum_fusion.3
  211.5 0.0 copy-done.1
  211.5 0.9 copy.38
  212.4 0.0 copy-done
  212.4 0.0 copy-start.2
  212.4 1.1 copy.39
  213.5 0.0 copy-done.2
  213.5 0.7 copy.40
  (6 shorter events, 0.1 us)
Async XLA Ops:
  150.8 59.1 %copy-start.3 = (f32[48,768]{1,0:T(8,128)S(1)}, f32[48,768]{1,0:T(8,128)}, u32[]{:S(2)}) copy-start(f32[48,768]{1,0:T(8,128)} %get-tuple-element.51) | copy-start | bytes 442372
  200.7 10.2 %copy-start.4 = (f32[2,48,128]{2,1,0:T(8,128)S(1)}, f32[2,48,128]{2,1,0:T(8,128)}, u32[]{:S(2)}) copy-start(f32[2,48,128]{2,1,0:T(8,128)} %get-tuple-element.53) | copy-start | bytes 147460
  200.7 10.8 %copy-start.1 = (bf16[4,256,384]{2,1,0:T(8,128)(2,1)S(1)}, bf16[4,256,384]{2,1,0:T(8,128)(2,1)}, u32[]{:S(2)}) copy-start(bf16[4,256,384]{2,1,0:T(8,128)(2,1)} %get-tuple-element.48) | copy-start | bytes 2359300
  208.2 4.2 %copy-start = (f32[4,256,384]{2,1,0:T(8,128)S(1)}, f32[4,256,384]{2,1,0:T(8,128)}, u32[]{:S(2)}) copy-start(f32[4,256,384]{2,1,0:T(8,128)} %get-tuple-element.49) | copy-start | bytes 4718596
  212.4 1.1 copy-start.2

commit v2 on v1

--- a/solution.py
+++ b/solution.py
@@ -19,7 +19,7 @@
 NN = ((1,), (0,))
 NT = ((1,), (1,))
 TN = ((0,), (0,))
-VMEM_LIMIT = 60 * 2**20
+VMEM_LIMIT = 62 * 2**20
 
 GAIN, INNER_GAIN, SKIP, BIAS, STEP_BIAS, RATE, TAPS = 0, 1, 2, 3, 4, 5, 6
 
@@ -724,18 +724,17 @@
     def __init__(self, backward, size, state, decay, out, refs):
         self.state, self.decay, self.out, self.size = state, decay, out, size
         (
-            self.slots, self.rates, self.total, self.through, self.arriving, self.leaving,
-            self.staged, self.s1, self.r1, self.s2, self.r2, self.zs, self.zr, self.s3, self.r3,
+            self.slots, self.rates, self.total, self.through, self.pair, self.pair_through,
+            self.far, self.leaving, self.staged, self.s1, self.r1, self.s2, self.r2, self.zs,
+            self.zr, self.s3, self.r3,
         ) = refs
         s, c, z, y, x = place()
-        self.c, self.p = c, s % PLANE
+        self.s, self.c, self.p = s, c, s % PLANE
         self.base = s - self.p
         self.order = tuple(range(PLANE - 1, -1, -1)) if backward else tuple(range(PLANE))
         self.rows = state.shape[1] // PLANE
         self.place = LINE - 1 - z if backward else z
-        self.before, self.after = self.place > 0, self.place < LINE - 1
         self.step = -PLANE if backward else PLANE
-        self.s = s
 
     @staticmethod
     def scratch(count, rows, nstate, heads):
@@ -745,20 +744,25 @@
             rates=pltpu.VMEM((count, PLANE, heads, nstate), F32),
             total=pltpu.VMEM((count, quarter, nstate), F32),
             through=pltpu.VMEM((count, 8, nstate), F32),
-            arriving=pltpu.VMEM((count, quarter, nstate), BF16),
+            pair=pltpu.VMEM((count, quarter, nstate), BF16),
+            pair_through=pltpu.VMEM((count, 8, nstate), F32),
+            far=pltpu.VMEM((count, quarter, nstate), BF16),
             leaving=pltpu.VMEM((count, quarter, nstate), BF16),
             staged=pltpu.VMEM((count, PLANE, quarter, nstate), BF16),
             s1=dma(count, PLANE), r1=dma(count, PLANE),
             s2=dma(count, PLANE), r2=dma(count, PLANE),
-            zs=dma(count), zr=dma(count),
+            zs=dma(count, 3), zr=dma(count, 3),
             s3=dma(count, PLANE), r3=dma(count, PLANE),
         )
 
     def relations(self):
         plane = [(self.p != j, (self.base + j, self.c)) for j in range(PLANE)]
+        s, c, at, step = self.s, self.c, self.place, self.step
         return plane + [
-            (self.before, (self.s - self.step, self.c)),
-            (self.after, (self.s + self.step, self.c)),
+            (at > 0, (s - step, c)),
+            (at < LINE - 1, (s + step, c)),
+            (at == 1, (s + 2 * step, c)),
+            (at == 3, (s - 2 * step, c)),
         ]
 
     def part(self, j):
@@ -777,10 +781,20 @@
             ),
         ]
 
-    def z_copy(self, i):
+    def to_pair(self, i):
+        device = (self.s + self.step, self.c)
+        return [
+            remote(self.leaving.at[i], self.pair.at[i], self.zs.at[i, 0], self.zr.at[i, 0], device),
+            remote(
+                self.through.at[i], self.pair_through.at[i], self.zs.at[i, 1], self.zr.at[i, 1],
+                device,
+            ),
+        ]
+
+    def to_far(self, i, n):
         return remote(
-            self.leaving.at[i], self.arriving.at[i], self.zs.at[i], self.zr.at[i],
-            (self.s + self.step, self.c),
+            self.leaving.at[i], self.far.at[i], self.zs.at[i, 0 if n == 1 else 2],
+            self.zr.at[i, 2], (self.s + n * self.step, self.c),
         )
 
     def last(self, i, j, quarter):
@@ -808,6 +822,16 @@
 
     def rate(self, i, j, n):
         return self.rates[i, j, pl.ds(self.p * (self.rows // self.size) + n, 1)]
+
+    def deliver(self, i, entering):
+        for n, rows in self.pieces():
+            held = entering(n, rows)
+            for at, j in enumerate(self.order):
+                self.staged[i, j, rows] = held.astype(BF16)
+                if at < PLANE - 1:
+                    held = self.rate(i, j, n) * held + self.slots[i, j, rows].astype(F32)
+        self.others(lambda j: self.last(i, j, self.p).start())
+        self.out[i, self.part(self.p)] = self.staged[i, self.p]
 
     def fold(self, i):
         def arrived(j):
@@ -825,36 +849,46 @@
             self.total[i, rows] = held
             self.through[i, n : n + 1] = rate
 
-    def chain(self, i):
-        @pl.when(self.before)
-        def _():
-            self.z_copy(i).wait_recv()
-
-        @pl.when(jnp.logical_not(self.before))
-        def _():
-            self.arriving[i] = jnp.zeros(self.arriving.shape[1:], BF16)
-
-        for n, rows in self.pieces():
-            self.leaving[i, rows] = (
-                self.total[i, rows]
-                + self.through[i, n : n + 1] * self.arriving[i, rows].astype(F32)
-            ).astype(BF16)
-        pl.when(self.after)(self.z_copy(i).start)
-        for n, rows in self.pieces():
-            held = self.arriving[i, rows].astype(F32)
-            for at, j in enumerate(self.order):
-                self.staged[i, j, rows] = held.astype(BF16)
-                if at < PLANE - 1:
-                    held = self.rate(i, j, n) * held + self.slots[i, j, rows].astype(F32)
-        self.others(lambda j: self.last(i, j, self.p).start())
-        self.out[i, self.part(self.p)] = self.staged[i, self.p]
-
-    def events(self, k):
-        count = self.state.shape[0]
-        pl.when((k >= 0) & (k < count))(lambda: self.start(k))
-        pl.when((k >= 1) & (k <= count))(lambda: self.fold(k - 1))
-        at = k - 1 - self.place
-        pl.when((at >= 0) & (at < count))(lambda: self.chain(at))
+        @pl.when((self.place == 0) | (self.place == 2))
+        def _():
+            self.leaving[i] = self.total[i].astype(BF16)
+            for copy in self.to_pair(i):
+                copy.start()
+
+        @pl.when(self.place == 0)
+        def _():
+            self.deliver(i, lambda n, rows: jnp.zeros((self.size, self.out.shape[2]), F32))
+
+    def join(self, i):
+        @pl.when(self.place == 1)
+        def _():
+            for copy in self.to_pair(i):
+                copy.wait_recv()
+            for n, rows in self.pieces():
+                self.leaving[i, rows] = (
+                    self.total[i, rows]
+                    + self.through[i, n : n + 1] * self.pair[i, rows].astype(F32)
+                ).astype(BF16)
+            for n in (1, 2):
+                self.to_far(i, n).start()
+            self.deliver(i, lambda n, rows: self.pair[i, rows].astype(F32))
+
+    def close(self, i):
+        @pl.when(self.place == 2)
+        def _():
+            self.to_far(i, 1).wait_recv()
+            self.deliver(i, lambda n, rows: self.far[i, rows].astype(F32))
+
+        @pl.when(self.place == 3)
+        def _():
+            for copy in self.to_pair(i):
+                copy.wait_recv()
+            self.to_far(i, 1).wait_recv()
+            self.deliver(
+                i,
+                lambda n, rows: self.pair[i, rows].astype(F32)
+                + self.pair_through[i, n : n + 1] * self.far[i, rows].astype(F32),
+            )
 
     def arrived(self, i):
         self.others(lambda j: self.last(i, j, j).wait_recv())
@@ -868,7 +902,16 @@
                 self.last(i, j, self.p).wait_send()
 
             self.others(close)
-            pl.when(self.after)(self.z_copy(i).wait_send)
+
+            @pl.when((self.place == 0) | (self.place == 2))
+            def _():
+                for copy in self.to_pair(i):
+                    copy.wait_send()
+
+            @pl.when(self.place == 1)
+            def _():
+                for n in (1, 2):
+                    self.to_far(i, n).wait_send()
 
 
 class Reduce:
@@ -1070,13 +1113,23 @@
         r.g_out.shape[0],
         picked(r, REDUCE_REFS),
     )
+    wide = inner + nstate + LANES
+    late = Reduce(
+        (
+            (r.dout, 0, wide // 2, True, r.g_x, 0, 0),
+            (r.dgate, 0, wide // 2, False, r.g_x, wide // 2, wide // 2),
+        ),
+        r.g_x.shape[0],
+        picked(r, LATE_REFS),
+    )
     spread = head_spread(inner, size)
     mine = pl.ds(pl.multiple_of(inner + c * nstate, LANES), nstate)
     side = pl.ds(pl.multiple_of(c * half, LANES), half)
     other_side = pl.ds(pl.multiple_of((1 - c) * half, LANES), half)
-    log_at, step_at, pre_at, entry_at, tail_at = (
-        slice(n * LANES, (n + 1) * LANES) for n in range(5)
-    )
+    log_at, step_at, pre_at, entry_at = (
+        slice(n * LANES, (n + 1) * LANES) for n in range(4)
+    )
+    scores_at = slice(half, half + length)
     own_at, slope_at, gpre_at = (
         slice(half + n * nstate, half + (n + 1) * nstate) for n in range(3)
     )
@@ -1092,6 +1145,7 @@
     swap_sums = swap(2, r.sums, r.sums_in)
     swap_out = swap(3, r.osend, r.out_in)
     swap_states = swap(4, r.bsend, r.brecv)
+    swap_part = swap(6, r.normal, r.low)
 
     def send_edge(i):
         return remote(r.edge.at[i], r.edge_in.at[i], r.ss.at[5, i], r.rs.at[5, i], to_prv)
@@ -1101,25 +1155,13 @@
         device = (s + 1, c if k == 0 else 1 - c)
         return remote(tails, r.halo.at[:, :, side], r.hs.at[k], r.hr.at[k], device)
 
-    stores = dict(
-        normed=lambda i: (r.normed_s.at[i, pl.ds(HALO, length)], r.normed.at[i]),
-        xs=lambda i: (r.xs_s.at[i], r.xs.at[i]),
-        ggate=lambda i: (r.ggate_s.at[i], r.ggate.at[i]),
-        keep=lambda i: (r.gate.at[i, :, pl.ds(0, half)], r.keep.at[i]),
-        gcx=lambda i: (r.gn.at[i], r.gcx.at[i]),
-        gpre=lambda i: (r.gate.at[i, :, gpre_at], r.gpre.at[i]),
-        gst=lambda i: (r.gate.at[i, :, own_at], r.gst.at[i]),
-        w=lambda i: (r.w, r.w_out),
-        w2=lambda i: (r.w2_full.at[:, pl.ds(0, inner)], r.w2_out),
-    )
-
-    def store(name, i):
-        source, target = stores[name](i)
-        n = tuple(stores).index(name)
-        return pltpu.make_async_copy(source, target, r.store.at[n, i])
-
-    def bias_row(at):
-        return r.prm[BIAS : BIAS + 1, at]
+    def store_grad(i):
+        return pltpu.make_async_copy(
+            r.full.at[i, :, pl.ds(0, half)], r.tokens_grad.at[i], r.store.at[0, i]
+        )
+
+    def store_mixed(i):
+        return pltpu.make_async_copy(r.g_in.at[i], r.mixed.at[i], r.store.at[1, i])
 
     def conv(at):
         pre = r.prm[BIAS : BIAS + 1, at]
@@ -1130,6 +1172,7 @@
 
     greet(
         prefix.relations()
+        + [(z != j, (s + (j - z) * PLANE, c)) for j in range(LINE)]
         + [
             (True, to_core),
             (nxt, (s + 1, c)),
@@ -1185,11 +1228,9 @@
     first_gather.first_arrived(-2, 2, -3, 3)
     second_gather.begin()
     first_gather.finish()
-    store("w", 0).start()
     kept, ones = triangle(length)
 
-    @pl.loop(0, count)
-    def _(i):
+    def project(i):
         xs = dot(r.normed_s[i], r.w[:, :channels]).astype(BF16)
         r.xs_s[i] = xs
         r.ext[...] = xs.astype(F32)
@@ -1210,7 +1251,6 @@
         r.aux[i, :, step_at] = step
         r.aux[i, :, pre_at] = step_pre
         r.aux[i, :, entry_at] = entry
-        r.aux[i, :, tail_at] = tail
         log_rows = log_decay.T
         whole_decay = jnp.where(
             doc_row[:, length - 1 :] == 0.0, jnp.exp(log_rows[:HEAD_ROWS, length - 1 :]), 0.0
@@ -1221,9 +1261,11 @@
         r.state[i] = dot(
             (inputs * expand(tail, spread)).astype(BF16), act[:, inner : inner + nstate], TN
         ).astype(BF16)
-        prefix.events(i)
-        store("normed", i).start()
-        store("xs", i).start()
+        prefix.start(i)
+
+    @pl.loop(0, count)
+    def _(i):
+        project(i)
 
         @pl.when(i == 1)
         def _():
@@ -1232,16 +1274,17 @@
 
         @pl.when(i == 2)
         def _():
+            prefix.fold(0)
             second_gather.z_arrived(-2, 2)
             second_gather.first_arrived(-1, 1)
 
         @pl.when(i == 3)
         def _():
+            prefix.fold(1)
             second_gather.z_arrived(-3, 3)
             second_gather.first_arrived(-2, 2)
 
-    @pl.loop(0, count)
-    def _(i):
+    def inside(i):
         log_decay = r.aux[i, :, log_at]
         log_rows = log_decay.T
         doc_col, doc_row = doc_numbers(r.doc[i], ones)
@@ -1257,24 +1300,52 @@
                 term = dot((scores * decay).astype(BF16), own)
                 total = term if total is None else total + term
             r.full[i, :, columns] = total
-        prefix.events(i + count)
+
+    @pl.loop(0, count)
+    def _(i):
+        inside(i)
 
         @pl.when(i == 0)
         def _():
+            prefix.join(0)
             second_gather.first_arrived(-3, 3)
 
+        @pl.when(i == 1)
+        def _():
+            prefix.fold(2)
+            prefix.join(1)
+
+        @pl.when(i == 2)
+        def _():
+            prefix.fold(3)
+            prefix.close(0)
+
+        @pl.when(i == 3)
+        def _():
+            prefix.join(2)
+            prefix.close(1)
+
     second_gather.finish()
-    store("w2", 0).start()
     for i in range(count):
         swap_grads(i).wait()
 
+    def gates(i):
+        r.gate[i] = dot(r.normed_s[i, HALO:], r.w2_full[:, :inner])
+        r.gn[i] = dot(either(c, r.g[i], r.g_in[i]), r.w2_full[:, inner:])
+
     @pl.loop(0, count)
     def _(i):
-        r.gate[i] = dot(r.normed_s[i, HALO:], r.w2_full[:, :inner])
-        r.gn[i] = dot(either(c, r.g[i], r.g_in[i]), r.w2_full[:, inner:])
-
-    @pl.loop(0, count)
-    def _(i):
+        gates(i)
+
+        @pl.when(i == 0)
+        def _():
+            prefix.join(3)
+
+        @pl.when(i == 1)
+        def _():
+            prefix.close(2)
+
+    def combine(i):
         prefix.arrived(i)
         values = r.act[i, :, :inner].astype(F32)
         entry = expand(r.aux[i, :, entry_at], spread)
@@ -1288,13 +1359,10 @@
             r.gn[i] * r.prm[INNER_GAIN : INNER_GAIN + 1, :inner] * gated, axis=-1, keepdims=True
         )
         lane = lax.broadcasted_iota(jnp.int32, (length, LANES), 1)
-        r.sums[i] = jnp.where(lane == 0, squares, jnp.where(lane == 1, cross, 0.0))
+        r.sums[i] = jnp.where(lane == 0, squares, jnp.where(lane == 1, cross, 0.0)).T[:EDGE]
         swap_sums(i).start()
 
-    prefix.finish()
-
-    @pl.loop(0, count)
-    def _(i):
+    def norm_back(i):
         swap_sums(i).wait_recv()
         values = r.act[i, :, :inner].astype(F32)
         mixed = r.full[i] + r.prm[SKIP : SKIP + 1, :inner] * values
@@ -1302,7 +1370,9 @@
         sig = sigmoid(gate)
         swish = gate * sig
         gated = mixed * swish
-        both = r.sums[i] + r.sums_in[i]
+        both = jnp.concatenate(
+            [r.sums[i] + r.sums_in[i], jnp.zeros((LANES - EDGE, length), F32)], axis=0
+        ).T
         inner_scale = lax.rsqrt(both[:, 0:1] / total_inner + EPSILON)
         gain = r.prm[INNER_GAIN : INNER_GAIN + 1, :inner]
         unit = gated * inner_scale
@@ -1321,22 +1391,34 @@
         r.prior[i] = dot(
             (dy * entry).astype(BF16), r.act[i, :, inner + nstate :], TN
         ).astype(BF16)
-        suffix.events(i)
-        r.small[1:2, :inner] += grad_inner
+        suffix.start(i)
+        r.small[0:1, :inner] += grad_inner
         per_head = head_sums(
             jnp.broadcast_to(jnp.sum(dy * values, axis=0, keepdims=True), (8, inner)), spread
         )
-        r.small[2:3, :LANES] += per_head[:1]
-        store("ggate", i).start()
-
-    @pl.loop(0, count)
-    def _(i):
+        r.small[1:2, :LANES] += per_head[:1]
+
+    combine(0)
+    combine(1)
+    prefix.close(3)
+    norm_back(0)
+    combine(2)
+    norm_back(1)
+    combine(3)
+    prefix.finish()
+    norm_back(2)
+    suffix.fold(0)
+    norm_back(3)
+    suffix.fold(1)
+
+    def outputs(i):
         r.ginputs[...] = dot(r.normal[i], r.w2_full[:, inner:], NT)
         r.gate[i, :, :half] = r.ginputs[:, side]
         r.osend[i] = r.ginputs[:, other_side].astype(BF16)
         swap_out(i).start()
-        store("keep", i).start()
-        suffix.events(i + count)
+
+    pl.loop(0, count)(outputs)
+    suffix.join(0)
 
     def weights_gradient(source, target, values, rows):
         for n in range(inner // 256):
@@ -1348,15 +1430,68 @@
             target[rows, at] = total.astype(BF16)
 
     weights_gradient(lambda i: r.g[i], r.dout, r.normal, side)
+    suffix.fold(2)
     weights_gradient(lambda i: r.g_in[i], r.dout, r.normal, other_side)
     reduce_.begin(0)
+    suffix.fold(3)
+    suffix.join(1)
+    suffix.close(0)
     weights_gradient(lambda i: r.normed_s[i, HALO:], r.dgate, r.ggate_s, slice(None))
     reduce_.begin(1)
+    suffix.join(2)
+
+    upper, ones_upper = triangle(length, True)
+
+    def back_inside(i):
+        log_decay = r.aux[i, :, log_at]
+        in_state = r.act[i, :, inner : inner + nstate]
+        out_state = r.act[i, :, inner + nstate :]
+        doc_col, doc_row = doc_numbers(r.doc[i], ones)
+        closed = jnp.where(upper & (doc_col == doc_row), 0.0, MASKED)
+        scores = dot(in_state, out_state, NT)
+        log_rows = log_decay.T
+        for pair in range(inner // LANES):
+            columns = slice(pair * LANES, (pair + 1) * LANES)
+            pair_dy = r.dy[i, :, columns]
+            pair_in = r.low[i, :, columns]
+            total = None
+            for h in (2 * pair, 2 * pair + 1):
+                chosen = left if h % 2 == 0 else ~left
+                own_dy = jnp.where(chosen, pair_dy, jnp.zeros_like(pair_dy))
+                decay = jnp.exp(log_rows[h : h + 1] - log_decay[:, h : h + 1] + closed)
+                term = dot((scores * decay).astype(BF16), own_dy)
+                total = term if total is None else total + term
+                grad_decay = dot(pair_in, own_dy, NT) * decay
+                if h == 0:
+                    r.gate[i, :, scores_at] = grad_decay
+                else:
+                    r.gate[i, :, scores_at] += grad_decay
+            r.gn[i, :, columns] = total
 
     @pl.loop(0, count)
     def _(i):
+        back_inside(i)
+
+        @pl.when(i == 0)
+        def _():
+            suffix.close(1)
+            suffix.join(3)
+
+        @pl.when(i == 1)
+        def _():
+            suffix.close(2)
+
+        @pl.when(i == 2)
+        def _():
+            suffix.close(3)
+            reduce_.second(3, -3)
+
+        @pl.when(i == 3)
+        def _():
+            reduce_.second(2, -2)
+
+    def back_rest(i):
         suffix.arrived(i)
-        log_decay = r.aux[i, :, log_at]
         step = r.aux[i, :, step_at]
         entry = r.aux[i, :, entry_at]
         values = r.act[i, :, :inner].astype(F32)
@@ -1365,33 +1500,16 @@
         later = r.later[i]
         wide_dy = r.dy[i].astype(F32)
         step_wide = expand(step, spread)
-        tail_wide = expand(r.aux[i, :, tail_at], spread)
+        log_decay = r.aux[i, :, log_at]
+        doc_col, doc_row = doc_numbers(r.doc[i], ones)
+        tail = jnp.where(
+            doc_col == doc_col[length - 1 :], jnp.exp(log_decay[length - 1 :] - log_decay), 0.0
+        )
+        tail_wide = expand(tail, spread)
         entry_wide = expand(entry, spread)
-        upper, ones_upper = triangle(length, True)
-        doc_col, doc_row = doc_numbers(r.doc[i], ones)
-        closed = jnp.where(upper & (doc_col == doc_row), 0.0, MASKED)
-        scores = dot(in_state, out_state, NT)
-        log_rows = log_decay.T
-        r.ginputs[...] = tail_wide * dot(in_state, later, NT)
-        for pair in range(inner // LANES):
-            columns = slice(pair * LANES, (pair + 1) * LANES)
-            pair_dy = r.dy[i, :, columns]
-            pair_in = r.low[i, :, columns]
-            total = r.ginputs[:, columns]
-            for h in (2 * pair, 2 * pair + 1):
-                chosen = left if h % 2 == 0 else ~left
-                own_dy = jnp.where(chosen, pair_dy, jnp.zeros_like(pair_dy))
-                decay = jnp.exp(log_rows[h : h + 1] - log_decay[:, h : h + 1] + closed)
-                total = total + dot((scores * decay).astype(BF16), own_dy)
-                grad_decay = dot(pair_in, own_dy, NT) * decay
-                if h == 0:
-                    r.dcb[...] = grad_decay
-                else:
-                    r.dcb[...] += grad_decay
-            r.ginputs[:, columns] = total
-        grad_inputs = r.ginputs[...]
-        grad_scores = r.dcb[...]
         inputs = values * step_wide
+        grad_inputs = r.gn[i] + tail_wide * dot(in_state, later, NT)
+        grad_scores = r.gate[i, :, scores_at]
         grad_in = dot(grad_scores.astype(BF16), out_state) + dot(
             (inputs * tail_wide).astype(BF16), later
         )
@@ -1401,7 +1519,6 @@
         is_first = c == 0
         r.gate[i, :, own_at] = jnp.where(is_first, grad_in, grad_out)
         r.bsend[i] = jnp.where(is_first, grad_out, grad_in).astype(BF16)
-        swap_states(i).start()
         entry_last = jnp.broadcast_to(entry[length - 1 :], (8, LANES))
         later_wide = later.astype(F32)
         lane_ones = jnp.ones((8, nstate), BF16)
@@ -1414,77 +1531,224 @@
         grad_log = head_sums(wide_dy * r.full[i], spread) - head_sums(
             r.low[i].astype(F32) * grad_inputs, spread
         )
+        swap_states(i).start()
         grad_rate_step = running_sum(ones_upper, grad_log) + ending
         rate = r.prm[RATE : RATE + 1, :LANES]
         grad_step = head_sums(values * grad_inputs, spread) + rate * grad_rate_step
         lane = lax.broadcasted_iota(jnp.int32, (length, LANES), 1)
         gpre = jnp.where(lane < heads, grad_step * sigmoid(r.aux[i, :, pre_at]), 0.0)
         r.gate[i, :, gpre_at] = gpre
-        store("gpre", i).start()
         grad_values = step_wide * grad_inputs + r.prm[SKIP : SKIP + 1, :inner] * wide_dy
         r.ext[...] = r.xs_s[i].astype(F32)
         px = conv(slice(0, inner))
         sig = sigmoid(px)
         gcx = grad_values * (sig * (1.0 + px * (1.0 - sig)))
         r.gn[i] = gcx
-        store("gcx", i).start()
         r.edge[i, :, :inner] = gcx[:EDGE]
         ps = conv(mine)
         sig = sigmoid(ps)
         r.gate[i, :, slope_at] = sig * (1.0 + ps * (1.0 - sig))
-        r.small[3:4, :LANES] += jnp.sum(gpre, axis=0, keepdims=True)
-        r.small[4:5, :LANES] += rate * jnp.sum(step * grad_rate_step, axis=0, keepdims=True)
-
-        def finish_states(n):
-            swap_states(n).wait_recv()
-            gst = (r.gate[n, :, own_at] + r.brecv[n].astype(F32)) * r.gate[n, :, slope_at]
-            r.gate[n, :, own_at] = gst
-            store("gst", n).start()
-            r.edge[n, :, inner:] = gst[:EDGE]
-            pl.when(prv)(send_edge(n).start)
-
+        r.small[1:2, LANES : 2 * LANES] += jnp.sum(gpre, axis=0, keepdims=True)
+        r.small[1:2, 2 * LANES : 3 * LANES] += rate * jnp.sum(
+            step * grad_rate_step, axis=0, keepdims=True
+        )
+
+
+    def finish_states(n):
+        swap_states(n).wait_recv()
+        gst = (r.gate[n, :, own_at] + r.brecv[n].astype(F32)) * r.gate[n, :, slope_at]
+        r.gate[n, :, own_at] = gst
+        r.edge[n, :, inner:] = gst[:EDGE]
+        pl.when(prv)(send_edge(n).start)
+
+    @pl.loop(0, count)
+    def _(i):
+        back_rest(i)
         pl.when(i > 0)(lambda: finish_states(i - 1))
 
         @pl.when(i == 0)
         def _():
-            reduce_.second(3, -3, 2, -2)
+            reduce_.second(1, -1)
 
         @pl.when(i == 1)
         def _():
-            reduce_.second(1, -1, 0)
+            reduce_.second(0)
             reduce_.third(3, -3)
 
         @pl.when(i == 2)
         def _():
             reduce_.third(2, -2)
 
-        @pl.when(i == count - 1)
-        def _():
-            finish_states(i)
+        @pl.when(i == 3)
+        def _():
             reduce_.third(1, -1)
 
-    reduce_.third(0)
+    r.conv_rows[...] = jnp.zeros_like(r.conv_rows)
+    r.bc[...] = jnp.zeros_like(r.bc)
+
+    def conv_back(i):
+        pl.when(nxt)(send_edge(i).wait_recv)
+        r.gext[:length, :inner] = r.gn[i]
+        r.gext[:length, inner:] = r.gate[i, :, own_at]
+        r.gext[length:] = jnp.where(nxt, r.edge_in[i], 0.0)
+        r.ext[:, :inner] = r.xs_s[i, :, :inner].astype(F32)
+        r.ext[:, inner : inner + nstate] = r.xs_s[i, :, mine].astype(F32)
+        grad_conv = r.gext[:length]
+        grad_in = None
+        for t in range(taps):
+            row = jnp.concatenate(
+                [r.prm[TAPS + t : TAPS + t + 1, :inner], r.prm[TAPS + t : TAPS + t + 1, mine]],
+                axis=1,
+            )
+            term = row * r.gext[taps - 1 - t : taps - 1 - t + length]
+            grad_in = term if grad_in is None else grad_in + term
+            start = HALO - taps + 1 + t
+            r.conv_rows[t : t + 1] += jnp.sum(
+                r.ext[start : start + length, : inner + nstate] * grad_conv, axis=0, keepdims=True
+            )
+        r.conv_rows[taps : taps + 1] += jnp.sum(grad_conv, axis=0, keepdims=True)
+        low = grad_in.astype(BF16)
+        low_pre = r.gate[i, :, gpre_at].astype(BF16)
+        part = dot(r.ggate_s[i], r.w2_full[:, :inner], NT)
+        part = part + dot(low[:, :inner], r.w[:, :inner], NT)
+        part = part + dot(low[:, inner:], r.w[:, mine], NT)
+        part = part + dot(low_pre, r.w[:, channels:], NT)
+        low_part = part.astype(BF16)
+        r.normal[i] = low_part
+        swap_part(i).start()
+        r.dy[i] = low[:, :inner]
+        r.gtail[i, :, :nstate] = low[:, inner:]
+        r.gtail[i, :, nstate:] = low_pre
+        tok = either(c, r.tok[i].astype(F32), r.tok_in[i].astype(F32))
+        unit = tok * lax.rsqrt(jnp.mean(tok * tok, axis=-1, keepdims=True) + EPSILON)
+        r.bc[0:1, :inner] += jnp.sum(low_part.astype(F32) * unit, axis=0, keepdims=True)
+
+    @pl.loop(0, count)
+    def _(i):
+        conv_back(i)
+
+        @pl.when(i == 0)
+        def _():
+            finish_states(count - 1)
+
+        @pl.when(i == 1)
+        def _():
+            reduce_.third(0)
+
+    def small_copy(source, target, at, device):
+        return remote(source, target, r.qs.at[at], r.qr.at[at], device)
+
+    core_copy = small_copy(r.bc, r.bc_in, 0, to_core)
+    x_copy = small_copy(r.work.at[0], r.from_x, 1, late.to_x)
+    y_copy = small_copy(r.work.at[1], r.from_y, 2, late.to_y)
+    states_copy = small_copy(r.states_s.at[c], r.states_s.at[c], 7, to_core)
+
+    def z_small(j, slot):
+        return remote(
+            r.work.at[2], r.from_z.at[slot], r.qs.at[3 + j], r.qr.at[3 + slot],
+            (s + (j - z) * PLANE, c),
+        )
+
+    for t in range(taps + 1):
+        begin = (t % 3) * 2 * nstate
+        own = r.conv_rows[t : t + 1, inner:]
+        row = 1 + t // 3
+        r.bc[row : row + 1, begin : begin + nstate] = jnp.where(c == 0, own, 0.0)
+        r.bc[row : row + 1, begin + nstate : begin + 2 * nstate] = jnp.where(c == 1, own, 0.0)
+    core_copy.start()
+
+    def gradient_block(source, at, target, start):
+        total = None
+        for i in range(count):
+            term = dot(r.normed_s[i, HALO:], source[i, :, at : at + 256], TN)
+            total = term if total is None else total + term
+        target[:, start : start + 256] = total.astype(BF16)
+
     reduce_.finish()
+    gradient_block(r.dy, 0, r.dout, 0)
+    core_copy.wait_recv()
+    r.work[0, 0:2] = r.small[0:2]
+    r.work[0, 2 : 3 + taps] = r.conv_rows[: taps + 1, :inner]
+    r.work[0, 3 + taps : 8] = jnp.zeros((5 - taps, inner), F32)
+    r.work[0, 8:16] = r.bc[...] + r.bc_in[...]
+    x_copy.start()
+    gradient_block(r.dy, 256, r.dout, 256)
+    late.begin(0)
+    gradient_block(r.dy, 512, r.dgate, 0)
+    gradient_block(r.gtail, 0, r.dgate, 256)
+    late.begin(1)
+
+    def tokens_back(i):
+        swap_part(i).wait_recv()
+        swap_out(i).wait_recv()
+        own_tok = r.tok[i].astype(F32)
+        tok = either(c, own_tok, r.tok_in[i].astype(F32))
+        scale = lax.rsqrt(jnp.mean(tok * tok, axis=-1, keepdims=True) + EPSILON)
+        unit = tok * scale
+        grad_normed = r.normal[i].astype(F32) + r.low[i].astype(F32)
+        grad = grad_normed * r.prm[GAIN : GAIN + 1, : 2 * half]
+        r.ginputs[...] = scale * (grad - unit * jnp.mean(grad * unit, axis=-1, keepdims=True))
+        r.full[i, :, :half] = r.g[i].astype(F32) + r.ginputs[:, side]
+        store_grad(i).start()
+        r.g_in[i] = (own_tok + (r.gate[i, :, :half] + r.out_in[i].astype(F32))).astype(BF16)
+        store_mixed(i).start()
+
+    @pl.loop(0, count)
+    def _(i):
+        tokens_back(i)
+
+        @pl.when(i == 0)
+        def _():
+            x_copy.wait_recv()
+            r.work[1] = r.work[0] + r.from_x[...]
+            y_copy.start()
+
+        @pl.when(i == 2)
+        def _():
+            y_copy.wait_recv()
+            r.work[2] = r.work[1] + r.from_y[...]
+            for j in range(LINE):
+                pl.when(z != j)(z_small(j, z).start)
+            r.from_z[z] = r.work[2]
+
+    late.second(3, -3, 2, -2)
+    late.third(3, -3)
+    late.second(1, -1)
+    late.third(2, -2)
+    late.second(0)
+    late.third(1, -1)
+    late.third(0, only=(1,))
+    r.states_s[c] = r.g_x[:, inner : inner + nstate]
+    states_copy.start()
+    late.third(0, only=(0,))
+    for j in range(LINE):
+        pl.when(z != j)(z_small(j, j).wait_recv)
+    r.sums_out[...] = (r.from_z[0] + r.from_z[1]) + (r.from_z[2] + r.from_z[3])
+    states_copy.wait()
+    r.states[...] = r.states_s[...]
+    core_copy.wait_send()
+    x_copy.wait_send()
+    y_copy.wait_send()
+    for j in range(LINE):
+        pl.when(z != j)(z_small(j, z).wait_send)
+    late.finish()
     suffix.finish()
 
     @pl.loop(0, count)
     def _(i):
         swap_sums(i).wait_send()
-        swap_out(i).wait()
+        swap_out(i).wait_send()
         swap_states(i).wait_send()
         pl.when(prv)(send_edge(i).wait_send)
-        pl.when(nxt)(send_edge(i).wait_recv)
-        for name in stores:
-            if name not in SINGLE:
-                store(name, i).wait()
-
-    for name in SINGLE:
-        store(name, 0).wait()
-
-
-SINGLE = tuple(dict(w=0, w2=0))
+        swap_part(i).wait_send()
+        store_grad(i).wait()
+        store_mixed(i).wait()
+
+
+LOCAL_REFS = tuple(dict(kept=0, mid_send=0))
+LATE_REFS = tuple(n if n in LOCAL_REFS else "l" + n for n in REDUCE_REFS)
 SECOND_REFS = tuple("s" + n for n in GATHER_REFS)
-SHARED_REFS = tuple(dict(total=0, through=0, leaving=0, staged=0))
+SHARED_REFS = tuple(dict(total=0, leaving=0, staged=0))
 SUFFIX_REFS = tuple(n if n in SHARED_REFS else "s" + n for n in SCAN_REFS)
 
 
@@ -1494,26 +1758,19 @@
     model = 2 * half
     channels = inner + 2 * nstate
     rows = w1.shape[0]
+    wide = inner + nstate + LANES
     ins = dict(
         tok=(tok, INSIDE), g=(g, INSIDE), doc=(doc, INSIDE), prm=(prm, INSIDE),
         w1=(w1, ANYWHERE), w2=(w2, ANYWHERE),
     )
     outs = dict(
-        normed=(shape((count, length, model), BF16), ANYWHERE),
-        xs=(shape((count, HALO + length, channels), BF16), ANYWHERE),
-        ggate=(shape((count, length, inner), BF16), ANYWHERE),
-        keep=(shape((count, length, half), F32), ANYWHERE),
-        gpre=(shape((count, length, LANES), F32), ANYWHERE),
-        gcx=(shape((count, length, inner), F32), ANYWHERE),
-        gst=(shape((count, length, nstate), F32), ANYWHERE),
-        out_in=(shape((count, length, half), BF16), ANYWHERE),
-        edge_in=(shape((count, EDGE, inner + nstate), F32), ANYWHERE),
-        w_out=(shape((model, w1.shape[1]), BF16), ANYWHERE),
-        w2_out=(shape((model, inner), BF16), ANYWHERE),
-        tok_in=(shape(tok.shape, BF16), INSIDE),
-        small=(shape((8, channels), F32), INSIDE),
+        mixed=(shape((count, length, half), BF16), ANYWHERE),
+        tokens_grad=(shape((count, length, half), F32), ANYWHERE),
         g_out=(shape((rows, inner), F32), INSIDE),
         g_gate=(shape((rows, inner), F32), INSIDE),
+        g_x=(shape((rows, wide), F32), INSIDE),
+        states=(shape((2, rows, nstate), F32), INSIDE),
+        sums_out=(shape((16, inner), F32), INSIDE),
     )
 
     def vmem(*dims, dtype=F32):
@@ -1524,13 +1781,29 @@
 
     scratch = dict(
         g_in=low(count, length, half),
+        tok_in=low(count, length, half),
+        out_in=low(count, length, half),
+        edge_in=vmem(count, EDGE, inner + nstate),
+        small=vmem(8, inner),
+        gtail=low(count, length, nstate + LANES),
+        gext=vmem(length + EDGE, inner + nstate),
+        conv_rows=vmem(8, inner + nstate),
+        states_s=vmem(2, rows, nstate),
+        bc=vmem(8, inner),
+        bc_in=vmem(8, inner),
+        work=vmem(3, 16, inner),
+        from_x=vmem(16, inner),
+        from_y=vmem(16, inner),
+        from_z=vmem(LINE, 16, inner),
+        qs=dma(8),
+        qr=dma(8),
         halo=low(count, HALO, model),
         w=low(model, w1.shape[1]),
         w2_full=low(model, 2 * inner),
         normed_s=low(count, HALO + length, model),
         xs_s=low(count, HALO + length, channels),
         act=low(count, length, channels),
-        aux=vmem(count, length, 5 * LANES),
+        aux=vmem(count, length, 4 * LANES),
         low=low(count, length, inner),
         dec=vmem(count, HEAD_ROWS, LANES),
         state=low(count, inner, nstate),
@@ -1540,8 +1813,8 @@
         full=vmem(count, length, inner),
         gate=vmem(count, length, inner),
         gn=vmem(count, length, inner),
-        sums=vmem(count, length, LANES),
-        sums_in=vmem(count, length, LANES),
+        sums=vmem(count, EDGE, length),
+        sums_in=vmem(count, EDGE, length),
         normal=low(count, length, inner),
         dy=low(count, length, inner),
         ggate_s=low(count, length, inner),
@@ -1550,15 +1823,14 @@
         dgate=low(model, inner),
         ext=vmem(HALO + length, channels),
         ginputs=vmem(length, inner),
-        dcb=vmem(length, length),
         bsend=low(count, length, nstate),
         brecv=low(count, length, nstate),
         edge=vmem(count, EDGE, inner + nstate),
-        ss=dma(6, count),
-        rs=dma(6, count),
+        ss=dma(7, count),
+        rs=dma(7, count),
         hs=dma(2),
         hr=dma(2),
-        store=dma(9, count),
+        store=dma(2, count),
     )
     scan = Scan.scratch(count, inner, nstate, HEAD_ROWS)
     gather = Gather.semaphores(2)
@@ -1566,266 +1838,34 @@
     scratch.update(scan)
     scratch.update(gather)
     scratch.update(zip(SECOND_REFS, gather.values()))
+    scratch.update(zip(LATE_REFS, Reduce.scratch(2, rows, wide).values()))
     scratch.update(Reduce.scratch(2, rows, 2 * inner))
     return fused_call(
         functools.partial(main_body, sizes, total_inner), None, ins, outs, scratch, 1, "main"
     )
-
-
-def back_body(sizes, r):
-    length, inner, nstate, size, taps = sizes
-    k = pl.program_id(0)
-    s, c, z, y, x = place()
-    to_core = (s, 1 - c)
-    wide = inner + nstate + LANES
-    reduce_ = Reduce(
-        (
-            (r.dx, 0, wide // 2, True, r.g_x, 0, 0),
-            (r.dx, wide // 2, wide // 2, False, r.g_x, wide // 2, wide // 2),
-        ),
-        r.g_x.shape[0],
-        picked(r, REDUCE_REFS),
-    )
-    lines = [(z != j, (s + (j - z) * PLANE, c)) for j in range(LINE)]
-
-    def swap_part(i):
-        return remote(r.part.at[i], r.part_in.at[i], r.ps.at[i], r.pr.at[i], to_core)
-
-    def small_copy(src, dst, at, device):
-        return remote(src, dst, r.qs.at[at], r.qr.at[at], device)
-
-    core_copy = small_copy(r.bc, r.bc_in, 0, to_core)
-    x_copy = small_copy(r.work.at[0], r.from_x, 1, reduce_.to_x)
-    y_copy = small_copy(r.work.at[1], r.from_y, 2, reduce_.to_y)
-    states_copy = small_copy(r.states_s.at[c], r.states_s.at[c], 7, to_core)
-
-    def z_small(j, slot):
-        return remote(
-            r.work.at[2], r.from_z.at[slot], r.qs.at[3 + j], r.qr.at[3 + slot],
-            (s + (j - z) * PLANE, c),
-        )
-
-    @pl.when(k == 0)
-    def _():
-        greet([(True, reduce_.to_x), (True, reduce_.to_y), (True, to_core)] + lines)
-
-    @pl.when(k < 4)
-    def _():
-        last = s == lax.axis_size("seq") - 1
-        mine = pl.ds(pl.multiple_of(inner + c * nstate, LANES), nstate)
-        r.gext[:length, :inner] = r.gcx[0]
-        r.gext[:length, inner:] = r.gst[0]
-        r.gext[length:] = jnp.where(last, 0.0, r.edge_in[0])
-        r.ext[:, :inner] = r.xs[0, :, :inner].astype(F32)
-        r.ext[:, inner:] = r.xs[0, :, mine].astype(F32)
-        grad_conv = r.gext[:length]
-        grad_in = None
-        rows = []
-        for t in range(taps):
-            row = jnp.concatenate(
-                [r.prm[TAPS + t : TAPS + t + 1, :inner], r.prm[TAPS + t : TAPS + t + 1, mine]],
-                axis=1,
-            )
-            term = row * r.gext[taps - 1 - t : taps - 1 - t + length]
-            grad_in = term if grad_in is None else grad_in + term
-            start = HALO - taps + 1 + t
-            rows.append(
-                jnp.sum(r.ext[start : start + length] * grad_conv, axis=0, keepdims=True)
-            )
-        rows.append(jnp.sum(grad_conv, axis=0, keepdims=True))
-        rows.append(jnp.zeros((8 - taps - 1, inner + nstate), F32))
-        rows = jnp.concatenate(rows, axis=0)
-        low = grad_in.astype(BF16)
-        low_pre = r.gpre[0].astype(BF16)
-        part = dot(r.ggate[0], r.w2[:, :inner], NT)
-        part = part + dot(low[:, :inner], r.w[:, :inner], NT)
-        part = part + dot(low[:, inner:], r.w[:, mine], NT)
-        part = part + dot(low_pre, r.w[:, inner + 2 * nstate :], NT)
-        r.part[k] = part.astype(BF16)
-        swap_part(k).start()
-        stacked = jnp.concatenate([low, low_pre], axis=1)
-        term = dot(r.normed[0], stacked, TN)
-
-        @pl.when(k == 0)
-        def _():
-            r.conv_rows[...] = rows
-            r.acc[...] = term
-
-        @pl.when(k > 0)
-        def _():
-            r.conv_rows[...] += rows
-            r.acc[...] += term
-
-    @pl.when(k == 3)
-    def _():
-        r.dx[...] = r.acc[...].astype(BF16)
-        reduce_.begin()
-        own = r.conv_rows[:, inner:]
-        r.bc[:, :nstate] = jnp.where(c == 0, own, 0.0)
-        r.bc[:, nstate:] = jnp.where(c == 1, own, 0.0)
-        core_copy.start()
-
-    @pl.when(k >= 4)
-    def _():
-        i = k - 4
-        swap_part(i).wait_recv()
-        own_tok = r.tok[0].astype(F32)
-        tok = either(c, own_tok, r.tok_in[0].astype(F32))
-        model = tok.shape[1]
-        scale = lax.rsqrt(jnp.mean(tok * tok, axis=-1, keepdims=True) + EPSILON)
-        unit = tok * scale
-        grad_normed = r.part[i].astype(F32) + r.part_in[i].astype(F32)
-        grad = grad_normed * r.prm[GAIN : GAIN + 1, :model]
-        r.wide[...] = scale * (grad - unit * jnp.mean(grad * unit, axis=-1, keepdims=True))
-        half = model // 2
-        r.tokens_grad[0] = (
-            r.g[0].astype(F32) + r.wide[:, pl.ds(pl.multiple_of(c * half, LANES), half)]
-        )
-        r.mixed[0] = (own_tok + (r.keep[0] + r.out_in[0].astype(F32))).astype(BF16)
-        gain = jnp.sum(grad_normed * unit, axis=0, keepdims=True)
-
-        @pl.when(i == 0)
-        def _():
-            r.gain_row[...] = gain
-
-        @pl.when(i > 0)
-        def _():
-            r.gain_row[...] += gain
-
-    @pl.when(k == 4)
-    def _():
-        reduce_.second(3, -3, 2, -2)
-
-    @pl.when(k == 5)
-    def _():
-        reduce_.second(1, -1, 0)
-        reduce_.third(3, -3)
-
-    @pl.when(k == 6)
-    def _():
-        reduce_.third(2, -2)
-
-    @pl.when(k == 7)
-    def _():
-        core_copy.wait_recv()
-        r.work[0] = jnp.zeros(r.work.shape[1:], F32)
-        r.work[0, 0:8] = r.small[...]
-        r.work[0, 0:1, :inner] = r.gain_row[...]
-        r.work[0, 8:16, :inner] = r.conv_rows[:, :inner]
-        r.work[0, 16:24, : 2 * nstate] = r.bc[...] + r.bc_in[...]
-        x_copy.start()
-        reduce_.third(1, -1)
-        x_copy.wait_recv()
-        r.work[1] = r.work[0] + r.from_x[...]
-        y_copy.start()
-        reduce_.third(0, only=(1,))
-        r.states_s[c] = r.g_x[:, inner : inner + nstate]
-        states_copy.start()
-        y_copy.wait_recv()
-        r.work[2] = r.work[1] + r.from_y[...]
-        for j in range(LINE):
-            pl.when(z != j)(z_small(j, z).start)
-        r.from_z[z] = r.work[2]
-        reduce_.third(0, only=(0,))
-        for j in range(LINE):
-            pl.when(z != j)(z_small(j, j).wait_recv)
-        r.sums[...] = (r.from_z[0] + r.from_z[1]) + (r.from_z[2] + r.from_z[3])
-        states_copy.wait()
-        r.states[...] = r.states_s[...]
-        core_copy.wait_send()
-        x_copy.wait_send()
-        y_copy.wait_send()
-        for j in range(LINE):
-            pl.when(z != j)(z_small(j, z).wait_send)
-        reduce_.finish()
-
-        @pl.loop(0, 4)
-        def _(i):
-            swap_part(i).wait_send()
-
-
-def back_call(sizes, m, tok, g, prm):
-    length, inner, nstate, size, taps = sizes
-    count, _, half = g.shape
-    model = 2 * half
-    channels = inner + 2 * nstate
-    rows = model // lax.axis_size("seq")
-    wide = inner + nstate + LANES
-    first, second = during(0), during(4)
-    ins = dict(
-        gcx=(m.gcx, stepped(m.gcx, first)),
-        gst=(m.gst, stepped(m.gst, first)),
-        gpre=(m.gpre, stepped(m.gpre, first)),
-        ggate=(m.ggate, stepped(m.ggate, first)),
-        edge_in=(m.edge_in, stepped(m.edge_in, first)),
-        xs=(m.xs, stepped(m.xs, first)),
-        normed=(m.normed, stepped(m.normed, first)),
-        tok=(tok, stepped(tok, second)),
-        tok_in=(m.tok_in, stepped(m.tok_in, second)),
-        g=(g, stepped(g, second)),
-        keep=(m.keep, stepped(m.keep, second)),
-        out_in=(m.out_in, stepped(m.out_in, second)),
-        small=(m.small, whole(m.small)),
-        prm=(prm, whole(prm)),
-        w=(m.w_out, whole(m.w_out)),
-        w2=(m.w2_out, whole(m.w2_out)),
-    )
-    grads = shape((count, length, half), F32)
-    mixed = shape((count, length, half), BF16)
-    g_x = shape((rows, wide), F32)
-    states = shape((2, rows, nstate), F32)
-    sums = shape((24, channels), F32)
-    outs = dict(
-        tokens_grad=(grads, stepped(grads, second)),
-        mixed=(mixed, stepped(mixed, second)),
-        g_x=(g_x, whole(g_x)),
-        sums=(sums, whole(sums)),
-        states=(states, whole(states)),
-    )
-    scratch = dict(
-        part=pltpu.VMEM((count, length, model), BF16),
-        part_in=pltpu.VMEM((count, length, model), BF16),
-        acc=pltpu.VMEM((model, wide), F32),
-        dx=pltpu.VMEM((model, wide), BF16),
-        conv_rows=pltpu.VMEM((8, inner + nstate), F32),
-        gain_row=pltpu.VMEM((1, model), F32),
-        ext=pltpu.VMEM((HALO + length, inner + nstate), F32),
-        gext=pltpu.VMEM((length + EDGE, inner + nstate), F32),
-        wide=pltpu.VMEM((length, model), F32),
-        states_s=pltpu.VMEM((2, rows, nstate), F32),
-        bc=pltpu.VMEM((8, 2 * nstate), F32),
-        bc_in=pltpu.VMEM((8, 2 * nstate), F32),
-        work=pltpu.VMEM((3, 24, channels), F32),
-        from_x=pltpu.VMEM((24, channels), F32),
-        from_y=pltpu.VMEM((24, channels), F32),
-        from_z=pltpu.VMEM((LINE, 24, channels), F32),
-        ps=dma(count), pr=dma(count), qs=dma(8), qr=dma(8),
-    )
-    scratch.update(Reduce.scratch(2, rows, wide))
-    return fused_call(functools.partial(back_body, sizes), 8, ins, outs, scratch, 4, "back")
 
 
 def fused_layer(sizes, total_inner, heads, tok, g, doc, prm, w, w2):
     length, inner, nstate, size, taps = sizes
     model = 2 * tok.shape[2]
     m = main_call(sizes, total_inner, tok, g, doc, prm, w, w2)
-    b = back_call(sizes, m, tok, g, prm)
-    sums = b.sums
+    sums = m.sums_out
+    shared = sums[9:11].reshape(-1)[: (taps + 1) * 2 * nstate].reshape(taps + 1, 2 * nstate)
     return (
-        b.mixed,
-        b.tokens_grad,
-        sums[0, :model],
-        jnp.stack([m.g_gate, b.g_x[:, :inner]], axis=1),
-        jnp.concatenate([b.states[0], b.states[1]], axis=1),
-        b.g_x[:, inner + nstate : inner + nstate + heads],
-        sums[8 : 8 + taps, :inner],
-        sums[8 + taps, :inner],
-        sums[16 : 16 + taps, : 2 * nstate],
-        sums[16 + taps, : 2 * nstate],
-        sums[3, :heads],
-        sums[4, :heads],
-        sums[2, :heads],
-        sums[1, :inner],
+        m.mixed,
+        m.tokens_grad,
+        sums[8, :model],
+        jnp.stack([m.g_gate, m.g_x[:, :inner]], axis=1),
+        jnp.concatenate([m.states[0], m.states[1]], axis=1),
+        m.g_x[:, inner + nstate : inner + nstate + heads],
+        sums[2 : 2 + taps],
+        sums[2 + taps],
+        shared[:taps],
+        shared[taps],
+        sums[1, LANES : LANES + heads],
+        sums[1, 2 * LANES : 2 * LANES + heads],
+        sums[1, :heads],
+        sums[0],
         m.g_out.T,
     )
 

time: 215 us -> 188 us (0.87)
  Pallas kernels: 188 us -> 163 us
  local copies, waits for them, and re-layouts: 18.8 us -> 15.9 us
    pallas_call x2 -> x1, Pallas kernels: 188 us -> 163 us  [fused_call(): pl.pallas_call(kernel, grid=(steps,) if steps else (), in_specs=[spec for...]
    slice x5 -> x7, local copies, waits for them, and re-layouts: 6.14 us -> 3.14 us  [the longest x1 0.74 us: fused_layer(): m.g_x[:, inner + nstate:inner + nstate + heads]]
    unnamed x17 -> x15, local copies, waits for them, and re-layouts: 6.03 us -> 6.03 us
where the time goes in v2:
time: 188 us; the launch traced here: 187 us
  Pallas kernels  163 us (87%)
  local copies, waits for them, and re-layouts  15.9 us (8%)
  other arithmetic  7.29 us (4%)
    pallas_call x1, Pallas kernels, fused_call(): pl.pallas_call(kernel, grid=(steps,) if steps else (), in_specs=[spec for...  163 us
    unnamed x15, local copies, waits for them, and re-layouts  6.03 us

profile of v2, /device:TPU:0, one launch (start us, length us, event | category | flops | bytes accessed | tf_op | source)
XLA Modules:
  0.0 187.3 jit_solution(10886876539884644639)
XLA Ops:
  0.6 0.9 copy.34
  1.6 1.6 pad_maximum_fusion.1.refs_5_
  3.1 0.8 copy.31
  3.9 1.4 fusion.1.refs_4_
  5.3 0.7 broadcast_in_dim.29
  6.0 0.1 reshape.69
  6.1 0.7 pad_maximum_fusion.4
  6.9 0.7 exponential_negate_fusion
  7.5 0.7 pad.25
  8.2 0.7 pad.26
  8.9 0.7 pad_maximum_fusion.5
  9.6 0.7 pad.28
  10.3 0.2 concatenate.20
  10.4 0.6 pad.30.refs_3_
  11.1 0.7 convert_element_type.22
  11.8 0.6 broadcast_in_dim.26.refs_2_
  12.4 163.4 %main.1 = (bf16[4,256,384]{2,1,0:T(8,128)(2,1)}, f32[4,256,384]{2,1,0:T(8,128)}, f32[48,768]{1,0:T(8,128)}, f32[48,768]{1,0:T(8,128)}, f32[48,1024]{1,0:T(8,128)...) custom-call(bf16[4,256,384]{2,1,0:T(8,128)(2,1)} %bitcast.31, bf16[4,256,384]{2,1,0:T(8,128)(2,1)} %bitcast.32, ...), custom_call_target="tpu_custom_call" | custom-call | tf_op jit(solution)/shard_map/main/pallas_call | solution.py:572
  175.9 0.0 copy-start.3
  175.9 0.0 copy-start.1
  175.9 0.8 slice_bitcast_fusion.2
  176.7 0.6 pad_maximum_fusion.3
  177.3 0.0 copy-start
  177.3 1.0 slice_bitcast_fusion
  178.4 0.9 pad_maximum_fusion
  179.3 0.9 copy.32
  180.3 0.0 copy-done.3
  180.3 0.6 slice_reduce_fusion
  180.9 0.5 slice_bitcast_fusion.3
  181.4 0.6 slice.75
  182.0 0.6 slice.76
  182.6 0.6 slice.64
  183.2 0.7 slice.63
  183.9 0.7 copy.33
  184.6 0.0 copy-done.1
  184.6 0.9 copy.38
  185.5 0.0 copy-done
  185.5 0.0 copy-start.2
  185.5 1.1 copy.39
  186.6 0.0 copy-done.2
  186.6 0.7 copy.40
  (7 shorter events, 0.1 us)
Async XLA Ops:
  175.9 4.4 %copy-start.3 = (f32[16,768]{1,0:T(8,128)S(1)}, f32[16,768]{1,0:T(8,128)}, u32[]{:S(2)}) copy-start(f32[16,768]{1,0:T(8,128)} %get-tuple-element.24) | copy-start | bytes 147460
  175.9 8.7 %copy-start.1 = (bf16[4,256,384]{2,1,0:T(8,128)(2,1)S(1)}, bf16[4,256,384]{2,1,0:T(8,128)(2,1)}, u32[]{:S(2)}) copy-start(bf16[4,256,384]{2,1,0:T(8,128)(2,1)} %get-tuple-element.22) | copy-start | bytes 2359300
  177.3 8.2 %copy-start = (f32[4,256,384]{2,1,0:T(8,128)S(1)}, f32[4,256,384]{2,1,0:T(8,128)}, u32[]{:S(2)}) copy-start(f32[4,256,384]{2,1,0:T(8,128)} %get-tuple-element.23) | copy-start | bytes 4718596
  185.5 1.1 copy-start.2

commit v3 on v2

--- a/solution.py
+++ b/solution.py
@@ -41,7 +41,7 @@
 
 
 def sigmoid(v):
-    return 1.0 / (1.0 + jnp.exp(-v))
+    return 0.5 * jnp.tanh(0.5 * v) + 0.5
 
 
 def softplus(v):
@@ -609,6 +609,9 @@
     return jnp.concatenate([low, jnp.where(core == 0, other, own)], axis=1)
 
 
+LINE_X, LINE_Y, PLANE_X, PLANE_Y = range(4)
+
+
 class Gather:
     def __init__(self, pieces, rows, sems):
         self.pieces, self.rows = pieces, rows
@@ -618,7 +621,11 @@
         self.up, self.down = self.z < LINE - 1, self.z > 0
         self.to_x, self.to_y = (s + 1 - 2 * self.x, c), (s + 2 - 4 * self.y, c)
         self.to_up, self.to_down = (s + PLANE, c), (s - PLANE, c)
+        kinds = [piece[4] for piece in pieces]
         self.span = range(len(pieces))
+        self.lines = [p for p in self.span if kinds[p] in (LINE_X, LINE_Y)]
+        self.planes = [p for p in self.span if kinds[p] in (PLANE_X, PLANE_Y)]
+        self.x_first = [kind in (LINE_X, PLANE_X) for kind in kinds]
 
     @staticmethod
     def semaphores(n):
@@ -639,10 +646,15 @@
     def local_copy(self, p):
         return pltpu.make_async_copy(self.own(p), self.at(p, self.s), self.local.at[p])
 
+    def block(self, p, zz):
+        if p in self.planes:
+            return self.at(p, zz * PLANE, PLANE)
+        return self.at(p, zz * PLANE + self.y * 2 + self.x)
+
     def z_copy(self, p, off):
         zz = self.z + off
-        dst = self.at(p, zz * PLANE + self.y * 2 + self.x)
-        src = self.own(p) if off == 0 else dst
+        dst = self.block(p, zz)
+        src = self.own(p) if off == 0 and p in self.lines else dst
         step = abs(off)
         moves = []
         if off <= 0:
@@ -657,12 +669,12 @@
         zz = self.z + off
         dst = self.at(p, zz * PLANE + self.y * 2 + self.x)
         src = self.own(p) if off == 0 else dst
-        device = self.to_x if self.pieces[p][4] else self.to_y
+        device = self.to_x if self.x_first[p] else self.to_y
         return remote(src, dst, self.as_.at[p, zz], self.ar.at[p, zz], device)
 
     def second_copies(self, p, off):
         zz = self.z + off
-        if self.pieces[p][4]:
+        if self.x_first[p]:
             pair = self.at(p, zz * PLANE + self.y * 2, 2)
             return [remote(pair, pair, self.bs.at[p, zz, 0], self.br.at[p, zz, 0], self.to_y)]
         copies = []
@@ -679,8 +691,9 @@
 
     def begin(self):
         for p in self.span:
-            for there, copy in self.z_copy(p, 0):
-                pl.when(there)(copy.start)
+            if p in self.lines:
+                for there, copy in self.z_copy(p, 0):
+                    pl.when(there)(copy.start)
             self.first_copy(p, 0).start()
             self.local_copy(p).start()
 
@@ -689,7 +702,7 @@
 
             @pl.when(self.exists(off))
             def _():
-                for p in self.span:
+                for p in self.lines:
                     for there, copy in self.z_copy(p, off):
                         copy.wait_recv()
                         pl.when(there)(copy.start)
@@ -700,24 +713,54 @@
 
             @pl.when(self.exists(off))
             def _():
-                for p in self.span:
+                for p in self.lines:
                     if off == 0:
                         self.local_copy(p).wait()
                     self.first_copy(p, off).wait_recv()
                     for copy in self.second_copies(p, off):
                         copy.start()
 
+    def plane_first(self):
+        for p in self.planes:
+            self.local_copy(p).wait()
+            self.first_copy(p, 0).wait_recv()
+            for copy in self.second_copies(p, 0):
+                copy.start()
+
+    def plane_second(self):
+        for p in self.planes:
+            for copy in self.second_copies(p, 0):
+                copy.wait_recv()
+            for there, copy in self.z_copy(p, 0):
+                pl.when(there)(copy.start)
+
+    def plane_arrived(self, *offs):
+        for off in offs:
+
+            @pl.when(self.exists(off))
+            def _():
+                for p in self.planes:
+                    for there, copy in self.z_copy(p, off):
+                        copy.wait_recv()
+                        pl.when(there)(copy.start)
+
     def finish(self):
         for off in OFFSETS:
 
             @pl.when(self.exists(off))
             def _():
-                for p in self.span:
+                for p in self.lines:
                     for copy in self.second_copies(p, off):
                         copy.wait()
                     self.first_copy(p, off).wait_send()
+                for p in self.span:
                     for there, copy in self.z_copy(p, off):
                         pl.when(there)(copy.wait_send)
+
+        for p in self.planes:
+            self.first_copy(p, 0).wait_send()
+            for copy in self.second_copies(p, 0):
+                copy.wait_send()
 
 
 class Scan:
@@ -1097,12 +1140,22 @@
     to_core, to_prv = (s, 1 - c), (s - 1, c)
     nxt, prv = s < LINE * PLANE - 1, s > 0
     first_gather = Gather(
-        ((r.w1, r.w, 0, 640, True), (r.w1, r.w, 640, r.w1.shape[1] - 640, False)),
+        (
+            (r.w1, r.w, 0, 512, LINE_X),
+            (r.w1, r.w, 512, 384, LINE_Y),
+            (r.w1, r.w, 896, 128, PLANE_X),
+            (r.w1, r.w, 1024, 128, PLANE_Y),
+        ),
         r.w1.shape[0],
         picked(r, GATHER_REFS),
     )
     second_gather = Gather(
-        ((r.w2, r.w2_full, 0, inner, True), (r.w2, r.w2_full, inner, inner, False)),
+        (
+            (r.w2, r.w2_full, 0, 512, LINE_X),
+            (r.w2, r.w2_full, 512, 512, LINE_Y),
+            (r.w2, r.w2_full, 1024, 256, PLANE_X),
+            (r.w2, r.w2_full, 1280, 256, PLANE_Y),
+        ),
         r.w2.shape[0],
         picked(r, SECOND_REFS),
     )
@@ -1188,7 +1241,9 @@
         swap_tokens(i).start()
     r.small[...] = jnp.zeros_like(r.small)
     first_gather.z_arrived(-1, 1)
+    first_gather.plane_first()
     first_gather.first_arrived(0)
+    second_gather.begin()
     for i in range(count):
         swap_grads(i).start()
 
@@ -1205,6 +1260,7 @@
         r.normed_s[i, HALO:, other_side] = (other * scale * gain_other).astype(BF16)
 
     first_gather.z_arrived(-2, 2)
+    first_gather.plane_second()
     first_gather.first_arrived(-1, 1)
     for k in range(2):
         pl.when(nxt)(halo_copy(k).wait_send)
@@ -1225,8 +1281,14 @@
             r.normed_s[i, :HALO] = jnp.zeros((HALO, 2 * half), BF16)
 
     first_gather.z_arrived(-3, 3)
-    first_gather.first_arrived(-2, 2, -3, 3)
-    second_gather.begin()
+    first_gather.plane_arrived(-1, 1)
+    first_gather.first_arrived(-2, 2)
+    second_gather.z_arrived(-1, 1)
+    second_gather.plane_first()
+    first_gather.plane_arrived(-2, 2)
+    first_gather.first_arrived(-3, 3)
+    second_gather.first_arrived(0)
+    first_gather.plane_arrived(-3, 3)
     first_gather.finish()
     kept, ones = triangle(length)
 
@@ -1267,22 +1329,27 @@
     def _(i):
         project(i)
 
+        @pl.when(i == 0)
+        def _():
+            second_gather.z_arrived(-2, 2)
+            second_gather.plane_second()
+            second_gather.first_arrived(-1, 1)
+
         @pl.when(i == 1)
         def _():
-            second_gather.z_arrived(-1, 1)
-            second_gather.first_arrived(0)
-
-        @pl.when(i == 2)
-        def _():
-            prefix.fold(0)
-            second_gather.z_arrived(-2, 2)
-            second_gather.first_arrived(-1, 1)
-
-        @pl.when(i == 3)
-        def _():
-            prefix.fold(1)
             second_gather.z_arrived(-3, 3)
             second_gather.first_arrived(-2, 2)
+
+        @pl.when(i == 2)
+        def _():
+            prefix.fold(0)
+            second_gather.plane_arrived(-1, 1)
+            second_gather.first_arrived(-3, 3)
+
+        @pl.when(i == 3)
+        def _():
+            prefix.fold(1)
+            second_gather.plane_arrived(-2, 2)
 
     def inside(i):
         log_decay = r.aux[i, :, log_at]
@@ -1308,7 +1375,7 @@
         @pl.when(i == 0)
         def _():
             prefix.join(0)
-            second_gather.first_arrived(-3, 3)
+            second_gather.plane_arrived(-3, 3)
 
         @pl.when(i == 1)
         def _():
@@ -1420,23 +1487,30 @@
     pl.loop(0, count)(outputs)
     suffix.join(0)
 
-    def weights_gradient(source, target, values, rows):
-        for n in range(inner // 256):
-            at = slice(n * 256, (n + 1) * 256)
+    def weights_gradient(source, target, values, start, rows, step):
+        for n in range(0, rows, step):
             total = None
             for i in range(count):
-                term = dot(source(i), values[i, :, at], TN)
+                term = dot(source(i, n, step), values[i], TN)
                 total = term if total is None else total + term
-            target[rows, at] = total.astype(BF16)
-
-    weights_gradient(lambda i: r.g[i], r.dout, r.normal, side)
+            target[pl.ds(pl.multiple_of(start + n, LANES), step), :] = total.astype(BF16)
+
+    def normed_block(i, n, step):
+        return r.normed_s[i, HALO:, n : n + step]
+
+    weights_gradient(
+        lambda i, n, step: r.g[i, :, n : n + step], r.dout, r.normal, c * half, half, LANES
+    )
     suffix.fold(2)
-    weights_gradient(lambda i: r.g_in[i], r.dout, r.normal, other_side)
+    weights_gradient(
+        lambda i, n, step: r.g_in[i, :, n : n + step], r.dout, r.normal, (1 - c) * half, half,
+        LANES,
+    )
     reduce_.begin(0)
     suffix.fold(3)
     suffix.join(1)
     suffix.close(0)
-    weights_gradient(lambda i: r.normed_s[i, HALO:], r.dgate, r.ggate_s, slice(None))
+    weights_gradient(normed_block, r.dgate, r.ggate_s, 0, 2 * half, 256)
     reduce_.begin(1)
     suffix.join(2)
 
@@ -1609,19 +1683,9 @@
         r.conv_rows[taps : taps + 1] += jnp.sum(grad_conv, axis=0, keepdims=True)
         low = grad_in.astype(BF16)
         low_pre = r.gate[i, :, gpre_at].astype(BF16)
-        part = dot(r.ggate_s[i], r.w2_full[:, :inner], NT)
-        part = part + dot(low[:, :inner], r.w[:, :inner], NT)
-        part = part + dot(low[:, inner:], r.w[:, mine], NT)
-        part = part + dot(low_pre, r.w[:, channels:], NT)
-        low_part = part.astype(BF16)
-        r.normal[i] = low_part
-        swap_part(i).start()
         r.dy[i] = low[:, :inner]
         r.gtail[i, :, :nstate] = low[:, inner:]
         r.gtail[i, :, nstate:] = low_pre
-        tok = either(c, r.tok[i].astype(F32), r.tok_in[i].astype(F32))
-        unit = tok * lax.rsqrt(jnp.mean(tok * tok, axis=-1, keepdims=True) + EPSILON)
-        r.bc[0:1, :inner] += jnp.sum(low_part.astype(F32) * unit, axis=0, keepdims=True)
 
     @pl.loop(0, count)
     def _(i):
@@ -1655,28 +1719,39 @@
         row = 1 + t // 3
         r.bc[row : row + 1, begin : begin + nstate] = jnp.where(c == 0, own, 0.0)
         r.bc[row : row + 1, begin + nstate : begin + 2 * nstate] = jnp.where(c == 1, own, 0.0)
+
+    half_wide = wide // 2
+
+    def last_gradient(values, target):
+        for n in range(0, 2 * half, 256):
+            total = None
+            for i in range(count):
+                term = dot(normed_block(i, n, 256), values(i), TN)
+                total = term if total is None else total + term
+            target[n : n + 256, :half_wide] = total.astype(BF16)
+
+    reduce_.finish()
+    last_gradient(lambda i: r.dy[i, :, :half_wide], r.dout)
+    late.begin(0)
+    last_gradient(
+        lambda i: jnp.concatenate([r.dy[i, :, half_wide:], r.gtail[i]], axis=1), r.dgate
+    )
+    late.begin(1)
+
+    def part_back(i):
+        part = dot(r.ggate_s[i], r.w2_full[:, :inner], NT)
+        part = part + dot(r.dy[i], r.w[:, :inner], NT)
+        part = part + dot(r.gtail[i, :, :nstate], r.w[:, mine], NT)
+        part = part + dot(r.gtail[i, :, nstate:], r.w[:, channels:], NT)
+        low_part = part.astype(BF16)
+        r.normal[i] = low_part
+        swap_part(i).start()
+        tok = either(c, r.tok[i].astype(F32), r.tok_in[i].astype(F32))
+        unit = tok * lax.rsqrt(jnp.mean(tok * tok, axis=-1, keepdims=True) + EPSILON)
+        r.bc[0:1, :inner] += jnp.sum(low_part.astype(F32) * unit, axis=0, keepdims=True)
+
+    pl.loop(0, count)(part_back)
     core_copy.start()
-
-    def gradient_block(source, at, target, start):
-        total = None
-        for i in range(count):
-            term = dot(r.normed_s[i, HALO:], source[i, :, at : at + 256], TN)
-            total = term if total is None else total + term
-        target[:, start : start + 256] = total.astype(BF16)
-
-    reduce_.finish()
-    gradient_block(r.dy, 0, r.dout, 0)
-    core_copy.wait_recv()
-    r.work[0, 0:2] = r.small[0:2]
-    r.work[0, 2 : 3 + taps] = r.conv_rows[: taps + 1, :inner]
-    r.work[0, 3 + taps : 8] = jnp.zeros((5 - taps, inner), F32)
-    r.work[0, 8:16] = r.bc[...] + r.bc_in[...]
-    x_copy.start()
-    gradient_block(r.dy, 256, r.dout, 256)
-    late.begin(0)
-    gradient_block(r.dy, 512, r.dgate, 0)
-    gradient_block(r.gtail, 0, r.dgate, 256)
-    late.begin(1)
 
     def tokens_back(i):
         swap_part(i).wait_recv()
@@ -1699,21 +1774,31 @@
 
         @pl.when(i == 0)
         def _():
+            core_copy.wait_recv()
+            r.work[0, 0:2] = r.small[0:2]
+            r.work[0, 2 : 3 + taps] = r.conv_rows[: taps + 1, :inner]
+            r.work[0, 3 + taps : 8] = jnp.zeros((5 - taps, inner), F32)
+            r.work[0, 8:16] = r.bc[...] + r.bc_in[...]
+            x_copy.start()
+
+        @pl.when(i == 1)
+        def _():
+            late.second(3, -3)
+
+        @pl.when(i == 2)
+        def _():
             x_copy.wait_recv()
             r.work[1] = r.work[0] + r.from_x[...]
             y_copy.start()
-
-        @pl.when(i == 2)
-        def _():
-            y_copy.wait_recv()
-            r.work[2] = r.work[1] + r.from_y[...]
-            for j in range(LINE):
-                pl.when(z != j)(z_small(j, z).start)
-            r.from_z[z] = r.work[2]
-
-    late.second(3, -3, 2, -2)
+            late.second(2, -2)
+
     late.third(3, -3)
     late.second(1, -1)
+    y_copy.wait_recv()
+    r.work[2] = r.work[1] + r.from_y[...]
+    for j in range(LINE):
+        pl.when(z != j)(z_small(j, z).start)
+    r.from_z[z] = r.work[2]
     late.third(2, -2)
     late.second(0)
     late.third(1, -1)
@@ -1833,7 +1918,7 @@
         store=dma(2, count),
     )
     scan = Scan.scratch(count, inner, nstate, HEAD_ROWS)
-    gather = Gather.semaphores(2)
+    gather = Gather.semaphores(4)
     scratch.update(zip(SUFFIX_REFS, scan.values()))
     scratch.update(scan)
     scratch.update(gather)
@@ -1845,29 +1930,134 @@
     )
 
 
-def fused_layer(sizes, total_inner, heads, tok, g, doc, prm, w, w2):
+def local_call(body, ins, outs, name):
+    names = list(ins) + list(outs)
+
+    def kernel(*refs):
+        body(Refs(names, refs))
+
+    results = pl.pallas_call(
+        kernel,
+        in_specs=[INSIDE for _ in ins],
+        out_specs=[INSIDE for _ in outs],
+        out_shape=list(outs.values()),
+        name=name,
+    )(*ins.values())
+    return Refs(list(outs), results)
+
+
+def pack_body(sizes, r):
     length, inner, nstate, size, taps = sizes
-    model = 2 * tok.shape[2]
-    m = main_call(sizes, total_inner, tok, g, doc, prm, w, w2)
-    sums = m.sums_out
-    shared = sums[9:11].reshape(-1)[: (taps + 1) * 2 * nstate].reshape(taps + 1, 2 * nstate)
-    return (
-        m.mixed,
-        m.tokens_grad,
-        sums[8, :model],
-        jnp.stack([m.g_gate, m.g_x[:, :inner]], axis=1),
-        jnp.concatenate([m.states[0], m.states[1]], axis=1),
-        m.g_x[:, inner + nstate : inner + nstate + heads],
-        sums[2 : 2 + taps],
-        sums[2 + taps],
-        shared[:taps],
-        shared[taps],
-        sums[1, LANES : LANES + heads],
-        sums[1, 2 * LANES : 2 * LANES + heads],
-        sums[1, :heads],
-        sums[0],
-        m.g_out.T,
-    )
+    heads = inner // size
+    channels = inner + 2 * nstate
+    model = r.norm_gain.shape[0]
+
+    def line(v):
+        return v.reshape(1, v.shape[0])
+
+    r.prm[...] = jnp.zeros_like(r.prm)
+    r.prm[GAIN : GAIN + 1, :model] = line(r.norm_gain[...])
+    r.prm[INNER_GAIN : INNER_GAIN + 1, :inner] = line(r.inner_gain[...])
+    r.prm[BIAS : BIAS + 1, :inner] = line(r.conv_bias_x[...])
+    r.prm[BIAS : BIAS + 1, inner:] = line(r.conv_bias_bc[...])
+    r.prm[STEP_BIAS : STEP_BIAS + 1, :heads] = line(r.step_bias[...])
+    r.prm[RATE : RATE + 1, :heads] = -jnp.exp(line(r.decay_log[...]))
+    r.prm[TAPS : TAPS + taps, :inner] = r.conv_taps_x[...]
+    r.prm[TAPS : TAPS + taps, inner:] = r.conv_taps_bc[...]
+    r.prm[SKIP : SKIP + 1, :heads] = line(r.skip_gain[...])
+    skip = jnp.broadcast_to(r.prm[SKIP : SKIP + 1, :LANES], (8, LANES))
+    spread = head_spread(inner, size)
+    r.prm[SKIP : SKIP + 1, :inner] = sum(dot(v, spread) for v in split3(skip))[:1]
+    r.w2[:, :inner] = r.features[:, 0, :]
+    same = lax.broadcasted_iota(jnp.int32, (heads, LANES), 0) == lax.broadcasted_iota(
+        jnp.int32, (heads, LANES), 1
+    )
+    r.w2[:, inner:] = r.output_projection[...]
+    r.w1[:, :inner] = r.features[:, 1, :]
+    r.w1[:, inner:channels] = r.state_weight[...]
+    r.w1[:, channels:] = dot(
+        r.step_weight[...], jnp.where(same, 1.0, 0.0).astype(BF16), TN
+    ).astype(BF16)
+    seqs = r.starts.shape[1]
+    for i in range(r.doc.shape[0]):
+        flags = r.starts[i // seqs, i % seqs : i % seqs + 1].astype(F32)
+        r.doc[i] = jnp.broadcast_to(flags, (8, length))
+
+
+def results_body(sizes, r):
+    length, inner, nstate, size, taps = sizes
+    heads = inner // size
+    r.norm_gain[...] = r.sums[8]
+    r.gate_x[:, 0, :] = r.g_gate[...]
+    r.gate_x[:, 1, :] = r.g_x[:, :inner]
+    r.state_weight[:, :nstate] = r.states[0]
+    r.state_weight[:, nstate:] = r.states[1]
+    r.step_weight[...] = r.g_x[:, inner + nstate :].T[:heads]
+    r.taps_x[...] = r.sums[2 : 2 + taps]
+    r.bias_x[...] = r.sums[2 + taps]
+    for t in range(taps + 1):
+        begin = (t % 3) * 2 * nstate
+        row = r.sums[9 + t // 3, begin : begin + 2 * nstate]
+        if t < taps:
+            r.taps_bc[t] = row
+        else:
+            r.bias_bc[...] = row
+    r.step_bias[...] = r.sums[1, LANES : LANES + heads]
+    r.decay_log[...] = r.sums[1, 2 * LANES : 2 * LANES + heads]
+    r.skip_gain[...] = r.sums[1, :heads]
+    r.inner_gain[...] = r.sums[0]
+
+
+def fused_layer(
+    sizes, total_inner, tok, g, starts, norm_gain, features, state_weight, step_weight, conv_taps_x,
+    conv_bias_x, conv_taps_bc, conv_bias_bc, step_bias, decay_log, skip_gain, inner_gain,
+    output_projection,
+):
+    length, inner, nstate, size, taps = sizes
+    heads = inner // size
+    count, _, half = tok.shape
+    model = 2 * half
+    rows = features.shape[0]
+    channels = inner + 2 * nstate
+    packed = local_call(
+        functools.partial(pack_body, sizes),
+        dict(
+            norm_gain=norm_gain, inner_gain=inner_gain, conv_bias_x=conv_bias_x,
+            conv_bias_bc=conv_bias_bc, step_bias=step_bias, decay_log=decay_log,
+            conv_taps_x=conv_taps_x, conv_taps_bc=conv_taps_bc, skip_gain=skip_gain,
+            features=features, state_weight=state_weight, step_weight=step_weight.T,
+            output_projection=output_projection.T, starts=starts,
+        ),
+        dict(
+            prm=shape((16, channels), F32),
+            w1=shape((rows, channels + LANES), BF16),
+            w2=shape((rows, 2 * inner), BF16),
+            doc=shape((count, 8, length), F32),
+        ),
+        "pack",
+    )
+    m = main_call(sizes, total_inner, tok, g, packed.doc, packed.prm, packed.w1, packed.w2)
+    o = local_call(
+        functools.partial(results_body, sizes),
+        dict(sums=m.sums_out, g_x=m.g_x, g_gate=m.g_gate, states=m.states),
+        dict(
+            norm_gain=shape((model,), F32),
+            gate_x=shape((rows, 2, inner), F32),
+            state_weight=shape((rows, 2 * nstate), F32),
+            step_weight=shape((heads, rows), F32),
+            taps_x=shape((taps, inner), F32),
+            bias_x=shape((inner,), F32),
+            taps_bc=shape((taps, 2 * nstate), F32),
+            bias_bc=shape((2 * nstate,), F32),
+            step_bias=shape((heads,), F32),
+            decay_log=shape((heads,), F32),
+            skip_gain=shape((heads,), F32),
+            inner_gain=shape((inner,), F32),
+        ),
+        "results",
+    )
+    o.step_weight = o.step_weight.T
+    return (m.mixed, m.tokens_grad) + tuple(o.__dict__.values()) + (m.g_out.T,)
 
 
 def shards(
@@ -1891,6 +2081,14 @@
 
     tok = tokens.reshape(count, length, half)
     g = out_grad.reshape(count, length, half)
+    if lax.axis_size("seq") == PLANE * LINE and lax.axis_size("head") == 2:
+        outputs = fused_layer(
+            sizes, total_inner, tok, g, doc_starts, norm_gain, input_gate_features,
+            input_state_weight, input_step_weight, conv_taps_x, conv_bias_x, conv_taps_bc,
+            conv_bias_bc, step_bias, decay_log, skip_gain, inner_gain, output_projection,
+        )
+        return tuple(o.reshape(tokens.shape) if n < 2 else o for n, o in enumerate(outputs))
+
     doc = jnp.broadcast_to(
         doc_starts.reshape(count, 1, length).astype(F32), (count, 8, length)
     )
@@ -1920,15 +2118,6 @@
         axis=1,
     )
     w_out_own = output_projection.T
-
-    if lax.axis_size("seq") == PLANE * LINE and lax.axis_size("head") == 2:
-        outputs = fused_layer(
-            sizes, total_inner, heads, tok, g, doc, prm, w_own[:, inner:],
-            jnp.concatenate([w_own[:, :inner], w_out_own], axis=1),
-        )
-        return tuple(
-            o.reshape(tokens.shape) if n < 2 else o for n, o in enumerate(outputs)
-        )
 
     w_in, w_out, tok_full, g_full, halo = plain_gather(
         w_own, w_out_own, tok, g, tok[:, length - HALO :]

time: 188 us -> 165 us (0.88)
  local copies, waits for them, and re-layouts: 15.9 us -> 3.9 us
  other arithmetic: 7.29 us -> 0 us
  Pallas kernels: 163 us -> 160 us
    pallas_call x1, Pallas kernels: 163 us -> 156 us  [fused_call(): pl.pallas_call(kernel, grid=(steps,) if steps else (), in_specs=[spec for...]
    concatenate x5 -> x0, other arithmetic: 5.01 us -> none  [the longest x1 1.56 us: shards(): jnp.concatenate([w_own[:, :inner], w_out_own], axis=1)]
    pallas_call x0 -> x2, Pallas kernels: none -> 4.19 us  [local_call(): pl.pallas_call(kernel, in_specs=[INSIDE for _ in ins], out_specs=[INSIDE...]
    slice x8 -> x0, local copies, waits for them, and re-layouts: 3.15 us -> none  [the longest x1 0.74 us: fused_layer(): m.g_x[:, inner + nstate:inner + nstate + heads]]
    pad x6 -> x0, local copies, waits for them, and re-layouts: 2.69 us -> none  [the longest x5 2.05 us: row(): return jnp.pad(v, (0, channels - v.shape[0]))[None]]
    unnamed x15 -> x7, local copies, waits for them, and re-layouts: 6.03 us -> 3.9 us
where the time goes in v3:
time: 165 us; the launch traced here: 164 us
  Pallas kernels  160 us (97%)
  local copies, waits for them, and re-layouts  3.9 us (2%)
    pallas_call x1, Pallas kernels, fused_call(): pl.pallas_call(kernel, grid=(steps,) if steps else (), in_specs=[spec for...  156 us
    pallas_call x2, Pallas kernels, local_call(): pl.pallas_call(kernel, in_specs=[INSIDE for _ in ins], out_specs=[INSIDE...  4.19 us
    unnamed x7, local copies, waits for them, and re-layouts  3.9 us

profile of v3, /device:TPU:0, one launch (start us, length us, event | category | flops | bytes accessed | tf_op | source)
XLA Modules:
  0.0 164.3 jit_solution(11803116775389706216)
XLA Ops:
  0.7 2.2 %pack.1 = (f32[16,1024]{1,0:T(8,128)}, bf16[48,1152]{1,0:T(8,128)(2,1)}, bf16[48,1536]{1,0:T(8,128)(2,1)}, f32[4,8,256]{2,1,0:T(8,128)}) custom-call(f32[768]{0:T(1024)} %refs_0_.1, f32[768]{0:T(1024)} %refs_1_.1, f32[768]{0:T(1024)} %refs_2_.1, f32[256]{0:T(256)} %refs_3_.1, f32[12]{0:T(128)} %refs_4_.1, f32[12]{0:T(128)} %refs_5_.1, f32[4,768]{1,0:T(4,128)} %refs_6_.1, ...), custom_call_target="tpu_custom_call" | custom-call | tf_op jit(solution)/shard_map/pack/pallas_call | solution.py:1939
  2.9 155.6 %main.1 = (bf16[4,256,384]{2,1,0:T(8,128)(2,1)}, f32[4,256,384]{2,1,0:T(8,128)}, f32[48,768]{1,0:T(8,128)}, f32[48,768]{1,0:T(8,128)}, f32[48,1024]{1,0:T(8,128)...) custom-call(bf16[4,256,384]{2,1,0:T(8,128)(2,1)} %bitcast.10, bf16[4,256,384]{2,1,0:T(8,128)(2,1)} %bitcast.11, ...), custom_call_target="tpu_custom_call" | custom-call | tf_op jit(solution)/shard_map/main/pallas_call | solution.py:572
  158.5 0.0 copy-start
  158.5 1.9 %results.1 = (f32[768]{0:T(1024)}, f32[48,2,768]{2,1,0:T(2,128)}, f32[48,256]{1,0:T(8,128)}, f32[12,48]{1,0:T(8,128)}, f32[4,768]{1,0:T(4,128)}, /*index=5*/f32[...) custom-call(f32[16,768]{1,0:T(8,128)} %get-tuple-element.44.refs_0_,, ...), custom_call_target="tpu_custom_call" | custom-call | tf_op jit(solution)/shard_map/results/pallas_call | solution.py:1939
  160.4 2.1 %copy.34 = bf16[2,2,256,384]{3,2,1,0:T(8,128)(2,1)} copy(bf16[2,2,256,384]{3,2,1,0:T(8,128)(2,1)} %bitcast.9) | data formatting | bytes 1572864
  162.5 0.0 copy-done
  162.5 0.0 copy-start.1
  162.5 1.1 copy.35
  163.7 0.0 copy-done.1
  163.7 0.7 copy.36
Async XLA Ops:
  158.5 4.1 %copy-start = (f32[4,256,384]{2,1,0:T(8,128)S(1)}, f32[4,256,384]{2,1,0:T(8,128)}, u32[]{:S(2)}) copy-start(f32[4,256,384]{2,1,0:T(8,128)} %get-tuple-element.43) | copy-start | bytes 4718596
  162.5 1.1 copy-start.1

commit v4 on v3

--- a/solution.py
+++ b/solution.py
@@ -744,14 +744,23 @@
                         copy.wait_recv()
                         pl.when(there)(copy.start)
 
-    def finish(self):
+    def received(self):
         for off in OFFSETS:
 
             @pl.when(self.exists(off))
             def _():
                 for p in self.lines:
                     for copy in self.second_copies(p, off):
-                        copy.wait()
+                        copy.wait_recv()
+
+    def drain(self):
+        for off in OFFSETS:
+
+            @pl.when(self.exists(off))
+            def _():
+                for p in self.lines:
+                    for copy in self.second_copies(p, off):
+                        copy.wait_send()
                     self.first_copy(p, off).wait_send()
                 for p in self.span:
                     for there, copy in self.z_copy(p, off):
@@ -1106,6 +1115,15 @@
                         self.mid_send[zz, :, at] = self.kept[zz, :, at].astype(BF16)
                         self.line_copy(p, zz, off > 0).start()
 
+    def near_sent(self):
+        for off in SUM_OFFSETS:
+
+            @pl.when(self.exists(off))
+            def _():
+                for p in self.span:
+                    for copy in self.near_copies(p, self.z + off):
+                        copy.wait_send()
+
     def finish(self):
         for off in SUM_OFFSETS:
 
@@ -1113,8 +1131,6 @@
             def _():
                 zz = self.z + off
                 for p in self.span:
-                    for copy in self.near_copies(p, zz):
-                        copy.wait_send()
                     if off == 0:
                         self.mid_copy(p, zz).wait_send()
                     else:
@@ -1289,16 +1305,31 @@
     first_gather.first_arrived(-3, 3)
     second_gather.first_arrived(0)
     first_gather.plane_arrived(-3, 3)
-    first_gather.finish()
+    first_gather.received()
     kept, ones = triangle(length)
 
+    chunk = 2 * LANES
+    chunks = [slice(n, n + chunk) for n in range(0, inner, chunk)]
+
+    def spread_of(pieces, at):
+        return sum(dot(piece, spread[:, at]) for piece in pieces)
+
+    def tail_of(log_decay, doc_col):
+        return jnp.where(
+            doc_col == doc_col[length - 1 :], jnp.exp(log_decay[length - 1 :] - log_decay), 0.0
+        )
+
+    def project_chunk(i, at):
+        xs = dot(r.normed_s[i], r.w[:, at]).astype(BF16)
+        r.xs_s[i, :, at] = xs
+        r.ext[:, at] = xs.astype(F32)
+        pre = conv(at)
+        act = (pre * sigmoid(pre)).astype(BF16)
+        r.act[i, :, at] = act
+        return act
+
     def project(i):
-        xs = dot(r.normed_s[i], r.w[:, :channels]).astype(BF16)
-        r.xs_s[i] = xs
-        r.ext[...] = xs.astype(F32)
-        pre = conv(slice(0, channels))
-        act = (pre * sigmoid(pre)).astype(BF16)
-        r.act[i] = act
+        project_chunk(i, slice(inner, channels))
         step_pre = (
             dot(r.normed_s[i, HALO:], r.w[:, channels:])
             + r.prm[STEP_BIAS : STEP_BIAS + 1, :LANES]
@@ -1306,23 +1337,25 @@
         step = softplus(step_pre)
         log_decay = running_sum(ones, step * r.prm[RATE : RATE + 1, :LANES])
         doc_col, doc_row = doc_numbers(r.doc[i], ones)
-        entry = jnp.where(doc_col == 0.0, jnp.exp(log_decay), 0.0)
-        last = log_decay[length - 1 :]
-        tail = jnp.where(doc_col == doc_col[length - 1 :], jnp.exp(last - log_decay), 0.0)
         r.aux[i, :, log_at] = log_decay
         r.aux[i, :, step_at] = step
         r.aux[i, :, pre_at] = step_pre
-        r.aux[i, :, entry_at] = entry
+        r.aux[i, :, entry_at] = jnp.where(doc_col == 0.0, jnp.exp(log_decay), 0.0)
         log_rows = log_decay.T
         whole_decay = jnp.where(
             doc_row[:, length - 1 :] == 0.0, jnp.exp(log_rows[:HEAD_ROWS, length - 1 :]), 0.0
         )
         r.dec[i] = jnp.broadcast_to(whole_decay, (HEAD_ROWS, LANES))
-        inputs = act[:, :inner].astype(F32) * expand(step, spread)
-        r.low[i] = inputs.astype(BF16)
-        r.state[i] = dot(
-            (inputs * expand(tail, spread)).astype(BF16), act[:, inner : inner + nstate], TN
-        ).astype(BF16)
+        steps, tails = split2(step), split2(tail_of(log_decay, doc_col))
+        for at in chunks:
+            act = project_chunk(i, at)
+            inputs = act.astype(F32) * spread_of(steps, at)
+            r.low[i, :, at] = inputs.astype(BF16)
+            r.state[i, at] = dot(
+                (inputs * spread_of(tails, at)).astype(BF16),
+                r.act[i, :, inner : inner + nstate],
+                TN,
+            ).astype(BF16)
         prefix.start(i)
 
     @pl.loop(0, count)
@@ -1350,23 +1383,31 @@
         def _():
             prefix.fold(1)
             second_gather.plane_arrived(-2, 2)
+
+    middle = length // 2
+    below = ((slice(0, middle), slice(0, middle)), (slice(middle, length), slice(0, length)))
+    above = ((slice(0, middle), slice(0, length)), (slice(middle, length), slice(middle, length)))
 
     def inside(i):
         log_decay = r.aux[i, :, log_at]
         log_rows = log_decay.T
         doc_col, doc_row = doc_numbers(r.doc[i], ones)
-        closed = jnp.where(kept & (doc_col == doc_row), 0.0, MASKED)
         scores = dot(r.act[i, :, inner + nstate :], r.act[i, :, inner : inner + nstate], NT)
+        scores = jnp.where(kept & (doc_col == doc_row), scores, 0.0)
         for pair in range(inner // LANES):
             columns = slice(pair * LANES, (pair + 1) * LANES)
             part = r.low[i, :, columns]
-            total = None
-            for h in (2 * pair, 2 * pair + 1):
-                decay = jnp.exp(log_decay[:, h : h + 1] - log_rows[h : h + 1] + closed)
-                own = jnp.where(left if h % 2 == 0 else ~left, part, jnp.zeros_like(part))
-                term = dot((scores * decay).astype(BF16), own)
-                total = term if total is None else total + term
-            r.full[i, :, columns] = total
+            sides = [jnp.where(chosen, part, jnp.zeros_like(part)) for chosen in (left, ~left)]
+            for to, ahead in below:
+                total = None
+                for n in range(2):
+                    h = 2 * pair + n
+                    decay = jnp.exp(
+                        jnp.minimum(log_decay[to, h : h + 1] - log_rows[h : h + 1, ahead], 0.0)
+                    )
+                    term = dot((scores[to, ahead] * decay).astype(BF16), sides[n][ahead])
+                    total = term if total is None else total + term
+                r.full[i, to, columns] = total
 
     @pl.loop(0, count)
     def _(i):
@@ -1392,7 +1433,7 @@
             prefix.join(2)
             prefix.close(1)
 
-    second_gather.finish()
+    second_gather.received()
     for i in range(count):
         swap_grads(i).wait()
 
@@ -1414,55 +1455,58 @@
 
     def combine(i):
         prefix.arrived(i)
-        values = r.act[i, :, :inner].astype(F32)
-        entry = expand(r.aux[i, :, entry_at], spread)
-        scanned = r.full[i] + dot(r.act[i, :, inner + nstate :], r.hin[i], NT) * entry
-        r.full[i] = scanned
-        mixed = scanned + r.prm[SKIP : SKIP + 1, :inner] * values
-        gate = r.gate[i]
-        gated = mixed * (gate * sigmoid(gate))
-        squares = jnp.sum(gated * gated, axis=-1, keepdims=True)
-        cross = jnp.sum(
-            r.gn[i] * r.prm[INNER_GAIN : INNER_GAIN + 1, :inner] * gated, axis=-1, keepdims=True
-        )
+        entries = split2(r.aux[i, :, entry_at])
+        squares, cross = jnp.zeros((length, chunk), F32), jnp.zeros((length, chunk), F32)
+        for at in chunks:
+            from_behind = dot(r.act[i, :, inner + nstate :], r.hin[i, at], NT)
+            scanned = r.full[i, :, at] + from_behind * spread_of(entries, at)
+            r.full[i, :, at] = scanned
+            mixed = scanned + r.prm[SKIP : SKIP + 1, at] * r.act[i, :, at].astype(F32)
+            gate = r.gate[i, :, at]
+            gated = mixed * (gate * sigmoid(gate))
+            squares += gated * gated
+            cross += r.gn[i, :, at] * r.prm[INNER_GAIN : INNER_GAIN + 1, at] * gated
+        squares = jnp.sum(squares, axis=-1, keepdims=True)
+        cross = jnp.sum(cross, axis=-1, keepdims=True)
         lane = lax.broadcasted_iota(jnp.int32, (length, LANES), 1)
         r.sums[i] = jnp.where(lane == 0, squares, jnp.where(lane == 1, cross, 0.0)).T[:EDGE]
         swap_sums(i).start()
 
     def norm_back(i):
         swap_sums(i).wait_recv()
-        values = r.act[i, :, :inner].astype(F32)
-        mixed = r.full[i] + r.prm[SKIP : SKIP + 1, :inner] * values
-        gate = r.gate[i]
-        sig = sigmoid(gate)
-        swish = gate * sig
-        gated = mixed * swish
         both = jnp.concatenate(
             [r.sums[i] + r.sums_in[i], jnp.zeros((LANES - EDGE, length), F32)], axis=0
         ).T
         inner_scale = lax.rsqrt(both[:, 0:1] / total_inner + EPSILON)
-        gain = r.prm[INNER_GAIN : INNER_GAIN + 1, :inner]
-        unit = gated * inner_scale
-        r.normal[i] = (unit * gain).astype(BF16)
-        grad_norm = r.gn[i]
-        grad_inner = jnp.sum(grad_norm * unit, axis=0, keepdims=True)
-        grad_gated = inner_scale * (grad_norm * gain) - unit * (
-            inner_scale * inner_scale * (both[:, 1:2] / total_inner)
-        )
-        dy = grad_gated * swish
-        r.dy[i] = dy.astype(BF16)
-        r.ggate_s[i] = (
-            grad_gated * mixed * (sig * (1.0 + gate * (1.0 - sig)))
-        ).astype(BF16)
-        entry = expand(r.aux[i, :, entry_at], spread)
-        r.prior[i] = dot(
-            (dy * entry).astype(BF16), r.act[i, :, inner + nstate :], TN
-        ).astype(BF16)
+        factor = inner_scale * inner_scale * (both[:, 1:2] / total_inner)
+        entries = split2(r.aux[i, :, entry_at])
+        per_head = None
+        for at in chunks:
+            values = r.act[i, :, at].astype(F32)
+            mixed = r.full[i, :, at] + r.prm[SKIP : SKIP + 1, at] * values
+            gate = r.gate[i, :, at]
+            sig = sigmoid(gate)
+            swish = gate * sig
+            unit = mixed * swish * inner_scale
+            gain = r.prm[INNER_GAIN : INNER_GAIN + 1, at]
+            r.normal[i, :, at] = (unit * gain).astype(BF16)
+            grad_norm = r.gn[i, :, at]
+            r.small[0:1, at] += jnp.sum(grad_norm * unit, axis=0, keepdims=True)
+            grad_gated = inner_scale * (grad_norm * gain) - unit * factor
+            dy = grad_gated * swish
+            r.dy[i, :, at] = dy.astype(BF16)
+            r.ggate_s[i, :, at] = (
+                grad_gated * mixed * (sig * (1.0 + gate * (1.0 - sig)))
+            ).astype(BF16)
+            r.prior[i, at] = dot(
+                (dy * spread_of(entries, at)).astype(BF16), r.act[i, :, inner + nstate :], TN
+            ).astype(BF16)
+            term = head_sums(
+                jnp.broadcast_to(jnp.sum(dy * values, axis=0, keepdims=True), (8, chunk)),
+                spread[:, at],
+            )
+            per_head = term if per_head is None else per_head + term
         suffix.start(i)
-        r.small[0:1, :inner] += grad_inner
-        per_head = head_sums(
-            jnp.broadcast_to(jnp.sum(dy * values, axis=0, keepdims=True), (8, inner)), spread
-        )
         r.small[1:2, :LANES] += per_head[:1]
 
     combine(0)
@@ -1506,12 +1550,10 @@
         lambda i, n, step: r.g_in[i, :, n : n + step], r.dout, r.normal, (1 - c) * half, half,
         LANES,
     )
-    reduce_.begin(0)
     suffix.fold(3)
     suffix.join(1)
     suffix.close(0)
     weights_gradient(normed_block, r.dgate, r.ggate_s, 0, 2 * half, 256)
-    reduce_.begin(1)
     suffix.join(2)
 
     upper, ones_upper = triangle(length, True)
@@ -1521,26 +1563,32 @@
         in_state = r.act[i, :, inner : inner + nstate]
         out_state = r.act[i, :, inner + nstate :]
         doc_col, doc_row = doc_numbers(r.doc[i], ones)
-        closed = jnp.where(upper & (doc_col == doc_row), 0.0, MASKED)
         scores = dot(in_state, out_state, NT)
+        scores = jnp.where(upper & (doc_col == doc_row), scores, 0.0)
         log_rows = log_decay.T
         for pair in range(inner // LANES):
             columns = slice(pair * LANES, (pair + 1) * LANES)
             pair_dy = r.dy[i, :, columns]
             pair_in = r.low[i, :, columns]
-            total = None
-            for h in (2 * pair, 2 * pair + 1):
-                chosen = left if h % 2 == 0 else ~left
-                own_dy = jnp.where(chosen, pair_dy, jnp.zeros_like(pair_dy))
-                decay = jnp.exp(log_rows[h : h + 1] - log_decay[:, h : h + 1] + closed)
-                term = dot((scores * decay).astype(BF16), own_dy)
-                total = term if total is None else total + term
-                grad_decay = dot(pair_in, own_dy, NT) * decay
-                if h == 0:
-                    r.gate[i, :, scores_at] = grad_decay
+            sides = [jnp.where(chosen, pair_dy, jnp.zeros_like(pair_dy)) for chosen in (left, ~left)]
+            for to, after in above:
+                total, grad = None, None
+                for n in range(2):
+                    h = 2 * pair + n
+                    own_dy = sides[n][after]
+                    decay = jnp.exp(
+                        jnp.minimum(log_rows[h : h + 1, after] - log_decay[to, h : h + 1], 0.0)
+                    )
+                    term = dot((scores[to, after] * decay).astype(BF16), own_dy)
+                    total = term if total is None else total + term
+                    term = dot(pair_in[to], own_dy, NT) * decay
+                    grad = term if grad is None else grad + term
+                at = slice(half + after.start, half + after.stop)
+                if pair == 0:
+                    r.gate[i, to, at] = grad
                 else:
-                    r.gate[i, :, scores_at] += grad_decay
-            r.gn[i, :, columns] = total
+                    r.gate[i, to, at] += grad
+                r.gn[i, to, columns] = total
 
     @pl.loop(0, count)
     def _(i):
@@ -1558,67 +1606,68 @@
         @pl.when(i == 2)
         def _():
             suffix.close(3)
-            reduce_.second(3, -3)
-
-        @pl.when(i == 3)
-        def _():
-            reduce_.second(2, -2)
+            reduce_.begin(0, 1)
 
     def back_rest(i):
         suffix.arrived(i)
+        doc_col, doc_row = doc_numbers(r.doc[i], ones)
+        log_decay = r.aux[i, :, log_at]
         step = r.aux[i, :, step_at]
-        entry = r.aux[i, :, entry_at]
-        values = r.act[i, :, :inner].astype(F32)
         in_state = r.act[i, :, inner : inner + nstate]
         out_state = r.act[i, :, inner + nstate :]
-        later = r.later[i]
-        wide_dy = r.dy[i].astype(F32)
-        step_wide = expand(step, spread)
-        log_decay = r.aux[i, :, log_at]
-        doc_col, doc_row = doc_numbers(r.doc[i], ones)
-        tail = jnp.where(
-            doc_col == doc_col[length - 1 :], jnp.exp(log_decay[length - 1 :] - log_decay), 0.0
+        steps, tails, entries = (
+            split2(v) for v in (step, tail_of(log_decay, doc_col), r.aux[i, :, entry_at])
         )
-        tail_wide = expand(tail, spread)
-        entry_wide = expand(entry, spread)
-        inputs = values * step_wide
-        grad_inputs = r.gn[i] + tail_wide * dot(in_state, later, NT)
-        grad_scores = r.gate[i, :, scores_at]
-        grad_in = dot(grad_scores.astype(BF16), out_state) + dot(
-            (inputs * tail_wide).astype(BF16), later
-        )
-        grad_out = dot(grad_scores.T.astype(BF16), in_state) + dot(
-            (wide_dy * entry_wide).astype(BF16), r.hin[i]
-        )
+        grad_scores = jnp.where(upper & (doc_col == doc_row), r.gate[i, :, scores_at], 0.0)
+        grad_in = dot(grad_scores.astype(BF16), out_state)
+        grad_out = dot(grad_scores.T.astype(BF16), in_state)
+        grad_log = jnp.zeros((length, LANES), F32)
+        grad_step = jnp.zeros((length, LANES), F32)
+        state_rows = []
+        for pair in range(inner // LANES):
+            at = slice(pair * LANES, (pair + 1) * LANES)
+            step_wide, tail_wide, entry_wide = (
+                spread_of(v, at) for v in (steps, tails, entries)
+            )
+            values = r.act[i, :, at].astype(F32)
+            dy = r.dy[i, :, at].astype(F32)
+            later, hin = r.later[i, at], r.hin[i, at]
+            grad_inputs = r.gn[i, :, at] + tail_wide * dot(in_state, later, NT)
+            grad_in += dot((values * step_wide * tail_wide).astype(BF16), later)
+            grad_out += dot((dy * entry_wide).astype(BF16), hin)
+            grad_log += head_sums(
+                dy * r.full[i, :, at] - r.low[i, :, at].astype(F32) * grad_inputs, spread[:, at]
+            )
+            grad_step += head_sums(values * grad_inputs, spread[:, at])
+            grad_values = step_wide * grad_inputs + r.prm[SKIP : SKIP + 1, at] * dy
+            r.ext[:, at] = r.xs_s[i, :, at].astype(F32)
+            px = conv(at)
+            sig = sigmoid(px)
+            gcx = grad_values * (sig * (1.0 + px * (1.0 - sig)))
+            r.gn[i, :, at] = gcx
+            r.edge[i, :, at] = gcx[:EDGE]
+            leaving = r.state[i, at].astype(F32)
+            for n in range(LANES // size):
+                rows = slice(n * size, (n + 1) * size)
+                h = pair * (LANES // size) + n
+                whole_state = leaving[rows] + r.dec[i, h : h + 1] * hin[rows].astype(F32)
+                state_rows.append(
+                    jnp.sum(later[rows].astype(F32) * whole_state, axis=0, keepdims=True)
+                )
         is_first = c == 0
         r.gate[i, :, own_at] = jnp.where(is_first, grad_in, grad_out)
         r.bsend[i] = jnp.where(is_first, grad_out, grad_in).astype(BF16)
-        entry_last = jnp.broadcast_to(entry[length - 1 :], (8, LANES))
-        later_wide = later.astype(F32)
-        lane_ones = jnp.ones((8, nstate), BF16)
-
-        def state_sums(other):
-            pieces = split2(later_wide * other.astype(F32))
-            return head_sums(sum(dot(lane_ones, piece, NT) for piece in pieces), spread)
-
-        ending = (state_sums(r.state[i]) + entry_last * state_sums(r.hin[i]))[:1]
-        grad_log = head_sums(wide_dy * r.full[i], spread) - head_sums(
-            r.low[i].astype(F32) * grad_inputs, spread
-        )
         swap_states(i).start()
+        state_rows.append(jnp.zeros((LANES - heads, LANES), F32))
+        pieces = split2(jnp.concatenate(state_rows, axis=0))
+        ending = sum(dot(jnp.ones((8, LANES), BF16), piece, NT) for piece in pieces)[:1]
         grad_rate_step = running_sum(ones_upper, grad_log) + ending
         rate = r.prm[RATE : RATE + 1, :LANES]
-        grad_step = head_sums(values * grad_inputs, spread) + rate * grad_rate_step
+        grad_step = grad_step + rate * grad_rate_step
         lane = lax.broadcasted_iota(jnp.int32, (length, LANES), 1)
         gpre = jnp.where(lane < heads, grad_step * sigmoid(r.aux[i, :, pre_at]), 0.0)
         r.gate[i, :, gpre_at] = gpre
-        grad_values = step_wide * grad_inputs + r.prm[SKIP : SKIP + 1, :inner] * wide_dy
-        r.ext[...] = r.xs_s[i].astype(F32)
-        px = conv(slice(0, inner))
-        sig = sigmoid(px)
-        gcx = grad_values * (sig * (1.0 + px * (1.0 - sig)))
-        r.gn[i] = gcx
-        r.edge[i, :, :inner] = gcx[:EDGE]
+        r.ext[:, mine] = r.xs_s[i, :, mine].astype(F32)
         ps = conv(mine)
         sig = sigmoid(ps)
         r.gate[i, :, slope_at] = sig * (1.0 + ps * (1.0 - sig))
@@ -1627,7 +1676,6 @@
             step * grad_rate_step, axis=0, keepdims=True
         )
 
-
     def finish_states(n):
         swap_states(n).wait_recv()
         gst = (r.gate[n, :, own_at] + r.brecv[n].astype(F32)) * r.gate[n, :, slope_at]
@@ -1640,52 +1688,49 @@
         back_rest(i)
         pl.when(i > 0)(lambda: finish_states(i - 1))
 
-        @pl.when(i == 0)
+        @pl.when(i == 1)
+        def _():
+            reduce_.second(3, -3)
+
+        @pl.when(i == 2)
+        def _():
+            reduce_.second(2, -2)
+
+        @pl.when(i == 3)
         def _():
             reduce_.second(1, -1)
-
-        @pl.when(i == 1)
-        def _():
-            reduce_.second(0)
-            reduce_.third(3, -3)
-
-        @pl.when(i == 2)
-        def _():
-            reduce_.third(2, -2)
-
-        @pl.when(i == 3)
-        def _():
-            reduce_.third(1, -1)
 
     r.conv_rows[...] = jnp.zeros_like(r.conv_rows)
     r.bc[...] = jnp.zeros_like(r.bc)
 
     def conv_back(i):
         pl.when(nxt)(send_edge(i).wait_recv)
-        r.gext[:length, :inner] = r.gn[i]
-        r.gext[:length, inner:] = r.gate[i, :, own_at]
-        r.gext[length:] = jnp.where(nxt, r.edge_in[i], 0.0)
-        r.ext[:, :inner] = r.xs_s[i, :, :inner].astype(F32)
-        r.ext[:, inner : inner + nstate] = r.xs_s[i, :, mine].astype(F32)
-        grad_conv = r.gext[:length]
-        grad_in = None
-        for t in range(taps):
-            row = jnp.concatenate(
-                [r.prm[TAPS + t : TAPS + t + 1, :inner], r.prm[TAPS + t : TAPS + t + 1, mine]],
-                axis=1,
-            )
-            term = row * r.gext[taps - 1 - t : taps - 1 - t + length]
-            grad_in = term if grad_in is None else grad_in + term
-            start = HALO - taps + 1 + t
-            r.conv_rows[t : t + 1] += jnp.sum(
-                r.ext[start : start + length, : inner + nstate] * grad_conv, axis=0, keepdims=True
-            )
-        r.conv_rows[taps : taps + 1] += jnp.sum(grad_conv, axis=0, keepdims=True)
-        low = grad_in.astype(BF16)
-        low_pre = r.gate[i, :, gpre_at].astype(BF16)
-        r.dy[i] = low[:, :inner]
-        r.gtail[i, :, :nstate] = low[:, inner:]
-        r.gtail[i, :, nstate:] = low_pre
+
+        def channel_block(source, at, own):
+            grad_conv = source[...]
+            r.gext[:length, at] = grad_conv
+            r.gext[length:, at] = jnp.where(nxt, r.edge_in[i, :, at], 0.0)
+            r.ext[:, at] = r.xs_s[i, :, own].astype(F32)
+            grad_in = None
+            for t in range(taps):
+                term = r.prm[TAPS + t : TAPS + t + 1, own] * r.gext[
+                    taps - 1 - t : taps - 1 - t + length, at
+                ]
+                grad_in = term if grad_in is None else grad_in + term
+                start = HALO - taps + 1 + t
+                r.conv_rows[t : t + 1, at] += jnp.sum(
+                    r.ext[start : start + length, at] * grad_conv, axis=0, keepdims=True
+                )
+            r.conv_rows[taps : taps + 1, at] += jnp.sum(grad_conv, axis=0, keepdims=True)
+            return grad_in.astype(BF16)
+
+        for n in range(0, inner, LANES):
+            at = slice(n, n + LANES)
+            r.dy[i, :, at] = channel_block(r.gn.at[i, :, at], at, at)
+        r.gtail[i, :, :nstate] = channel_block(
+            r.gate.at[i, :, own_at], slice(inner, inner + nstate), mine
+        )
+        r.gtail[i, :, nstate:] = r.gate[i, :, gpre_at].astype(BF16)
 
     @pl.loop(0, count)
     def _(i):
@@ -1694,10 +1739,19 @@
         @pl.when(i == 0)
         def _():
             finish_states(count - 1)
+            reduce_.second(0)
 
         @pl.when(i == 1)
         def _():
-            reduce_.third(0)
+            reduce_.third(3, -3)
+
+        @pl.when(i == 2)
+        def _():
+            reduce_.third(2, -2)
+
+        @pl.when(i == 3)
+        def _():
+            reduce_.third(1, -1)
 
     def small_copy(source, target, at, device):
         return remote(source, target, r.qs.at[at], r.qr.at[at], device)
@@ -1730,13 +1784,15 @@
                 total = term if total is None else total + term
             target[n : n + 256, :half_wide] = total.astype(BF16)
 
-    reduce_.finish()
+    reduce_.near_sent()
     last_gradient(lambda i: r.dy[i, :, :half_wide], r.dout)
     late.begin(0)
     last_gradient(
         lambda i: jnp.concatenate([r.dy[i, :, half_wide:], r.gtail[i]], axis=1), r.dgate
     )
     late.begin(1)
+    reduce_.third(0)
+    reduce_.finish()
 
     def part_back(i):
         part = dot(r.ggate_s[i], r.w2_full[:, :inner], NT)
@@ -1750,7 +1806,18 @@
         unit = tok * lax.rsqrt(jnp.mean(tok * tok, axis=-1, keepdims=True) + EPSILON)
         r.bc[0:1, :inner] += jnp.sum(low_part.astype(F32) * unit, axis=0, keepdims=True)
 
-    pl.loop(0, count)(part_back)
+    @pl.loop(0, count)
+    def _(i):
+        part_back(i)
+
+        @pl.when(i == 1)
+        def _():
+            late.second(3, -3)
+
+        @pl.when(i == 2)
+        def _():
+            late.second(2, -2)
+
     core_copy.start()
 
     def tokens_back(i):
@@ -1774,6 +1841,10 @@
 
         @pl.when(i == 0)
         def _():
+            late.second(1, -1)
+
+        @pl.when(i == 1)
+        def _():
             core_copy.wait_recv()
             r.work[0, 0:2] = r.small[0:2]
             r.work[0, 2 : 3 + taps] = r.conv_rows[: taps + 1, :inner]
@@ -1781,26 +1852,20 @@
             r.work[0, 8:16] = r.bc[...] + r.bc_in[...]
             x_copy.start()
 
-        @pl.when(i == 1)
-        def _():
-            late.second(3, -3)
-
-        @pl.when(i == 2)
-        def _():
-            x_copy.wait_recv()
-            r.work[1] = r.work[0] + r.from_x[...]
-            y_copy.start()
-            late.second(2, -2)
-
-    late.third(3, -3)
-    late.second(1, -1)
+        @pl.when(i == 3)
+        def _():
+            late.third(3, -3)
+
+    late.second(0)
+    x_copy.wait_recv()
+    r.work[1] = r.work[0] + r.from_x[...]
+    y_copy.start()
+    late.third(2, -2)
     y_copy.wait_recv()
     r.work[2] = r.work[1] + r.from_y[...]
     for j in range(LINE):
         pl.when(z != j)(z_small(j, z).start)
     r.from_z[z] = r.work[2]
-    late.third(2, -2)
-    late.second(0)
     late.third(1, -1)
     late.third(0, only=(1,))
     r.states_s[c] = r.g_x[:, inner : inner + nstate]
@@ -1816,8 +1881,11 @@
     y_copy.wait_send()
     for j in range(LINE):
         pl.when(z != j)(z_small(j, z).wait_send)
+    late.near_sent()
     late.finish()
     suffix.finish()
+    for gather in (first_gather, second_gather):
+        gather.drain()
 
     @pl.loop(0, count)
     def _(i):

time: 165 us -> 157 us (0.952)
  Pallas kernels: 160 us -> 153 us
    pallas_call x1, Pallas kernels: 156 us -> 148 us  [fused_call(): pl.pallas_call(kernel, grid=(steps,) if steps else (), in_specs=[spec for...]
where the time goes in v4:
time: 157 us
  Pallas kernels  153 us (97%)
  local copies, waits for them, and re-layouts  3.9 us (2%)
    pallas_call x1, Pallas kernels, fused_call(): pl.pallas_call(kernel, grid=(steps,) if steps else (), in_specs=[spec for...  148 us
    pallas_call x2, Pallas kernels, local_call(): pl.pallas_call(kernel, in_specs=[INSIDE for _ in ins], out_specs=[INSIDE...  4.19 us
    unnamed x7, local copies, waits for them, and re-layouts  3.9 us

profile of v4, /device:TPU:0, one launch (start us, length us, event | category | flops | bytes accessed | tf_op | source)
XLA Modules:
  0.0 157.2 jit_solution(13910166418876089665)
XLA Ops:
  0.7 2.2 %pack.1 = (f32[16,1024]{1,0:T(8,128)}, bf16[48,1152]{1,0:T(8,128)(2,1)}, bf16[48,1536]{1,0:T(8,128)(2,1)}, f32[4,8,256]{2,1,0:T(8,128)}) custom-call(f32[768]{0:T(1024)} %refs_0_.1, f32[768]{0:T(1024)} %refs_1_.1, f32[768]{0:T(1024)} %refs_2_.1, f32[256]{0:T(256)} %refs_3_.1, f32[12]{0:T(128)} %refs_4_.1, f32[12]{0:T(128)} %refs_5_.1, f32[4,768]{1,0:T(4,128)} %refs_6_.1, ...), custom_call_target="tpu_custom_call" | custom-call | tf_op jit(solution)/shard_map/pack/pallas_call | solution.py:2007
  2.9 148.4 %main.1 = (bf16[4,256,384]{2,1,0:T(8,128)(2,1)}, f32[4,256,384]{2,1,0:T(8,128)}, f32[48,768]{1,0:T(8,128)}, f32[48,768]{1,0:T(8,128)}, f32[48,1024]{1,0:T(8,128)...) custom-call(bf16[4,256,384]{2,1,0:T(8,128)(2,1)} %bitcast.10, bf16[4,256,384]{2,1,0:T(8,128)(2,1)} %bitcast.11, ...), custom_call_target="tpu_custom_call" | custom-call | tf_op jit(solution)/shard_map/main/pallas_call | solution.py:572
  151.4 0.0 copy-start
  151.4 1.9 %results.1 = (f32[768]{0:T(1024)}, f32[48,2,768]{2,1,0:T(2,128)}, f32[48,256]{1,0:T(8,128)}, f32[12,48]{1,0:T(8,128)}, f32[4,768]{1,0:T(4,128)}, /*index=5*/f32[...) custom-call(f32[16,768]{1,0:T(8,128)} %get-tuple-element.44.refs_0_,, ...), custom_call_target="tpu_custom_call" | custom-call | tf_op jit(solution)/shard_map/results/pallas_call | solution.py:2007
  153.3 2.1 %copy.34 = bf16[2,2,256,384]{3,2,1,0:T(8,128)(2,1)} copy(bf16[2,2,256,384]{3,2,1,0:T(8,128)(2,1)} %bitcast.9) | data formatting | bytes 1572864
  155.4 0.0 copy-done
  155.4 0.0 copy-start.1
  155.4 1.1 copy.35
  156.6 0.0 copy-done.1
  156.6 0.7 copy.36
Async XLA Ops:
  151.4 4.1 %copy-start = (f32[4,256,384]{2,1,0:T(8,128)S(1)}, f32[4,256,384]{2,1,0:T(8,128)}, u32[]{:S(2)}) copy-start(f32[4,256,384]{2,1,0:T(8,128)} %get-tuple-element.43) | copy-start | bytes 4718596
  155.4 1.1 copy-start.1

commit v5 on v4

--- a/solution.py
+++ b/solution.py
@@ -1842,9 +1842,6 @@
         @pl.when(i == 0)
         def _():
             late.second(1, -1)
-
-        @pl.when(i == 1)
-        def _():
             core_copy.wait_recv()
             r.work[0, 0:2] = r.small[0:2]
             r.work[0, 2 : 3 + taps] = r.conv_rows[: taps + 1, :inner]
@@ -1852,21 +1849,27 @@
             r.work[0, 8:16] = r.bc[...] + r.bc_in[...]
             x_copy.start()
 
+        @pl.when(i == 1)
+        def _():
+            late.third(3, -3)
+
+        @pl.when(i == 2)
+        def _():
+            late.second(0)
+
         @pl.when(i == 3)
         def _():
-            late.third(3, -3)
-
-    late.second(0)
+            late.third(2, -2)
+
     x_copy.wait_recv()
     r.work[1] = r.work[0] + r.from_x[...]
     y_copy.start()
-    late.third(2, -2)
+    late.third(1, -1)
     y_copy.wait_recv()
     r.work[2] = r.work[1] + r.from_y[...]
     for j in range(LINE):
         pl.when(z != j)(z_small(j, z).start)
     r.from_z[z] = r.work[2]
-    late.third(1, -1)
     late.third(0, only=(1,))
     r.states_s[c] = r.g_x[:, inner : inner + nstate]
     states_copy.start()
@@ -2072,6 +2075,9 @@
             r.bias_bc[...] = row
     r.step_bias[...] = r.sums[1, LANES : LANES + heads]
     r.decay_log[...] = r.sums[1, 2 * LANES : 2 * LANES + heads]
+    r.out_weight[...] = r.g_out[...]
+    r.mixed[...] = r.mixed_in[...]
+    r.tokens_grad[...] = r.grad_in[...]
     r.skip_gain[...] = r.sums[1, :heads]
     r.inner_gain[...] = r.sums[0]
 
@@ -2107,8 +2113,13 @@
     m = main_call(sizes, total_inner, tok, g, packed.doc, packed.prm, packed.w1, packed.w2)
     o = local_call(
         functools.partial(results_body, sizes),
-        dict(sums=m.sums_out, g_x=m.g_x, g_gate=m.g_gate, states=m.states),
         dict(
+            sums=m.sums_out, g_x=m.g_x, g_gate=m.g_gate, states=m.states, g_out=m.g_out,
+            mixed_in=m.mixed, grad_in=m.tokens_grad,
+        ),
+        dict(
+            mixed=shape((count, length, half), BF16),
+            tokens_grad=shape((count, length, half), F32),
             norm_gain=shape((model,), F32),
             gate_x=shape((rows, 2, inner), F32),
             state_weight=shape((rows, 2 * nstate), F32),
@@ -2121,11 +2132,12 @@
             decay_log=shape((heads,), F32),
             skip_gain=shape((heads,), F32),
             inner_gain=shape((inner,), F32),
+            out_weight=shape((rows, inner), F32),
         ),
         "results",
     )
-    o.step_weight = o.step_weight.T
-    return (m.mixed, m.tokens_grad) + tuple(o.__dict__.values()) + (m.g_out.T,)
+    o.step_weight, o.out_weight = o.step_weight.T, o.out_weight.T
+    return tuple(o.__dict__.values())
 
 
 def shards(

time: 157 us -> 155 us (0.987)
  local copies, waits for them, and re-layouts: 3.9 us -> 0 us
    unnamed x7 -> x0, local copies, waits for them, and re-layouts: 3.9 us -> none
    pallas_call x2, Pallas kernels: 4.19 us -> 5.87 us  [local_call(): pl.pallas_call(kernel, in_specs=[INSIDE for _ in ins], out_specs=[INSIDE...]
where the time goes in v5:
time: 155 us
  Pallas kernels  154 us (99%)
    pallas_call x1, Pallas kernels, fused_call(): pl.pallas_call(kernel, grid=(steps,) if steps else (), in_specs=[spec for...  148 us
    pallas_call x2, Pallas kernels, local_call(): pl.pallas_call(kernel, in_specs=[INSIDE for _ in ins], out_specs=[INSIDE...  5.87 us

profile of v5, /device:TPU:0, one launch (start us, length us, event | category | flops | bytes accessed | tf_op | source)
XLA Modules:
  0.0 154.5 jit_solution(13025376520686427546)
XLA Ops:
  0.7 2.2 %pack.1 = (f32[16,1024]{1,0:T(8,128)}, bf16[48,1152]{1,0:T(8,128)(2,1)}, bf16[48,1536]{1,0:T(8,128)(2,1)}, f32[4,8,256]{2,1,0:T(8,128)}) custom-call(f32[768]{0:T(1024)} %refs_0_.1, f32[768]{0:T(1024)} %refs_1_.1, f32[768]{0:T(1024)} %refs_2_.1, f32[256]{0:T(256)} %refs_3_.1, f32[12]{0:T(128)} %refs_4_.1, f32[12]{0:T(128)} %refs_5_.1, f32[4,768]{1,0:T(4,128)} %refs_6_.1, ...), custom_call_target="tpu_custom_call" | custom-call | tf_op jit(solution)/shard_map/pack/pallas_call | solution.py:2010
  2.9 147.8 %main.1 = (bf16[4,256,384]{2,1,0:T(8,128)(2,1)}, f32[4,256,384]{2,1,0:T(8,128)}, f32[48,768]{1,0:T(8,128)}, f32[48,768]{1,0:T(8,128)}, f32[48,1024]{1,0:T(8,128)...) custom-call(bf16[4,256,384]{2,1,0:T(8,128)(2,1)} %bitcast.8, bf16[4,256,384]{2,1,0:T(8,128)(2,1)} %bitcast.9, ...), custom_call_target="tpu_custom_call" | custom-call | tf_op jit(solution)/shard_map/main/pallas_call | solution.py:572
  150.7 3.6 %results.1 = (bf16[4,256,384]{2,1,0:T(8,128)(2,1)}, f32[4,256,384]{2,1,0:T(8,128)}, f32[768]{0:T(1024)}, f32[48,2,768]{2,1,0:T(2,128)}, f32[48,256]{1,0:T(8,128)...) custom-call(f32[16,768]{1,0:T(8,128)} %get-tuple-element.45.refs_0_,, ...), custom_call_target="tpu_custom_call" | custom-call | tf_op jit(solution)/shard_map/results/pallas_call | solution.py:2010
